TPU v7x, 32 devices: a whole 2x2x4 slice. The times are simulated.
32 devices in a mesh: seq: 8 (over z, core), dp: 4 (over y, x).
Axes of the slice: x: 2, y: 2, z: 4, core: 2. Of those that a mesh axis runs over, the one named last changes fastest.
Arguments:
- tokens: bfloat16 [2, 4, 1024, 2048], P(None, 'dp', 'seq'), may hold values from -6 to 6
- doc_ends: int32 [2, 4, 18], P(None, 'dp'), may hold values from 60 to 1024, as said below
- input_gain: bfloat16 [2048], P(('seq', 'dp')), may hold values from 0.5 to 1.5
- mixer_in: bfloat16 [2048, 6704], P(('seq', 'dp')), may hold values from -0.125 to 0.125
- conv_weight: bfloat16 [4, 3584], P(None, ('seq', 'dp')), may hold values from -3 to 3
- conv_bias: bfloat16 [3584], P(('seq', 'dp')), may hold values from -2 to 2
- head_params: float32 [3, 48], replicated, may hold values from -8.2 to 1.5, as said below
- mixer_gain: bfloat16 [3072], P(('seq', 'dp')), may hold values from 0.5 to 1.5
- mixer_out: bfloat16 [3072, 2048], P(('seq', 'dp')), may hold values from -0.109375 to 0.109375
- attn_qkv: bfloat16 [2048, 1536], P(('seq', 'dp')), may hold values from -0.125 to 0.125
- attn_out: bfloat16 [1024, 2048], P(('seq', 'dp')), may hold values from -1 to 1
- ffn_gain: bfloat16 [2048], P(('seq', 'dp')), may hold values from 0.5 to 1.5
- gate_up: bfloat16 [2048, 8192], P(('seq', 'dp')), may hold values from -0.125 to 0.125
- down_proj: bfloat16 [4096, 2048], P(('seq', 'dp')), may hold values from -0.09375 to 0.09375
- out_grad: bfloat16 [2, 4, 1024, 2048], P(None, 'dp', 'seq'), may hold values from -6 to 6
Outputs:
- layer_out: bfloat16 [2, 4, 1024, 2048], P(None, 'dp', 'seq')
- token_grad: float32 [2, 4, 1024, 2048], P(None, 'dp', 'seq')
- input_gain_grad: float32 [2048], P(('seq', 'dp'))
- mixer_in_grad: float32 [2048, 6704], P(('seq', 'dp'))
- conv_weight_grad: float32 [4, 3584], P(None, ('seq', 'dp'))
- conv_bias_grad: float32 [3584], P(('seq', 'dp'))
- head_params_grad: float32 [3, 48], replicated
- mixer_gain_grad: float32 [3072], P(('seq', 'dp'))
- mixer_out_grad: float32 [3072, 2048], P(('seq', 'dp'))
- attn_qkv_grad: float32 [2048, 1536], P(('seq', 'dp'))
- attn_out_grad: float32 [1024, 2048], P(('seq', 'dp'))
- ffn_gain_grad: float32 [2048], P(('seq', 'dp'))
- gate_up_grad: float32 [2048, 8192], P(('seq', 'dp'))
- down_proj_grad: float32 [4096, 2048], P(('seq', 'dp'))
Inputs may be any that keep to these rules, and one draw needn't show every extreme that they name: `doc_ends`: Non-decreasing along the last dimension; the last entry is 1024. For each index of dp, one of its 2 sequences, chosen at random, is one document of 1024 tokens; in the others documents have 60 to 800 tokens, the last one of a sequence possibly fewer, and unused slots hold 1024. `head_params`: row 0 holds logarithms of positive decay rates, row 1 time-step biases, row 2 skip weights.
All inputs are finite; a program needn't handle non-finite values.
Results may differ from a plain program's by a relative error of at most 0.015.
Values may be sent and summed in bfloat16 or wider, within the bound.
No kernel may reach another device: no remote copies, remote signals or barrier semaphores. Data moves between devices by JAX's collectives and lax.ppermute only.
A program may use at most 512 MiB of HBM per device.

v0:
```python
from functools import partial

import jax
import jax.numpy as jnp
from jax import lax
from jax.sharding import PartitionSpec as P

HEADS = 48
HEAD_DIM = 64
STATE = 256
ATT_HEADS = 8
KV_HEADS = 2
ATT_DIM = 128


epsilon = 1e-05
rope_base = 10000.0
highest = lax.Precision.HIGHEST


def passed_along(value, axis, by):
    length = lax.axis_size(axis)
    pairs = [(i, i + by) for i in range(length) if 0 <= i + by < length]
    return lax.ppermute(value, axis, pairs)


def entering_2(value, axis, combine, identity):
    length, here = (lax.axis_size(axis), lax.axis_index(axis))
    everything = jax.tree.map(
        lambda part, kind: lax.all_gather(part.astype(kind), axis),
        value,
        (jnp.bfloat16, jnp.bfloat16),
    )
    start = jax.tree.map(
        lambda part, zero: jnp.broadcast_to(jnp.asarray(zero, part.dtype), part.shape),
        value,
        identity,
    )

    def turn(k, before):
        reached = k < here
        new = combine(
            before, jax.tree.map(lambda part, own: part[k].astype(own.dtype), everything, value)
        )
        return jax.tree.map(lambda a, b: jnp.where(reached, a, b), new, before)

    return lax.fori_loop(0, length, turn, start)


def carried_in(value, axis, join, neutral):
    count = lax.axis_size(axis)
    place = lax.axis_index(axis)
    ahead = count - 1 - place
    gathered = jax.tree.map(
        lambda a, kind: lax.all_gather(a.astype(kind), axis),
        value,
        jax.tree.map(lambda a: jnp.bfloat16 if a.dtype == jnp.float32 else a.dtype, value),
    )
    state = jax.tree.map(lambda a, e: jnp.zeros_like(a) + jnp.asarray(e, a.dtype), value, neutral)

    def one(turn, state):
        source = count - 1 - turn
        return join(
            state,
            jax.tree.map(
                lambda a, own: lax.dynamic_index_in_dim(a, source, 0, False).astype(own.dtype),
                gathered,
                value,
            ),
        )

    return lax.fori_loop(0, ahead, one, state)


def shortened(value):
    return jax.tree.map(lambda a: a.astype(jnp.bfloat16) if a.dtype == jnp.float32 else a, value)


def rms_scale(values, gain):
    return values * lax.rsqrt(jnp.mean(values * values, axis=-1, keepdims=True) + epsilon) * gain


def segment_of(positions, end_points):
    counted = jnp.sum((end_points[None, :] <= positions[:, None]).astype(jnp.int32), axis=1)
    return jnp.where(positions < 0, -1, counted)


def rope_tables(positions, head_width):
    half_width = head_width // 2
    freqs = jnp.power(rope_base, -jnp.arange(half_width, dtype=jnp.float32) * (2.0 / head_width))
    angles = positions.astype(jnp.float32)[:, None] * freqs[None, :]
    return (
        jnp.concatenate([jnp.cos(angles), jnp.cos(angles)], axis=1),
        jnp.concatenate([jnp.sin(angles), jnp.sin(angles)], axis=1),
    )


def rotate_half(values, cosine, sine):
    half_width = values.shape[-1] // 2
    turned = jnp.concatenate([-values[..., half_width:], values[..., :half_width]], axis=-1)
    return values * cosine[:, None, :] + turned * sine[:, None, :]


def attention_prep(qkv_rows, cosine, sine):
    row_count = qkv_rows.shape[0]
    query_width = ATT_HEADS * ATT_DIM
    key_width = KV_HEADS * ATT_DIM
    queries = rotate_half(
        qkv_rows[:, :query_width].reshape(row_count, ATT_HEADS, ATT_DIM), cosine, sine
    )
    keys = rotate_half(
        qkv_rows[:, query_width : query_width + key_width].reshape(row_count, KV_HEADS, ATT_DIM),
        cosine,
        sine,
    )
    values = qkv_rows[:, query_width + key_width :].reshape(row_count, KV_HEADS, ATT_DIM)
    return (queries, keys, values)


def tap_masks(seg_ext, row_count, kernel):
    own_segment = seg_ext[kernel - 1 :]
    return jnp.stack(
        [
            (seg_ext[offset : offset + row_count] == own_segment).astype(jnp.float32)
            for offset in range(kernel)
        ],
        axis=1,
    )


def conv_part(extended, dt_raw, conv_weight, conv_bias, head_params, taps):
    row_count = dt_raw.shape[0]
    total = conv_bias[None, :]
    for offset in range(conv_weight.shape[0]):
        total = (
            total
            + extended[offset : offset + row_count]
            * conv_weight[offset][None, :]
            * taps[:, offset : offset + 1]
        )
    conv_out = jax.nn.silu(total)
    step_size = jax.nn.softplus(dt_raw + head_params[1][None, :])
    log_decay = -jnp.exp(head_params[0])[None, :] * step_size
    return (conv_out, step_size, log_decay)


def block_masks(seg_here, seg_before):
    row_count = seg_here.shape[0]
    order = jnp.arange(row_count, dtype=jnp.int32)
    within = ((order[None, :] <= order[:, None]) & (seg_here[:, None] == seg_here[None, :])).astype(
        jnp.float32
    )
    entering = (seg_here == seg_before).astype(jnp.float32)
    trailing = (seg_here == seg_here[row_count - 1]).astype(jnp.float32)
    passing = (seg_here[row_count - 1] == seg_before).astype(jnp.float32)
    return (within, entering, trailing, passing)


def block_output(conv_out, step_size, log_cum, head_params, state_in, within, entering, inner):
    row_count, head_count = step_size.shape
    state_width = (conv_out.shape[1] - inner) // 2
    head_inputs = conv_out[:, :inner].reshape(row_count, head_count, inner // head_count)
    input_proj = conv_out[:, inner : inner + state_width]
    output_proj = conv_out[:, inner + state_width :]
    intersection = jnp.dot(output_proj, input_proj.T, precision=highest)
    gap_log = log_cum[:, None, :] - log_cum[None, :, :]
    mask_cube = within[:, :, None]
    mixing = (
        intersection[:, :, None]
        * jnp.exp(jnp.where(mask_cube > 0, gap_log, 0.0))
        * mask_cube
        * step_size[None, :, :]
    )
    outputs = jnp.einsum("tsh,shp->thp", mixing, head_inputs, precision=highest)
    carried = jnp.einsum("tn,hpn->thp", output_proj, state_in, precision=highest)
    outputs = outputs + carried * (jnp.exp(log_cum) * entering[:, None])[:, :, None]
    outputs = outputs + head_params[2][None, :, None] * head_inputs
    return outputs.reshape(row_count, inner)


def block_state(conv_out, step_size, log_cum, trailing, passing, inner):
    row_count, head_count = step_size.shape
    state_width = (conv_out.shape[1] - inner) // 2
    head_inputs = conv_out[:, :inner].reshape(row_count, head_count, inner // head_count)
    input_proj = conv_out[:, inner : inner + state_width]
    last_log = log_cum[row_count - 1]
    keeping = jnp.exp(last_log[None, :] - log_cum) * trailing[:, None] * step_size
    scaled = head_inputs * keeping[:, :, None]
    states = jnp.einsum("shp,sn->hpn", scaled, input_proj, precision=highest)
    return (jnp.exp(last_log) * passing, states)


def combine_states(earlier, later):
    return (earlier[0] * later[0], later[0][:, None, None] * earlier[1] + later[1])


def swiglu(gate_vals):
    half_width = gate_vals.shape[1] // 2
    return jax.nn.silu(gate_vals[:, :half_width]) * gate_vals[:, half_width:]


def cross_rows(left, right):
    return lax.dot_general(
        left, right, (((0,), (0,)), ((), ())), preferred_element_type=jnp.float32
    )


def back_dot(grads, weight):
    return lax.dot_general(
        grads, weight, (((1,), (1,)), ((), ())), preferred_element_type=jnp.float32
    )


def add_up(totals, terms):
    if totals is None:
        return list(terms)
    return [left + right for left, right in zip(totals, terms)]


def spread_heads(head_grad):
    return jnp.broadcast_to(
        head_grad[None], (lax.axis_size("seq") * lax.axis_size("dp"),) + head_grad.shape
    )


def local(
    tokens,
    doc_ends,
    input_gain,
    mixer_in,
    conv_weight,
    conv_bias,
    head_params,
    mixer_gain,
    mixer_out,
    attn_qkv,
    attn_out,
    ffn_gain,
    gate_up,
    down_proj,
    out_grad,
):
    micro_count = tokens.shape[0]
    row_count = tokens.shape[2]
    kernel = conv_weight.shape[0]
    inner = HEADS * HEAD_DIM
    key_width = KV_HEADS * ATT_DIM
    repeat = ATT_HEADS // KV_HEADS
    scale = ATT_DIM ** (-0.5)
    seq_count = lax.axis_size("seq")
    start = lax.axis_index("seq") * row_count
    local_pos = start + jnp.arange(row_count, dtype=jnp.int32)
    all_pos = jnp.arange(row_count * seq_count, dtype=jnp.int32)
    ext_pos = start - (kernel - 1) + jnp.arange(row_count + kernel - 1, dtype=jnp.int32)
    cosine, sine = rope_tables(local_pos, ATT_DIM)
    shards = (
        input_gain,
        mixer_in,
        conv_weight,
        conv_bias,
        mixer_gain,
        mixer_out,
        attn_qkv,
        attn_out,
        ffn_gain,
        gate_up,
        down_proj,
    )
    fetched = (
        lax.all_gather(shards[0], ("seq", "dp"), axis=0, tiled=True),
        lax.all_gather(shards[1], ("seq", "dp"), axis=0, tiled=True),
        lax.all_gather(shards[2], ("seq", "dp"), axis=1, tiled=True),
        lax.all_gather(shards[3], ("seq", "dp"), axis=0, tiled=True),
        lax.all_gather(shards[4], ("seq", "dp"), axis=0, tiled=True),
        lax.all_gather(shards[5], ("seq", "dp"), axis=0, tiled=True),
        lax.all_gather(shards[6], ("seq", "dp"), axis=0, tiled=True),
        lax.all_gather(shards[7], ("seq", "dp"), axis=0, tiled=True),
        lax.all_gather(shards[8], ("seq", "dp"), axis=0, tiled=True),
        lax.all_gather(shards[9], ("seq", "dp"), axis=0, tiled=True),
        lax.all_gather(shards[10], ("seq", "dp"), axis=0, tiled=True),
    )
    (
        gain_in,
        proj_in,
        conv_taps,
        conv_shift,
        gain_mix,
        proj_mix,
        proj_qkv,
        proj_att,
        gain_ffn,
        proj_gu,
        proj_down,
    ) = fetched
    layer_rows = []
    saved = []
    for batch_index in range(micro_count):
        token_vals = tokens[batch_index, 0].astype(jnp.float32)
        end_points = doc_ends[batch_index, 0]
        seg_ext = segment_of(ext_pos, end_points)
        seg_here = seg_ext[kernel - 1 :]
        seg_before = segment_of(jnp.reshape(start - 1, (1,)), end_points)[0]
        within, entering, trailing, passing = block_masks(seg_here, seg_before)
        taps = tap_masks(seg_ext, row_count, kernel)
        seg_all = segment_of(all_pos, end_points)
        visible = (all_pos[None, :] <= local_pos[:, None]) & (seg_all[None, :] == seg_here[:, None])
        normed_in, pull_in_norm = jax.vjp(rms_scale, token_vals, gain_in.astype(jnp.float32))
        normed_b = normed_in.astype(jnp.bfloat16)
        mixed = jnp.dot(normed_b, proj_in, preferred_element_type=jnp.float32)
        gate_z = mixed[:, :inner]
        conv_low = mixed[:, inner : 2 * inner + 2 * STATE].astype(jnp.bfloat16)
        dt_raw = mixed[:, 2 * inner + 2 * STATE :]
        edge_rows = passed_along(conv_low[row_count - (kernel - 1) :], "seq", 1)
        extended = jnp.concatenate([edge_rows, conv_low], axis=0).astype(jnp.float32)

        def first_part(ext_rows, dt_rows, taps_f32, shift_f32, head_vals, taps=taps):
            conv_out, step_size, log_decay = conv_part(
                ext_rows, dt_rows, taps_f32, shift_f32, head_vals, taps
            )
            return (conv_out, step_size, jnp.cumsum(log_decay, axis=0))

        (conv_out, step_size, log_cum), pull_first = jax.vjp(
            first_part,
            extended,
            dt_raw,
            conv_taps.astype(jnp.float32),
            conv_shift.astype(jnp.float32),
            head_params,
        )
        (passed, states), pull_state = jax.vjp(
            partial(block_state, trailing=trailing, passing=passing, inner=inner),
            conv_out,
            step_size,
            log_cum,
        )
        prior = entering_2(
            (passed, states), "seq", combine_states, (jnp.ones_like(passed), jnp.zeros_like(states))
        )
        state_in = prior[1]

        def out_part(
            conv_vals,
            step_vals,
            log_vals,
            gate_vals,
            gain_vals,
            head_vals,
            state_vals,
            within=within,
            entering=entering,
        ):
            outputs = block_output(
                conv_vals, step_vals, log_vals, head_vals, state_vals, within, entering, inner
            )
            return rms_scale(outputs * jax.nn.silu(gate_vals), gain_vals)

        mixer_normed, pull_out = jax.vjp(
            out_part,
            conv_out,
            step_size,
            log_cum,
            gate_z,
            gain_mix.astype(jnp.float32),
            head_params,
            state_in,
        )
        mixer_b = mixer_normed.astype(jnp.bfloat16)
        mixer_branch = jnp.dot(mixer_b, proj_mix, preferred_element_type=jnp.float32)
        qkv_rows = jnp.dot(normed_b, proj_qkv, preferred_element_type=jnp.float32)
        (queries, keys, values), pull_att = jax.vjp(
            partial(attention_prep, cosine=cosine, sine=sine), qkv_rows
        )
        queries_b = queries.astype(jnp.bfloat16)
        kv_local = jnp.concatenate(
            [keys.reshape(row_count, key_width), values.reshape(row_count, key_width)], axis=1
        ).astype(jnp.bfloat16)
        kv_all = lax.all_gather(kv_local, "seq", axis=0, tiled=True)
        key_heads = kv_all[:, :key_width].reshape(-1, KV_HEADS, ATT_DIM).transpose(1, 0, 2)
        value_heads = kv_all[:, key_width:].reshape(-1, KV_HEADS, ATT_DIM).transpose(1, 0, 2)
        grouped = queries_b.reshape(row_count, KV_HEADS, repeat, ATT_DIM).transpose(1, 2, 0, 3)
        scores = (
            jnp.einsum("grtd,gkd->grtk", grouped, key_heads, preferred_element_type=jnp.float32)
            * scale
        )
        scores = jnp.where(visible[None, None], scores, -1e30)
        top_score = jnp.max(scores, axis=-1, keepdims=True)
        expd = jnp.exp(scores - top_score)
        total_weight = jnp.sum(expd, axis=-1, keepdims=True)
        probs_b = (expd / total_weight).astype(jnp.bfloat16)
        log_total = top_score + jnp.log(total_weight)
        attended = jnp.einsum(
            "grtk,gkd->grtd", probs_b, value_heads, preferred_element_type=jnp.float32
        )
        attended_b = (
            attended.transpose(2, 0, 1, 3)
            .reshape(row_count, ATT_HEADS * ATT_DIM)
            .astype(jnp.bfloat16)
        )
        attn_branch = jnp.dot(attended_b, proj_att, preferred_element_type=jnp.float32)
        hidden = token_vals + mixer_branch + attn_branch
        ffn_normed, pull_ffn_norm = jax.vjp(rms_scale, hidden, gain_ffn.astype(jnp.float32))
        ffn_b = ffn_normed.astype(jnp.bfloat16)
        gate_vals = jnp.dot(ffn_b, proj_gu, preferred_element_type=jnp.float32)
        activated, pull_swiglu = jax.vjp(swiglu, gate_vals)
        activated_b = activated.astype(jnp.bfloat16)
        result = hidden + jnp.dot(activated_b, proj_down, preferred_element_type=jnp.float32)
        layer_rows.append(result.astype(jnp.bfloat16))
        saved.append(
            dict(
                pull_in_norm=pull_in_norm,
                normed_b=normed_b,
                pull_first=pull_first,
                pull_state=pull_state,
                passed=passed,
                state_in=state_in,
                pull_out=pull_out,
                mixer_b=mixer_b,
                pull_att=pull_att,
                grouped=grouped,
                key_heads=key_heads,
                value_heads=value_heads,
                log_total=log_total,
                visible=visible,
                attended_b=attended_b,
                pull_ffn_norm=pull_ffn_norm,
                ffn_b=ffn_b,
                pull_swiglu=pull_swiglu,
                activated_b=activated_b,
            )
        )
    (
        gain_in,
        proj_in,
        conv_taps,
        conv_shift,
        gain_mix,
        proj_mix,
        proj_qkv,
        proj_att,
        gain_ffn,
        proj_gu,
        proj_down,
    ) = fetched
    ffn_totals = None
    ffn_sums = None
    hidden_grads = []
    for batch_index in range(micro_count):
        kept = saved[batch_index]
        grad_rows = out_grad[batch_index, 0]
        down_grad = cross_rows(kept["activated_b"], grad_rows)
        act_grad = back_dot(grad_rows, proj_down)
        gate_grad = kept["pull_swiglu"](act_grad)[0].astype(jnp.bfloat16)
        gu_grad = cross_rows(kept["ffn_b"], gate_grad)
        ffn_in_grad = back_dot(gate_grad, proj_gu)
        hidden_part, ffn_gain_grad = kept["pull_ffn_norm"](ffn_in_grad)
        ffn_totals = add_up(ffn_totals, (gu_grad, down_grad, ffn_gain_grad))
        hidden_grads.append(hidden_part + grad_rows.astype(jnp.float32))
    ffn_sums = (
        lax.psum_scatter(ffn_totals[0], ("seq", "dp"), scatter_dimension=0, tiled=True),
        lax.psum_scatter(ffn_totals[1], ("seq", "dp"), scatter_dimension=0, tiled=True),
        lax.psum_scatter(ffn_totals[2], ("seq", "dp"), scatter_dimension=0, tiled=True),
    )
    attn_totals = None
    attn_sums = None
    normed_grads = []
    for batch_index in range(micro_count):
        kept = saved[batch_index]
        hidden_b = hidden_grads[batch_index].astype(jnp.bfloat16)
        grouped = kept["grouped"]
        key_heads = kept["key_heads"]
        value_heads = kept["value_heads"]
        att_out_grad = cross_rows(kept["attended_b"], hidden_b)
        attended_grad = back_dot(hidden_b, proj_att).astype(jnp.bfloat16)
        grad_heads = attended_grad.reshape(row_count, KV_HEADS, repeat, ATT_DIM).transpose(
            1, 2, 0, 3
        )
        again_scores = (
            jnp.einsum("grtd,gkd->grtk", grouped, key_heads, preferred_element_type=jnp.float32)
            * scale
        )
        probs = jnp.where(
            kept["visible"][None, None], jnp.exp(again_scores - kept["log_total"]), 0.0
        )
        probs_grad = jnp.einsum(
            "grtd,gkd->grtk", grad_heads, value_heads, preferred_element_type=jnp.float32
        )
        scores_grad = (
            probs * (probs_grad - jnp.sum(probs * probs_grad, axis=-1, keepdims=True))
        ).astype(jnp.bfloat16)
        query_grad = (
            jnp.einsum("grtk,gkd->grtd", scores_grad, key_heads, preferred_element_type=jnp.float32)
            * scale
        )
        key_grad = (
            jnp.einsum("grtk,grtd->gkd", scores_grad, grouped, preferred_element_type=jnp.float32)
            * scale
        )
        value_grad = jnp.einsum(
            "grtk,grtd->gkd",
            probs.astype(jnp.bfloat16),
            grad_heads,
            preferred_element_type=jnp.float32,
        )
        kv_terms = jnp.concatenate(
            [
                key_grad.transpose(1, 0, 2).reshape(-1, key_width),
                value_grad.transpose(1, 0, 2).reshape(-1, key_width),
            ],
            axis=1,
        )
        kv_grad = lax.psum_scatter(
            kv_terms.astype(jnp.bfloat16), "seq", scatter_dimension=0, tiled=True
        ).astype(jnp.float32)
        qkv_grad = kept["pull_att"](
            (
                query_grad.transpose(2, 0, 1, 3).reshape(row_count, ATT_HEADS, ATT_DIM),
                kv_grad[:, :key_width].reshape(row_count, KV_HEADS, ATT_DIM),
                kv_grad[:, key_width:].reshape(row_count, KV_HEADS, ATT_DIM),
            )
        )[0]
        qkv_b = qkv_grad.astype(jnp.bfloat16)
        qkv_weight_grad = cross_rows(kept["normed_b"], qkv_b)
        normed_grads.append(back_dot(qkv_b, proj_qkv))
        attn_totals = add_up(attn_totals, (qkv_weight_grad, att_out_grad))
    attn_sums = (
        lax.psum_scatter(attn_totals[0], ("seq", "dp"), scatter_dimension=0, tiled=True),
        lax.psum_scatter(attn_totals[1], ("seq", "dp"), scatter_dimension=0, tiled=True),
    )
    mixer_totals = None
    mixer_sums = None
    token_rows = []
    for batch_index in range(micro_count):
        kept = saved[batch_index]
        hidden_b = hidden_grads[batch_index].astype(jnp.bfloat16)
        passed = kept["passed"]
        mix_out_grad = cross_rows(kept["mixer_b"], hidden_b)
        mixer_normed_grad = back_dot(hidden_b, proj_mix)
        (
            conv_grad_a,
            step_grad_a,
            log_grad_a,
            gate_z_grad,
            mix_gain_grad,
            head_grad_a,
            state_here,
        ) = kept["pull_out"](mixer_normed_grad)
        later = carried_in(
            (passed, state_here),
            "seq",
            combine_states,
            (jnp.ones_like(passed), jnp.zeros_like(state_here)),
        )
        carried = later[1]
        passed_grad = jnp.sum(carried * kept["state_in"], axis=(1, 2))
        conv_grad_b, step_grad_b, log_grad_b = kept["pull_state"]((passed_grad, carried))
        ext_grad, dt_grad, conv_taps_grad, conv_shift_grad, head_grad_c = kept["pull_first"](
            (conv_grad_a + conv_grad_b, step_grad_a + step_grad_b, log_grad_a + log_grad_b)
        )
        back_rows = passed_along(shortened(ext_grad[: kernel - 1]), "seq", -1)
        conv_in_grad = ext_grad[kernel - 1 :] + jnp.pad(
            back_rows, ((row_count - (kernel - 1), 0), (0, 0))
        )
        mixed_b = jnp.concatenate([gate_z_grad, conv_in_grad, dt_grad], axis=1).astype(jnp.bfloat16)
        mix_in_grad = cross_rows(kept["normed_b"], mixed_b)
        normed_grad = normed_grads[batch_index] + back_dot(mixed_b, proj_in)
        token_part, gain_in_grad = kept["pull_in_norm"](normed_grad)
        head_grad = head_grad_a + head_grad_c
        mixer_totals = add_up(
            mixer_totals,
            (
                gain_in_grad,
                mix_in_grad,
                conv_taps_grad,
                conv_shift_grad,
                head_grad,
                mix_gain_grad,
                mix_out_grad,
            ),
        )
        token_rows.append(token_part + hidden_grads[batch_index])
    mixer_sums = (
        lax.psum_scatter(mixer_totals[0], ("seq", "dp"), scatter_dimension=0, tiled=True),
        lax.psum_scatter(mixer_totals[1], ("seq", "dp"), scatter_dimension=0, tiled=True),
        lax.psum_scatter(mixer_totals[2], ("seq", "dp"), scatter_dimension=1, tiled=True),
        lax.psum_scatter(mixer_totals[3], ("seq", "dp"), scatter_dimension=0, tiled=True),
        lax.psum_scatter(
            spread_heads(mixer_totals[4]), ("seq", "dp"), scatter_dimension=0, tiled=True
        ),
        lax.psum_scatter(mixer_totals[5], ("seq", "dp"), scatter_dimension=0, tiled=True),
        lax.psum_scatter(mixer_totals[6], ("seq", "dp"), scatter_dimension=0, tiled=True),
    )
    layer_out = jnp.stack(layer_rows)[:, None]
    token_grad = jnp.stack(token_rows)[:, None]
    return (
        layer_out,
        token_grad,
        mixer_sums[0],
        mixer_sums[1],
        mixer_sums[2],
        mixer_sums[3],
        mixer_sums[4][0],
        mixer_sums[5],
        mixer_sums[6],
        attn_sums[0],
        attn_sums[1],
        ffn_sums[2],
        ffn_sums[0],
        ffn_sums[1],
    )


def solution(mesh):
    return jax.shard_map(
        local,
        mesh=mesh,
        in_specs=(
            P(None, "dp", "seq", None),
            P(None, "dp", None),
            P(("seq", "dp")),
            P(("seq", "dp"), None),
            P(None, ("seq", "dp")),
            P(("seq", "dp")),
            P(),
            P(("seq", "dp")),
            P(("seq", "dp"), None),
            P(("seq", "dp"), None),
            P(("seq", "dp"), None),
            P(("seq", "dp")),
            P(("seq", "dp"), None),
            P(("seq", "dp"), None),
            P(None, "dp", "seq", None),
        ),
        out_specs=(
            P(None, "dp", "seq", None),
            P(None, "dp", "seq", None),
            P(("seq", "dp")),
            P(("seq", "dp"), None),
            P(None, ("seq", "dp")),
            P(("seq", "dp")),
            P(),
            P(("seq", "dp")),
            P(("seq", "dp"), None),
            P(("seq", "dp"), None),
            P(("seq", "dp"), None),
            P(("seq", "dp")),
            P(("seq", "dp"), None),
            P(("seq", "dp"), None),
        ),
        check_vma=False,
    )
```

profile of v0, /device:TPU:0, one launch (start us, length us, event | category | flops | bytes accessed | tf_op | source)
XLA Modules:
  0.0 5457.0 jit_solution(3339013221703083039)
XLA Ops:
  12.1 42.7 all-reduce.64
  55.5 67.1 %all-gather.4 = bf16[32,112,4]{1,2,0:T(4,128)(2,1)S(1)} all-gather(bf16[1,112,4]{1,2,0:T(4,128)(2,1)} %bitcast.603), channel_id=1, replica_groups=mesh['seq'=8,'dp'=4] {'seq','dp'}, dimensions={0}, use_global_device_ids=true | all-gather | bytes 29568 | tf_op jit(solution)/shard_map/all_gather | solution.py:272
  140.9 111.4 %all-gather.20.cloned.1.call-done = bf16[2048,6704]{1,0:T(8,128)(2,1)} async-done(((bf16[64,6704]{1,0:T(8,128)(2,1)}), bf16[2048,6704]{1,0:T(8,128)(2,1)}) %all-gather.20.cloned.1.call-update) | async-done | bytes 27459600 | tf_op jit(solution)/shard_map/all_gather | solution.py:271
  252.4 18.1 fusion.318
  272.7 18.4 fusion.319
  309.7 6.8 fusion.51
  368.2 10.9 all-gather.6
  381.3 10.1 all-gather.5
  395.8 41.7 all-gather.38.cloned.1.call-done
  437.5 43.4 while.59
  485.8 6.4 fusion.62
  496.3 38.2 all-gather.22.cloned.1.call-done
  534.6 7.9 convolution_add_fusion.10
  542.5 55.2 %all-gather.28.cloned.1.call-done = bf16[1024,2048]{1,0:T(8,128)(2,1)} async-done(((bf16[32,2048]{1,0:T(8,128)(2,1)}), bf16[1024,2048]{1,0:T(8,128)(2,1)}) %all-gather.28.cloned.1.call-update) | async-done | bytes 4194320 | tf_op jit(solution)/shard_map/all_gather | solution.py:277
  602.0 113.2 %all-gather.36.cloned.1.call-done = bf16[384,64,256]{2,1,0:T(8,128)(2,1)} async-done(((bf16[48,64,256]{2,1,0:T(8,128)(2,1)}), bf16[384,64,256]{2,1,0:T(8,128)(2,1)}) %all-gather.36.cloned.1.call-update) | async-done | bytes 12582928 | tf_op jit(solution)/shard_map/all_gather | solution.py:30
  715.3 25.1 while.58
  744.5 6.5 fusion.63
  753.6 8.0 convolution_add_fusion.11
  763.5 147.7 %all-gather.30.cloned.1.call-done = bf16[2048,8192]{1,0:T(8,128)(2,1)} async-done(((bf16[64,8192]{1,0:T(8,128)(2,1)}), bf16[2048,8192]{1,0:T(8,128)(2,1)}) %all-gather.30.cloned.1.call-update) | async-done | bytes 33554448 | tf_op jit(solution)/shard_map/all_gather | solution.py:279
  911.2 18.3 fusion.284
  929.5 17.2 fusion.283
  946.8 80.2 %all-gather.32.cloned.1.call-done = bf16[4096,2048]{1,0:T(8,128)(2,1)} async-done(((bf16[128,2048]{1,0:T(8,128)(2,1)}), bf16[4096,2048]{1,0:T(8,128)(2,1)}) %all-gather.32.cloned.1.call-update) | async-done | bytes 16777232 | tf_op jit(solution)/shard_map/all_gather | solution.py:280
  1027.0 15.8 fusion.208
  1042.8 15.5 fusion.207
  1058.3 19.4 fusion.203
  1077.7 21.1 multiply_reduce_fusion.26
  1102.2 8.0 fusion.320
  1111.1 6.8 multiply_reduce_fusion.14
  1118.0 7.4 multiply_reduce_fusion.16
  1171.8 9.7 fusion.55
  1188.7 7.9 fusion.53
  1199.8 6.6 fusion.142
  1212.6 5.2 bitcast_add_fusion.1
  1222.4 22.9 all-gather.42.cloned.1.call-done
  1245.7 19.3 while.57
  1265.1 7.1 broadcast_multiply_fusion.2
  1277.3 84.5 %all-gather.40.cloned.1.call-done = bf16[384,64,256]{2,1,0:T(8,128)(2,1)} async-done(((bf16[48,64,256]{2,1,0:T(8,128)(2,1)}), bf16[384,64,256]{2,1,0:T(8,128)(2,1)}) %all-gather.40.cloned.1.call-update) | async-done | bytes 12582928 | tf_op jit(solution)/shard_map/all_gather | solution.py:55
  1362.2 18.9 while.56
  1381.2 11.9 multiply_reduce_fusion.9
  1402.6 6.6 multiply_reduce_fusion.13
  1411.3 8.0 convolution_add_fusion.5
  1431.8 6.4 convolution_add_fusion.4
  1439.6 11.9 fusion.285
  1451.5 16.6 convolution_add_fusion.3
  1469.7 13.2 fusion.192
  1482.8 24.7 convolution_add_fusion.2
  1520.1 6.7 broadcast_multiply_fusion
  1533.9 5.5 pad_add_fusion.1
  1566.1 21.9 fusion.173
  1588.1 35.9 convolution_add_fusion.1
  1625.2 26.2 fusion.202
  1651.4 44.3 convolution_add_fusion
  1696.8 8.6 fusion.20
  1705.5 8.3 fusion.21
  1715.6 15.9 fusion.172
  1731.6 6.4 convolution_add_fusion.8
  1738.0 15.7 fusion.174
  1753.7 6.9 fusion.151
  1760.6 43.7 all-reduce.63
  1813.5 97.4 %reduce-scatter.20.cloned.1.call-done = f32[64,1536]{1,0:T(8,128)} async-done(((f32[2048,1536]{1,0:T(8,128)}), f32[64,1536]{1,0:T(8,128)}) %reduce-scatter.20.cloned.1.call-update) | async-done | bytes 393232 | tf_op jit(solution)/shard_map/reduce_scatter | solution.py:526
  1910.9 251.5 %reduce-scatter.18.cloned.1.call-done = f32[96,2048]{1,0:T(8,128)} async-done(((f32[3072,2048]{1,0:T(8,128)}), f32[96,2048]{1,0:T(8,128)}) %reduce-scatter.18.cloned.1.call-update) | async-done | bytes 786448 | tf_op jit(solution)/shard_map/reduce_scatter | solution.py:590
  2162.4 710.3 %reduce-scatter.26.cloned.1.call-done = f32[128,2048]{1,0:T(8,128)} async-done(((f32[4096,2048]{1,0:T(8,128)}), f32[128,2048]{1,0:T(8,128)}) %reduce-scatter.26.cloned.1.call-update) | async-done | bytes 1048592 | tf_op jit(solution)/shard_map/reduce_scatter | solution.py:460
  2872.6 1169.5 %reduce-scatter.16.cloned.1.call-done = f32[64,6704]{1,0:T(8,128)} async-done(((f32[2048,6704]{1,0:T(8,128)}), f32[64,6704]{1,0:T(8,128)}) %reduce-scatter.16.cloned.1.call-update) | async-done | bytes 1716240 | tf_op jit(solution)/shard_map/reduce_scatter | solution.py:583
  4042.1 1407.9 %reduce-scatter.24.cloned.1.call-done = f32[64,8192]{1,0:T(8,128)} async-done(((f32[2048,8192]{1,0:T(8,128)}), f32[64,8192]{1,0:T(8,128)}) %reduce-scatter.24.cloned.1.call-update) | async-done | bytes 2097168 | tf_op jit(solution)/shard_map/reduce_scatter | solution.py:459
  (924 shorter events, 388.4 us)
Async XLA Ops:
  7.2 115.5 %copy-start.9 = (bf16[2,1,128,2048]{3,2,1,0:T(8,128)(2,1)S(1)}, bf16[2,1,128,2048]{3,2,1,0:T(8,128)(2,1)}, u32[]{:S(2)}) copy-start(bf16[2,1,128,2048]{3,2,1,0:T(8,128)(2,1)} %param.24) | copy-start | bytes 3145732
  7.2 116.5 %all-gather.24.cloned.1.call-start = ((), (), s32[]{:S(2)}) async-start(), calls=%async_computation.11 | async-start | bytes 6488064 | tf_op jit(solution)/shard_map/all_gather | solution.py:276
  7.9 244.4 %all-gather.20.cloned.1.call-start = ((), (), s32[]{:S(2)}) async-start(), calls=%async_computation.9 | async-start | bytes 28655616 | tf_op jit(solution)/shard_map/all_gather | solution.py:271
  8.7 338.8 %all-gather.34.cloned.1.call-start = ((), (), s32[]{:S(2)}) async-start(), calls=%async_computation.16 | async-start | bytes 1179648 | tf_op jit(solution)/shard_map/all_gather | solution.py:377
  54.8 217.8 %copy-start.70 = (f32[2048]{0:T(1024)}, f32[2048]{0:T(1024)S(1)}, u32[]{:S(2)}) copy-start(f32[2048]{0:T(1024)S(1)} %convert_element_type.395) | copy-start | bytes 24580
  55.3 68.3 %copy-start.125 = (f32[128,128]{1,0:T(8,128)}, f32[128,128]{1,0:T(8,128)S(1)}, u32[]{:S(2)}) copy-start(f32[128,128]{1,0:T(8,128)S(1)} %pad_maximum_fusion.10) | copy-start | bytes 196612
  55.4 68.2 %copy-start.116 = (f32[128,128]{0,1:T(8,128)}, f32[128,128]{0,1:T(8,128)S(1)}, u32[]{:S(2)}) copy-start(f32[128,128]{0,1:T(8,128)S(1)} %copy.496) | copy-start | bytes 196612
  122.7 209.7 %copy-start.121 = (f32[128,128]{1,0:T(8,128)}, f32[128,128]{1,0:T(8,128)S(1)}, u32[]{:S(2)}) copy-start(f32[128,128]{1,0:T(8,128)S(1)} %pad_maximum_fusion.11) | copy-start | bytes 196612
  123.6 149.1 %copy-start.168 = (f32[128]{0:T(128)}, f32[128]{0:T(128)S(1)}, u32[]{:S(2)}) copy-start(f32[128]{0:T(128)S(1)} %fusion.256) | copy-start | bytes 1540
  123.6 128.8 %copy-start.165 = (f32[128]{0:T(128)}, f32[128]{0:T(128)S(1)}, u32[]{:S(2)}) copy-start(f32[128]{0:T(128)S(1)} %fusion.253) | copy-start | bytes 1540
  133.8 218.1 %all-gather.26.cloned.1.call-start = ((), (), s32[]{:S(2)}) async-start(), calls=%async_computation.12 | async-start | bytes 1179648 | tf_op jit(solution)/shard_map/all_gather | solution.py:377
  138.1 169.3 %copy-start.146 = (f32[3584]{0:T(1024)}, f32[3584]{0:T(1024)S(1)}, u32[]{:S(2)}) copy-start(f32[3584]{0:T(1024)S(1)} %get-tuple-element.550) | copy-start | bytes 43012
  138.1 169.3 %copy-start.147 = (f32[3584]{0:T(1024)}, f32[3584]{0:T(1024)S(1)}, u32[]{:S(2)}) copy-start(f32[3584]{0:T(1024)S(1)} %get-tuple-element.551) | copy-start | bytes 43012
  138.1 169.3 %copy-start.148 = (f32[3584]{0:T(1024)}, f32[3584]{0:T(1024)S(1)}, u32[]{:S(2)}) copy-start(f32[3584]{0:T(1024)S(1)} %get-tuple-element.552) | copy-start | bytes 43012
  138.1 169.3 %copy-start.149 = (f32[3584]{0:T(1024)}, f32[3584]{0:T(1024)S(1)}, u32[]{:S(2)}) copy-start(f32[3584]{0:T(1024)S(1)} %get-tuple-element.553) | copy-start | bytes 43012
  138.9 163.6 %copy-start.225 = (f32[128]{0:T(128)}, f32[128]{0:T(128)S(1)}, u32[]{:S(2)}) copy-start(f32[128]{0:T(128)S(1)} %get-tuple-element.735) | copy-start | bytes 1540
  138.9 163.6 %copy-start.245 = (f32[128]{0:T(128)}, f32[128]{0:T(128)S(1)}, u32[]{:S(2)}) copy-start(f32[128]{0:T(128)S(1)} %get-tuple-element.734) | copy-start | bytes 1540
  138.9 168.6 %copy-start.231 = (f32[128]{0:T(128)}, f32[128]{0:T(128)S(1)}, u32[]{:S(2)}) copy-start(f32[128]{0:T(128)S(1)} %get-tuple-element.736) | copy-start | bytes 1540
  138.9 168.6 %copy-start.234 = (f32[128]{0:T(128)}, f32[128]{0:T(128)S(1)}, u32[]{:S(2)}) copy-start(f32[128]{0:T(128)S(1)} %get-tuple-element.737) | copy-start | bytes 1540
  138.9 168.6 %copy-start.235 = (f32[128]{0:T(128)}, f32[128]{0:T(128)S(1)}, u32[]{:S(2)}) copy-start(f32[128]{0:T(128)S(1)} %get-tuple-element.738) | copy-start | bytes 1540
  139.4 161.6 %copy-start.244 = (f32[48]{0:T(128)}, f32[48]{0:T(128)S(1)}, u32[]{:S(2)}) copy-start(f32[48]{0:T(128)S(1)} %get-tuple-element.723) | copy-start | bytes 580
  139.4 185.4 %copy-start.185 = (f32[48]{0:T(128)}, f32[48]{0:T(128)S(1)}, u32[]{:S(2)}) copy-start(f32[48]{0:T(128)S(1)} %get-tuple-element.724) | copy-start | bytes 580
  140.1 167.4 %copy-start.236 = (f32[128]{0:T(128)}, f32[128]{0:T(128)S(1)}, u32[]{:S(2)}) copy-start(f32[128]{0:T(128)S(1)} %get-tuple-element.729) | copy-start | bytes 1540
  140.1 167.4 %copy-start.238 = (f32[128]{0:T(128)}, f32[128]{0:T(128)S(1)}, u32[]{:S(2)}) copy-start(f32[128]{0:T(128)S(1)} %get-tuple-element.730) | copy-start | bytes 1540
  140.1 167.4 %copy-start.240 = (f32[128]{0:T(128)}, f32[128]{0:T(128)S(1)}, u32[]{:S(2)}) copy-start(f32[128]{0:T(128)S(1)} %get-tuple-element.731) | copy-start | bytes 1540
  140.2 184.7 %copy-start.228 = (f32[128]{0:T(128)}, f32[128]{0:T(128)S(1)}, u32[]{:S(2)}) copy-start(f32[128]{0:T(128)S(1)} %get-tuple-element.728) | copy-start | bytes 1540
  140.2 184.6 %copy-start.247 = (f32[128]{0:T(128)}, f32[128]{0:T(128)S(1)}, u32[]{:S(2)}) copy-start(f32[128]{0:T(128)S(1)} %get-tuple-element.727) | copy-start | bytes 1540
  140.9 296.6 %all-gather.38.cloned.1.call-start = ((), (), s32[]{:S(2)}) async-start(), calls=%async_computation.24 | async-start | bytes 14155776 | tf_op jit(solution)/shard_map/all_gather | solution.py:30
  293.7 9.5 collective-permute-start
  297.4 8.9 collective-permute-start.1
  301.9 65.0 %copy-start.86 = (f32[128,48]{1,0:T(8,128)}, f32[128,48]{1,0:T(8,128)S(1)}, u32[]{:S(2)}) copy-start(f32[128,48]{1,0:T(8,128)S(1)} %reduce_window_sum.35) | copy-start | bytes 73732
  322.0 212.6 %all-gather.22.cloned.1.call-start = ((), (), s32[]{:S(2)}) async-start(), calls=%async_computation.10 | async-start | bytes 12976128 | tf_op jit(solution)/shard_map/all_gather | solution.py:275
  322.6 275.2 %all-gather.28.cloned.1.call-start = ((), (), s32[]{:S(2)}) async-start(), calls=%async_computation.13 | async-start | bytes 4325376 | tf_op jit(solution)/shard_map/all_gather | solution.py:277
  323.3 392.0 %all-gather.36.cloned.1.call-start = ((), (), s32[]{:S(2)}) async-start(), calls=%async_computation.23 | async-start | bytes 14155776 | tf_op jit(solution)/shard_map/all_gather | solution.py:30
  324.2 43.4 copy-start.88
  330.7 580.5 %all-gather.30.cloned.1.call-start = ((), (), s32[]{:S(2)}) async-start(), calls=%async_computation.14 | async-start | bytes 34603008 | tf_op jit(solution)/shard_map/all_gather | solution.py:279
  331.4 695.6 %all-gather.32.cloned.1.call-start = ((), (), s32[]{:S(2)}) async-start(), calls=%async_computation.15 | async-start | bytes 17301504 | tf_op jit(solution)/shard_map/all_gather | solution.py:280
  332.0 913.4 %all-gather.42.cloned.1.call-start = ((), (), s32[]{:S(2)}) async-start(), calls=%async_computation.26 | async-start | bytes 14155776 | tf_op jit(solution)/shard_map/all_gather | solution.py:55
  381.3 744.1 %copy-start.144 = (f32[128,48]{0,1:T(8,128)}, f32[128,48]{0,1:T(8,128)S(1)}, u32[]{:S(2)}) copy-start(f32[128,48]{0,1:T(8,128)S(1)} %copy.519) | copy-start | bytes 73732
  393.0 737.4 %copy-start.143 = (f32[128,48]{0,1:T(8,128)}, f32[128,48]{0,1:T(8,128)S(1)}, u32[]{:S(2)}) copy-start(f32[128,48]{0,1:T(8,128)S(1)} %copy.495) | copy-start | bytes 73732
  394.4 91.3 %copy-start.154 = (f32[128,128]{1,0:T(8,128)}, f32[128,128]{1,0:T(8,128)S(1)}, u32[]{:S(2)}) copy-start(f32[128,128]{1,0:T(8,128)S(1)} %fusion.224) | copy-start | bytes 196612
  395.8 348.7 %copy-start.151 = (f32[128,128]{1,0:T(8,128)}, f32[128,128]{1,0:T(8,128)S(1)}, u32[]{:S(2)}) copy-start(f32[128,128]{1,0:T(8,128)S(1)} %fusion.234) | copy-start | bytes 196612
  496.3 621.6 %copy-start.207 = (f32[128]{0:T(128)}, f32[128]{0:T(128)S(1)}, u32[]{:S(2)}) copy-start(f32[128]{0:T(128)S(1)} %fusion.257) | copy-start | bytes 1540
  602.0 113.3 %copy-start.269 = (f32[128]{0:T(128)}, f32[128]{0:T(128)S(1)}, u32[]{:S(2)}) copy-start(f32[128]{0:T(128)S(1)} %get-tuple-element.753) | copy-start | bytes 1540
  602.0 496.8 %copy-start.179 = (f32[128]{0:T(128)}, f32[128]{0:T(128)S(1)}, u32[]{:S(2)}) copy-start(f32[128]{0:T(128)S(1)} %fusion.258) | copy-start | bytes 1540
  740.4 459.3 %copy-start.3 = (f32[48,64,256]{2,1,0:T(8,128)}, f32[48,64,256]{2,1,0:T(8,128)S(1)}, u32[]{:S(2)}) copy-start(f32[48,64,256]{2,1,0:T(8,128)S(1)} %get-tuple-element.375) | copy-start | bytes 9437188
  753.6 364.4 %copy-start.205 = (f32[128]{0:T(128)}, f32[128]{0:T(128)S(1)}, u32[]{:S(2)}) copy-start(f32[128]{0:T(128)S(1)} %fusion.254) | copy-start | bytes 1540
  761.7 149.5 %copy-start.102 = (f32[2048]{0:T(1024)S(1)}, f32[2048]{0:T(1024)}, u32[]{:S(2)}) copy-start(f32[2048]{0:T(1024)} %convert_element_type.419) | copy-start | bytes 24580
  763.5 335.4 %copy-start.177 = (f32[128]{0:T(128)}, f32[128]{0:T(128)S(1)}, u32[]{:S(2)}) copy-start(f32[128]{0:T(128)S(1)} %fusion.255) | copy-start | bytes 1540
  1130.3 231.6 %all-gather.40.cloned.1.call-start = ((), (), s32[]{:S(2)}) async-start(), calls=%async_computation.25 | async-start | bytes 14155776 | tf_op jit(solution)/shard_map/all_gather | solution.py:55
  1135.6 289.9 %reduce-scatter.28.cloned.1.call-start = ((), (), s32[]{:S(2)}) async-start(), calls=%async_computation.27 | async-start | bytes 1179648
  1196.6 230.9 %reduce-scatter.30.cloned.1.call-start = ((), (), s32[]{:S(2)}) async-start(), calls=%async_computation.28 | async-start | bytes 1179648
  1222.4 589.6 %reduce-scatter.32.cloned.1.call-start = ((), (), s32[]{:S(2)}) async-start(), calls=%async_computation.29 | async-start | bytes 1892352
  1411.2 402.3 %reduce-scatter.22.cloned.1.call-start = ((), (), s32[]{:S(2)}) async-start(), calls=%async_computation.20 | async-start | bytes 8650752 | tf_op jit(solution)/shard_map/reduce_scatter | solution.py:527
  1419.3 491.6 %reduce-scatter.20.cloned.1.call-start = ((), (), s32[]{:S(2)}) async-start(), calls=%async_computation.19 | async-start | bytes 12976128 | tf_op jit(solution)/shard_map/reduce_scatter | solution.py:526
  1438.2 724.1 %reduce-scatter.18.cloned.1.call-start = ((), (), s32[]{:S(2)}) async-start(), calls=%async_computation.18 | async-start | bytes 25952256 | tf_op jit(solution)/shard_map/reduce_scatter | solution.py:590
  1468.1 1404.5 %reduce-scatter.26.cloned.1.call-start = ((), (), s32[]{:S(2)}) async-start(), calls=%async_computation.22 | async-start | bytes 34603008 | tf_op jit(solution)/shard_map/reduce_scatter | solution.py:460
  1507.6 2534.5 %reduce-scatter.16.cloned.1.call-start = ((), (), s32[]{:S(2)}) async-start(), calls=%async_computation.17 | async-start | bytes 57311232 | tf_op jit(solution)/shard_map/reduce_scatter | solution.py:583
  1532.6 24.5 collective-permute-start.3
  1542.5 16.0 collective-permute-start.2
  1624.0 3826.0 %reduce-scatter.24.cloned.1.call-start = ((), (), s32[]{:S(2)}) async-start(), calls=%async_computation.21 | async-start | bytes 69206016 | tf_op jit(solution)/shard_map/reduce_scatter | solution.py:459
  1753.6 53.5 copy-start.251
  1753.7 53.5 copy-start.253
  1753.7 53.5 copy-start.257
  (235 other events, 1343.4 us)
Sparse Core Ops, SparseCore 0:
  10.9 72.6 all-gather.23
  86.5 165.7 all-gather.19
  254.0 20.2 all-gather.33
  275.8 21.6 all-gather.25
  322.1 115.3 all-gather.37
  440.2 94.2 all-gather.21
  537.4 60.2 all-gather.27
  600.0 115.2 all-gather.35
  718.2 192.9 all-gather.29
  913.9 113.0 all-gather.31
  1130.4 114.8 all-gather.41
  1246.9 114.9 all-gather.39
  1364.1 30.6 reduce-scatter.27
  1396.9 30.5 reduce-scatter.29
  1429.7 134.8 reduce-scatter.31
  1567.4 179.5 reduce-scatter.21
  1754.5 156.3 reduce-scatter.19
  1917.7 244.5 reduce-scatter.17
  2165.3 707.2 reduce-scatter.25
  2875.5 1166.5 reduce-scatter.15
  4045.2 1404.7 reduce-scatter.23
where the time goes:
time: 5470 us; the launch traced here: 5460 us
  waiting for transfers between devices  4340 us (79%)
  matrix products  603 us (11%)
  other arithmetic  219 us (4%)
  blocking collectives  175 us (3%)
  local copies, waits for them, and re-layouts  93.9 us (2%)
    reduce_scatter x1, waiting for transfers between devices, local(): lax.psum_scatter(ffn_totals[0], ('seq', 'dp'), scatter_dimension=0, tiled...  1410 us
    reduce_scatter x1, waiting for transfers between devices, local(): lax.psum_scatter(mixer_totals[1], ('seq', 'dp'), scatter_dimension=0, til...  1170 us
    reduce_scatter x1, waiting for transfers between devices, local(): lax.psum_scatter(ffn_totals[1], ('seq', 'dp'), scatter_dimension=0, tiled...  710 us
    reduce_scatter x1, waiting for transfers between devices, local(): lax.psum_scatter(mixer_totals[6], ('seq', 'dp'), scatter_dimension=0, til...  251 us
    dot_general x12, matrix products, cross_rows(): lax.dot_general(left, right, (((0,), (0,)), ((), ())), preferred_element_...  215 us
    all_gather x2, waiting for transfers between devices, entering_2(): lax.all_gather(part.astype(kind), axis)  155 us
    all_gather x1, waiting for transfers between devices, local(): lax.all_gather(shards[9], ('seq', 'dp'), axis=0, tiled=True)  148 us
    dot_general x12, matrix products, back_dot(): lax.dot_general(grads, weight, (((1,), (1,)), ((), ())), preferred_elemen...  141 us
  transfers between devices with their start and end apart: 25, of which 15 were waited for; matrix products, arithmetic and copies ran while one was open for 15% of the time, Pallas kernels for 0%

commit v1 on v0

v1 whole, which is shorter than its diff:
```python
from functools import partial

import jax
import jax.numpy as jnp
from jax import lax
from jax.sharding import PartitionSpec as P

D = 2048
FF = 4096
HEADS = 48
HEAD_DIM = 64
STATE = 256
ATT_HEADS = 8
KV_HEADS = 2
ATT_DIM = 128
INNER = HEADS * HEAD_DIM
CONV = 4
DT_PAD = 128

epsilon = 1e-05
rope_base = 10000.0
f32 = jnp.float32
bf16 = jnp.bfloat16


def permuted(value, axis, by):
    pairs = [(i, i ^ by) for i in range(lax.axis_size(axis))]
    return lax.ppermute(value, axis, pairs)


def small_gather(value):
    rows = value[None]
    for axis in ("dp", "seq"):
        here = lax.axis_index(axis)
        by = 1
        while by < lax.axis_size(axis):
            other = permuted(rows, axis, by)
            upper = (here & by) != 0
            rows = jnp.where(
                upper, jnp.concatenate([other, rows]), jnp.concatenate([rows, other])
            )
            by *= 2
    return rows


def summed(value, axes):
    for axis in axes:
        by = 1
        while by < lax.axis_size(axis):
            value = value + permuted(value, axis, by)
            by *= 2
    return value


def turned_order(value, here, count):
    by = 1
    tail = value.shape[1:]
    while by < count:
        split = value.reshape(count // (2 * by), 2, by, *tail)
        flipped = jnp.concatenate([split[:, 1:], split[:, :1]], axis=1)
        value = jnp.where((here & by) != 0, flipped, split).reshape(count, *tail)
        by *= 2
    return value


def exchanged(blocks, axis):
    count, here = lax.axis_size(axis), lax.axis_index(axis)
    ready = turned_order(blocks, here, count)
    got = [ready[0]] + [permuted(ready[k], axis, k) for k in range(1, count)]
    return turned_order(jnp.stack(got), here, count)


def dp_gather(value):
    if lax.axis_size("dp") != 4:
        return lax.all_gather(value, "dp", axis=0)
    half = value.shape[0] // 2
    one = permuted(value, "dp", 1)
    two = permuted(value, "dp", 2)
    three = jnp.concatenate([permuted(one[:half], "dp", 2), permuted(two[half:], "dp", 1)])
    return jnp.stack([value, one, two, three])


def dp_scatter(total):
    if lax.axis_size("dp") != 4:
        return lax.psum_scatter(total, "dp", scatter_dimension=0).astype(f32)
    half = total.shape[1] // 2
    low, high = total[:, :half], total[:, half:]
    low_in = permuted(jnp.stack([low[1], low[3]]), "dp", 1).astype(f32)
    high_in = permuted(high[2:], "dp", 2).astype(f32)
    low_on = (low[2].astype(f32) + low_in[1]).astype(bf16)
    high_on = (high[1].astype(f32) + high_in[1]).astype(bf16)
    low_own = low[0].astype(f32) + low_in[0] + permuted(low_on, "dp", 2).astype(f32)
    high_own = high[0].astype(f32) + high_in[0] + permuted(high_on, "dp", 1).astype(f32)
    return jnp.concatenate([low_own, high_own])


def segment_of(positions, end_points):
    counted = jnp.sum((end_points[None, :] <= positions[:, None]).astype(jnp.int32), axis=1)
    return jnp.where(positions < 0, -1, counted)


def rope_tables(positions):
    half = ATT_DIM // 2
    freqs = jnp.power(rope_base, -jnp.arange(half, dtype=f32) * (2.0 / ATT_DIM))
    angles = positions.astype(f32)[:, None] * freqs[None, :]
    cosine, sine = jnp.cos(angles), jnp.sin(angles)
    return jnp.concatenate([cosine, cosine], axis=1), jnp.concatenate([sine, sine], axis=1)


def turned(values, cosine, sine):
    half = ATT_DIM // 2
    swapped = jnp.concatenate([-values[..., half:], values[..., :half]], axis=-1)
    return values * cosine + swapped * sine


def turned_back(values, cosine, sine):
    return turned(values, cosine, -sine)


def rms_row(values):
    return lax.rsqrt(jnp.mean(values * values, axis=-1, keepdims=True) + epsilon)


def rms_back(grad, values, gain):
    r = rms_row(values)
    scaled = grad * gain
    along = jnp.mean(scaled * values, axis=-1, keepdims=True)
    return scaled * r - values * (r * r * r) * along, jnp.sum(grad * values * r, axis=0)


def silu_back(value):
    sig = jax.nn.sigmoid(value)
    return sig * (1.0 + value * (1.0 - sig))


def dot(left, right):
    return jnp.dot(left, right, preferred_element_type=f32)


def dot_t(left, right):
    return lax.dot_general(left, right, (((1,), (1,)), ((), ())), preferred_element_type=f32)


def cross(left, right):
    return lax.dot_general(left, right, (((0,), (0,)), ((), ())), preferred_element_type=f32)


def mixer_core(x_in, bc_in, dt_raw, gate_z, w_x, b_x, w_bc, b_bc, head, seg, blocks):
    rows, inner = x_in.shape
    heads = head.shape[1]
    width = inner // heads
    per = rows // blocks
    conv_in = jnp.concatenate([x_in, bc_in], axis=1)
    weight = jnp.concatenate([w_x, w_bc], axis=1)
    total = jnp.concatenate([b_x, b_bc])[None, :]
    for tap in range(CONV):
        back = CONV - 1 - tap
        if back:
            moved = jnp.pad(conv_in[: rows - back], ((back, 0), (0, 0)))
            seg_moved = jnp.pad(seg[: rows - back], (back, 0), constant_values=-1)
        else:
            moved, seg_moved = conv_in, seg
        same = (seg_moved == seg).astype(f32)[:, None]
        total = total + moved * weight[tap][None, :] * same
    conv_out = jax.nn.silu(total)
    step = jax.nn.softplus(dt_raw + head[1][None, :])
    decay = -jnp.exp(head[0])[None, :] * step
    tril = jnp.tril(jnp.ones((per, per), f32))
    cum = jnp.einsum(
        "ts,bsh->bth", tril, decay.reshape(blocks, per, heads), precision=lax.Precision.HIGHEST
    )
    step = step.reshape(blocks, per, heads)
    x = conv_out[:, :inner].reshape(blocks, per, heads, width)
    b = conv_out[:, inner : inner + STATE].reshape(blocks, per, STATE)
    c = conv_out[:, inner + STATE :].reshape(blocks, per, STATE)
    seg_b = seg.reshape(blocks, per)
    prior = jnp.concatenate([jnp.full((1,), -1, jnp.int32), seg_b[:-1, per - 1]])
    order = jnp.arange(per)
    within = (order[None, :, None] >= order[None, None, :]) & (
        seg_b[:, :, None] == seg_b[:, None, :]
    )
    entering = (seg_b == prior[:, None]).astype(f32)
    last = seg_b[:, per - 1]
    trailing = (seg_b == last[:, None]).astype(f32)
    passing = (last == prior).astype(f32)
    both = jnp.einsum("btn,bsn->bts", c, b, preferred_element_type=f32)
    gap = cum[:, :, None, :] - cum[:, None, :, :]
    mask = within[..., None]
    mixing = both[..., None] * jnp.where(mask, jnp.exp(jnp.where(mask, gap, 0.0)), 0.0)
    mixing = mixing * step[:, None, :, :]
    y = jnp.einsum("btsh,bshp->bthp", mixing, x, preferred_element_type=f32)
    end = cum[:, per - 1]
    keeping = jnp.exp(end[:, None, :] - cum) * trailing[:, :, None] * step
    states = jnp.einsum("bshp,bsn->bhpn", x * keeping[..., None], b, preferred_element_type=f32)
    passed = jnp.exp(end) * passing[:, None]
    state = jnp.zeros(states.shape[1:], f32)
    entered = []
    for k in range(blocks):
        entered.append(state)
        state = passed[k][:, None, None] * state + states[k]
    entered = jnp.stack(entered)
    carried = jnp.einsum("btn,bhpn->bthp", c, entered, preferred_element_type=f32)
    y = y + carried * (jnp.exp(cum) * entering[..., None])[..., None]
    y = y + head[2][None, None, :, None] * x
    return y.reshape(rows, inner) * jax.nn.silu(gate_z)


def local(
    tokens,
    doc_ends,
    input_gain,
    mixer_in,
    conv_weight,
    conv_bias,
    head_params,
    mixer_gain,
    mixer_out,
    attn_qkv,
    attn_out,
    ffn_gain,
    gate_up,
    down_proj,
    out_grad,
):
    n = lax.axis_size("seq")
    nd = lax.axis_size("dp")
    s = lax.axis_index("seq")
    d = lax.axis_index("dp")
    micro, _, per, _ = tokens.shape
    own = micro * per
    length = n * per
    rows = n * own
    owner = mixer_in.shape[0]
    inner = INNER // n
    heads = HEADS // n
    ffl = FF // n
    parts = n // ATT_HEADS
    group = ATT_HEADS // KV_HEADS
    scale = ATT_DIM ** (-0.5)
    conv_ch = INNER + 2 * STATE

    def dp_order(value):
        return turned_order(value, d, nd) if nd == 4 else value

    def mixed_order(value):
        split = dp_order(value.reshape(own, n, nd, owner).transpose(2, 0, 1, 3))
        return split.transpose(1, 0, 2, 3).reshape(own, D)

    def plain_order(value):
        split = dp_order(value.reshape(own, nd, n, owner).transpose(1, 0, 2, 3))
        return split.transpose(1, 2, 0, 3).reshape(own, D)

    def row_weight(value):
        return dp_order(dp_gather(value)).reshape(-1, D)

    def row_grad(total):
        return dp_scatter(dp_order(total.reshape(nd, -1, D)))

    def to_seq(value):
        return value.reshape(n, micro, per, -1).transpose(1, 0, 2, 3).reshape(micro, length, -1)

    def from_seq(value):
        return value.reshape(micro, n, per, -1).transpose(1, 0, 2, 3).reshape(rows, -1)

    def gathered(value):
        return lax.all_gather(value, "seq", axis=0, tiled=True)

    def scattered(value):
        return lax.psum_scatter(
            value.astype(bf16), "seq", scatter_dimension=0, tiled=True
        ).astype(f32)

    token_rows = tokens.reshape(own, D).astype(f32)
    grad_rows = out_grad.reshape(own, D)

    cols = [
        mixer_in[:, :INNER].reshape(owner, n, inner).transpose(1, 0, 2),
        mixer_in[:, INNER : 2 * INNER].reshape(owner, n, inner).transpose(1, 0, 2),
        jnp.broadcast_to(
            mixer_in[:, 2 * INNER : 2 * INNER + 2 * STATE][None], (n, owner, 2 * STATE)
        ),
        jnp.pad(
            mixer_in[:, 2 * INNER + 2 * STATE :].reshape(owner, n, heads).transpose(1, 0, 2),
            ((0, 0), (0, 0), (0, DT_PAD - heads)),
        ),
    ]
    by_head = attn_qkv.reshape(owner, ATT_HEADS + 2 * KV_HEADS, ATT_DIM).transpose(1, 0, 2)
    q_of = [k // parts for k in range(n)]
    k_of = [ATT_HEADS + q // group for q in q_of]
    v_of = [ATT_HEADS + KV_HEADS + q // group for q in q_of]
    for of in (q_of, k_of, v_of):
        cols.append(jnp.stack([by_head[k] for k in of]))
    sizes = [inner, inner, 2 * STATE, DT_PAD, ATT_DIM, ATT_DIM, ATT_DIM]
    starts = [sum(sizes[:k]) for k in range(len(sizes) + 1)]
    sent_in = exchanged(jnp.concatenate(cols, axis=2), "seq")
    w_in = dp_gather(sent_in).reshape(D, starts[-1])
    sent_gu = exchanged(
        gate_up.reshape(owner, 2, n, ffl).transpose(2, 0, 1, 3).reshape(n, owner, 2 * ffl), "seq"
    )
    w_gu = dp_gather(sent_gu).reshape(D, 2 * ffl)
    w_mix = row_weight(mixer_out)
    w_att = row_weight(attn_out)
    if parts > 1:
        other = permuted(w_att, "seq", 1)
        w_att = jnp.where(
            (s & 1) != 0, jnp.concatenate([other, w_att]), jnp.concatenate([w_att, other])
        )
    w_down = row_weight(down_proj)

    tap_count = conv_weight.shape[1]
    small = small_gather(
        jnp.concatenate(
            [input_gain, conv_weight.reshape(-1), conv_bias, mixer_gain, ffn_gain]
        )
    )
    cuts = [owner, CONV * tap_count, tap_count, mixer_gain.shape[0], owner]
    at = [sum(cuts[:k]) for k in range(len(cuts) + 1)]
    small = small.astype(f32)
    gain_in = small[:, at[0] : at[1]].reshape(-1)
    taps = (
        small[:, at[1] : at[2]].reshape(-1, CONV, tap_count).transpose(1, 0, 2).reshape(CONV, -1)
    )
    shift = small[:, at[2] : at[3]].reshape(-1)
    gain_mix = lax.dynamic_slice_in_dim(
        small[:, at[3] : at[4]].reshape(-1), s * inner, inner
    )
    gain_ffn = small[:, at[4] : at[5]].reshape(-1)
    w_x = lax.dynamic_slice_in_dim(taps, s * inner, inner, axis=1)
    b_x = lax.dynamic_slice_in_dim(shift, s * inner, inner)
    w_bc, b_bc = taps[:, INNER:], shift[INNER:]
    head = lax.dynamic_slice_in_dim(head_params, s * heads, heads, axis=1)

    normed_own = (token_rows * rms_row(token_rows) * gain_in).astype(bf16)
    normed = gathered(mixed_order(normed_own))
    grads = gathered(lax.optimization_barrier((grad_rows, normed[:8, :128]))[0])
    mixed = dot(normed, w_in)
    gate_z, x_in, bc_in, dt_raw, q_raw, k_raw, v_raw = (
        mixed[:, starts[k] : starts[k + 1]] for k in range(7)
    )
    positions = jnp.arange(length, dtype=jnp.int32)
    seg = jnp.stack([segment_of(positions, doc_ends[m, 0]) for m in range(micro)])

    def core(gate_z, x_in, bc_in, dt_raw, w_x, b_x, w_bc, b_bc, head):
        def one(z, x, bc, dt, seg_m):
            return mixer_core(x, bc, dt, z, w_x, b_x, w_bc, b_bc, head, seg_m, n)

        return from_seq(
            jax.vmap(one)(to_seq(gate_z), to_seq(x_in), to_seq(bc_in), to_seq(dt_raw), seg)
        )

    gated, pull_core = jax.vjp(
        core,
        gate_z,
        x_in.astype(bf16).astype(f32),
        bc_in.astype(bf16).astype(f32),
        dt_raw[:, :heads],
        w_x,
        b_x,
        w_bc,
        b_bc,
        head,
    )
    squares = summed(jnp.sum(gated * gated, axis=1), ("seq",)) / INNER
    r_mix = lax.rsqrt(squares + epsilon)[:, None]
    mixer_b = (gated * r_mix * gain_mix).astype(bf16)

    cosine, sine = rope_tables(positions)
    queries = turned(to_seq(q_raw), cosine, sine).astype(bf16)
    keys = turned(to_seq(k_raw), cosine, sine).astype(bf16)
    values = to_seq(v_raw).astype(bf16)
    part = s % parts

    def taken(value):
        if parts == 1:
            return value
        split = value.reshape(micro, n // parts, parts, per, -1)
        split = lax.dynamic_index_in_dim(split, part, 2, False)
        return split.reshape(micro, length // parts, -1)

    def put_back(value):
        if parts == 1:
            return value
        split = value.reshape(micro, n // parts, 1, per, -1)
        here = (jnp.arange(parts) == part)[None, None, :, None, None]
        return jnp.where(here, split, 0).reshape(micro, length, -1)

    q_pos = taken(jnp.broadcast_to(positions[None, :, None], (micro, length, 1)))
    q_seg = taken(seg[:, :, None])
    queries = taken(queries)
    visible = (positions[None, None, :] <= q_pos) & (seg[:, None, :] == q_seg)
    scores = jnp.einsum("mtd,mkd->mtk", queries, keys, preferred_element_type=f32) * scale
    scores = jnp.where(visible, scores, -1e30)
    top = jnp.max(scores, axis=-1, keepdims=True)
    expd = jnp.exp(scores - top)
    probs_b = (expd / jnp.sum(expd, axis=-1, keepdims=True)).astype(bf16)
    attended = jnp.einsum("mtk,mkd->mtd", probs_b, values, preferred_element_type=f32)
    attended_b = from_seq(put_back(attended.astype(bf16)))
    branches = dot(mixer_b, w_mix) + dot(attended_b, w_att)
    branches, _ = lax.optimization_barrier((branches.astype(bf16), grads[:8, :128]))
    hidden = token_rows + scattered(branches)
    ffn_own = (hidden * rms_row(hidden) * gain_ffn).astype(bf16)
    ffn_in = gathered(mixed_order(ffn_own))
    gate_vals = dot(ffn_in, w_gu)
    gate, up = gate_vals[:, :ffl], gate_vals[:, ffl:]
    activated_b = (jax.nn.silu(gate) * up).astype(bf16)
    ffn_out = dot(activated_b, w_down)

    act_grad = dot_t(grads, w_down)
    gate_grad = jnp.concatenate(
        [act_grad * up * silu_back(gate), act_grad * jax.nn.silu(gate)], axis=1
    ).astype(bf16)
    ffn_in_grad = plain_order(scattered(dot_t(gate_grad, w_gu)))
    gu_total = cross(ffn_in, gate_grad).astype(bf16)
    down_total = cross(activated_b, grads).astype(bf16)
    hidden_part, ffn_gain_grad = rms_back(ffn_in_grad, hidden, gain_ffn)
    hidden_grad = hidden_part + grad_rows.astype(f32)
    hidden_b = gathered(hidden_grad.astype(bf16))

    ffn_out, _ = lax.optimization_barrier((ffn_out.astype(bf16), hidden_b[:8, :128]))
    layer_out = (hidden + scattered(ffn_out)).astype(bf16)

    att_grad = taken(to_seq(dot_t(hidden_b, w_att).astype(bf16)))
    probs = probs_b.astype(f32)
    probs_grad = jnp.einsum("mtd,mkd->mtk", att_grad, values, preferred_element_type=f32)
    scores_grad = (
        probs * (probs_grad - jnp.sum(probs * probs_grad, axis=-1, keepdims=True))
    ).astype(bf16)
    q_grad = jnp.einsum("mtk,mkd->mtd", scores_grad, keys, preferred_element_type=f32) * scale
    k_grad = jnp.einsum("mtk,mtd->mkd", scores_grad, queries, preferred_element_type=f32) * scale
    v_grad = jnp.einsum("mtk,mtd->mkd", probs_b, att_grad, preferred_element_type=f32)
    q_grad = from_seq(turned_back(put_back(q_grad), cosine, sine).astype(bf16))
    k_grad = from_seq(turned_back(k_grad, cosine, sine).astype(bf16))
    v_grad = from_seq(v_grad.astype(bf16))

    mix_grad = dot_t(hidden_b, w_mix)
    scaled = mix_grad * gain_mix
    along = summed(jnp.sum(scaled * gated, axis=1), ("seq",))[:, None] / INNER
    mix_gain_grad = jnp.sum(mix_grad * gated * r_mix, axis=0)
    gated_grad = scaled * r_mix - gated * (r_mix * r_mix * r_mix) * along
    z_g, x_g, bc_g, dt_g, w_x_g, b_x_g, w_bc_g, b_bc_g, head_g = pull_core(gated_grad)
    mixed_grad = jnp.concatenate(
        [
            z_g.astype(bf16),
            x_g.astype(bf16),
            bc_g.astype(bf16),
            jnp.pad(dt_g, ((0, 0), (0, DT_PAD - heads))).astype(bf16),
            q_grad,
            k_grad,
            v_grad,
        ],
        axis=1,
    )
    in_back, _ = lax.optimization_barrier(
        (dot_t(mixed_grad, w_in).astype(bf16), layer_out[:8, :128])
    )
    normed_grad = plain_order(scattered(in_back))
    in_total = cross(normed, mixed_grad).astype(bf16)
    mix_total = cross(mixer_b, hidden_b).astype(bf16)
    att_total = cross(attended_b, hidden_b).astype(bf16)
    token_part, in_gain_grad = rms_back(normed_grad, token_rows, gain_in)
    token_grad = token_part + hidden_grad

    def to_owners(total):
        part_sum = dp_scatter(total.reshape(nd, n * owner, -1)).astype(bf16)
        return exchanged(part_sum.reshape(n, owner, -1), "seq").astype(f32)

    gu_sum = to_owners(gu_total)
    gate_up_grad = (
        gu_sum.reshape(n, owner, 2, ffl).transpose(1, 2, 0, 3).reshape(owner, 2 * FF)
    )
    down_grad = row_grad(down_total)
    mixer_out_grad = row_grad(mix_total)
    if parts > 1:
        half = att_total.shape[0] // 2
        low, high = att_total[:half], att_total[half:]
        odd = (s & 1) != 0
        other = permuted(jnp.where(odd, low, high), "seq", 1)
        att_total = (jnp.where(odd, high, low).astype(f32) + other.astype(f32)).astype(bf16)
    attn_out_grad = row_grad(att_total)
    in_sum = to_owners(in_total)
    pieces = [in_sum[:, :, starts[k] : starts[k + 1]] for k in range(7)]
    mixer_in_grad = jnp.concatenate(
        [
            pieces[0].transpose(1, 0, 2).reshape(owner, INNER),
            pieces[1].transpose(1, 0, 2).reshape(owner, INNER),
            jnp.sum(pieces[2], axis=0),
            pieces[3][:, :, :heads].transpose(1, 0, 2).reshape(owner, HEADS),
        ],
        axis=1,
    )
    q_sum = pieces[4].reshape(ATT_HEADS, parts, owner, ATT_DIM).sum(axis=1)
    k_sum = pieces[5].reshape(KV_HEADS, n // KV_HEADS, owner, ATT_DIM).sum(axis=1)
    v_sum = pieces[6].reshape(KV_HEADS, n // KV_HEADS, owner, ATT_DIM).sum(axis=1)
    attn_qkv_grad = (
        jnp.concatenate([q_sum, k_sum, v_sum]).transpose(1, 0, 2).reshape(owner, -1)
    )

    def placed(value, width):
        full = jnp.zeros(value.shape[:-1] + (width,), f32)
        return lax.dynamic_update_slice_in_dim(
            full, value, s * value.shape[-1], axis=value.ndim - 1
        )

    conv_full = jnp.concatenate([placed(jnp.concatenate([w_x_g, b_x_g[None]]), INNER),
                                 jnp.concatenate([w_bc_g, b_bc_g[None]])], axis=1)
    flat = jnp.concatenate(
        [
            ffn_gain_grad,
            placed(mix_gain_grad, INNER),
            conv_full.reshape(-1),
            placed(head_g, HEADS).reshape(-1),
        ]
    )
    flat = jnp.concatenate(
        [summed(in_gain_grad, ("seq", "dp")), summed(flat, ("seq", "dp"))]
    )
    index = s * nd + d

    def mine(value):
        width = value.shape[-1] // (n * nd)
        return lax.dynamic_slice_in_dim(value, index * width, width, axis=value.ndim - 1)

    ends = [D, 2 * D, 2 * D + INNER, 2 * D + INNER + (CONV + 1) * conv_ch]
    conv_full = flat[ends[2] : ends[3]].reshape(CONV + 1, conv_ch)
    conv_own = mine(conv_full)
    return (
        layer_out.reshape(micro, 1, per, D),
        token_grad.reshape(micro, 1, per, D),
        mine(flat[: ends[0]]),
        mixer_in_grad,
        conv_own[:CONV],
        conv_own[CONV],
        flat[ends[3] :].reshape(3, HEADS),
        mine(flat[ends[1] : ends[2]]),
        mixer_out_grad,
        attn_qkv_grad,
        attn_out_grad,
        mine(flat[ends[0] : ends[1]]),
        gate_up_grad,
        down_grad,
    )


def solution(mesh):
    rows = P(("seq", "dp"), None)
    vector = P(("seq", "dp"))
    activations = P(None, "dp", "seq", None)
    return jax.shard_map(
        local,
        mesh=mesh,
        in_specs=(
            activations,
            P(None, "dp", None),
            vector,
            rows,
            P(None, ("seq", "dp")),
            vector,
            P(),
            vector,
            rows,
            rows,
            rows,
            vector,
            rows,
            rows,
            activations,
        ),
        out_specs=(
            activations,
            activations,
            vector,
            rows,
            P(None, ("seq", "dp")),
            vector,
            P(),
            vector,
            rows,
            rows,
            rows,
            vector,
            rows,
            rows,
        ),
        check_vma=False,
    )
```

time: 5470 us -> 1440 us (0.26)
  waiting for transfers between devices: 4340 us -> 611 us
  matrix products: 603 us -> 212 us
  blocking collectives: 175 us -> 0 us
  starting transfers between devices: 8.04 us -> 168 us
  local copies, waits for them, and re-layouts: 93.9 us -> 199 us
    reduce_scatter x6 -> x4, waiting for transfers between devices: 3640 us -> 175 us  [scattered(): lax.psum_scatter(value.astype(bf16), 'seq', scatter_dimension=0, tiled=True)]
    all_gather x12 -> x4, waiting for transfers between devices: 695 us -> 127 us  [gathered(): return lax.all_gather(value, 'seq', axis=0, tiled=True)]
    dot_general x72 -> x34, matrix products: 603 us -> 206 us  [the longest x5 63.9 us: dot(): return jnp.dot(left, right, preferred_element_type=f32)]
    ppermute x4 -> x89, waiting for transfers between devices: 0.02 us -> 309 us  [permuted(): return lax.ppermute(value, axis, pairs)]
    ppermute x4 -> x89, starting transfers between devices: 6.84 us -> 168 us  [permuted(): return lax.ppermute(value, axis, pairs)]
    all_gather x3 -> x0, blocking collectives: 88.1 us -> none  [the longest x1 67.1 us: local(): lax.all_gather(shards[2], ('seq', 'dp'), axis=1, tiled=True)]
    unnamed x2 -> x0, blocking collectives: 86.4 us -> none
  transfers between devices with their start and end apart: 25 -> 97, of which waited for: 15 -> 43; matrix products, arithmetic and copies ran while one was open for 15% -> 21% of each run, Pallas kernels for 0% -> 0%
where the time goes in v1:
time: 1440 us; the launch traced here: 1430 us
  waiting for transfers between devices  611 us (42%)
  other arithmetic  220 us (15%)
  matrix products  212 us (15%)
  local copies, waits for them, and re-layouts  199 us (14%)
  starting transfers between devices  168 us (12%)
  between operations  19.5 us (1%)
    ppermute x89, waiting for transfers between devices, permuted(): return lax.ppermute(value, axis, pairs)  309 us
    reduce_scatter x4, waiting for transfers between devices, scattered(): lax.psum_scatter(value.astype(bf16), 'seq', scatter_dimension=0, tiled=True)  175 us
    ppermute x89, starting transfers between devices, permuted(): return lax.ppermute(value, axis, pairs)  168 us
    all_gather x4, waiting for transfers between devices, gathered(): return lax.all_gather(value, 'seq', axis=0, tiled=True)  127 us
    dot_general x5, matrix products, dot(): return jnp.dot(left, right, preferred_element_type=f32)  63.9 us
    unnamed x551, local copies, waits for them, and re-layouts  62.3 us
    dot_general x5, matrix products, dot_t(): lax.dot_general(left, right, (((1,), (1,)), ((), ())), preferred_element_...  58.8 us
    dot_general x5, matrix products, cross(): lax.dot_general(left, right, (((0,), (0,)), ((), ())), preferred_element_...  48.7 us
  transfers between devices with their start and end apart: 97, of which 43 were waited for; matrix products, arithmetic and copies ran while one was open for 21% of the time, Pallas kernels for 0%

profile of v1, /device:TPU:0, one launch (start us, length us, event | category | flops | bytes accessed | tf_op | source)
XLA Modules:
  0.0 1429.4 jit_solution(10058010683661844964)
XLA Ops:
  80.0 13.6 collective-permute-done.6
  93.6 9.8 collective-permute-done.7
  105.6 5.0 collective-permute-done.8
  113.2 29.7 %collective-permute-done.9 = bf16[64,1792]{1,0:T(8,128)(2,1)S(1)} collective-permute-done((bf16[64,1792]{1,0:T(8,128)(2,1)S(1)}, bf16[64,1792]{1,0:T(8,128)(2,1)S(1)}, u32[]{:S(2)}, u32[]{:S(2)}) %collective-permute-start.9) | collective-permute-done | bytes 229408 | tf_op jit(solution)/shard_map/ppermute | solution.py:28
  151.5 40.2 %collective-permute-done.21 = bf16[48,2048]{1,0:T(8,128)(2,1)S(1)} collective-permute-done((bf16[48,2048]{1,0:T(8,128)(2,1)S(1)}, bf16[48,2048]{1,0:T(8,128)(2,1)S(1)}, u32[]{:S(2)}, u32[]{:S(2)}) %collective-permute-start.21) | collective-permute-done | bytes 196640 | tf_op jit(solution)/shard_map/ppermute | solution.py:28
  199.2 16.8 %collective-permute-done.14 = bf16[4,64,1792]{2,1,0:T(8,128)(2,1)S(1)} collective-permute-done((bf16[4,64,1792]{2,1,0:T(8,128)(2,1)S(1)}, bf16[4,64,1792]{2,1,0:T(8,128)(2,1)S(1)}, u32[]{:S(2)}, u32[]{:S(2)}) %collective-permute-start.14) | collective-permute-done | bytes 917536 | tf_op jit(solution)/shard_map/ppermute | solution.py:28
  217.3 3.8 pad_maximum_fusion
  221.1 21.9 %fusion.307 = (bf16[2048,1792]{1,0:T(8,128)(2,1)}, f32[2048,1792]{1,0:T(8,128)S(1)}) fusion(bf16[2048,2048]{0,1:T(8,128)(2,1)} %all-gather.5.cloned.1.call-done, bf16[2048,1792]{1,0:T(8,128)(2,1)} %bitcast.1375), kind=kOutput, calls=%fused_computation.776 | convolution fusion | flops 15036055552 | bytes 37748736 | tf_op jit(solution)/shard_map/dot_general | solution.py:137
  253.6 8.8 fusion.6
  269.5 3.8 slice.1242
  288.6 4.0 copy.788
  303.3 4.6 fusion.47
  311.5 5.6 fusion.44
  317.9 5.3 fusion.308
  323.2 31.3 %collective-permute-start.17 = (f32[2048]{0:T(1024)S(1)}, f32[2048]{0:T(1024)S(1)}, u32[]{:S(2)}, u32[]{:S(2)}) collective-permute-start(f32[2048]{0:T(1024)S(1)} %add.512), channel_id=1, source_target_pairs={{0,8},{4,12},{8,0},{12,4},{16,24},{20,28},{24,16},{28,20},{1,9},{5... | collective-permute-start | bytes 24584 | tf_op jit(solution)/shard_map/ppermute | solution.py:28
  354.5 4.6 divide_convert_fusion
  367.4 8.1 fusion.313
  375.5 11.4 add_convert_fusion
  387.7 86.5 %reduce-scatter.5.cloned.1.call-done = bf16[256,2048]{1,0:T(8,128)(2,1)} async-done(((bf16[2048,2048]{1,0:T(8,128)(2,1)}), bf16[256,2048]{1,0:T(8,128)(2,1)}) %reduce-scatter.5.cloned.1.call-update) | async-done | bytes 1048592 | tf_op jit(solution)/shard_map/reduce_scatter | solution.py:269
  495.2 12.7 collective-permute-done.28
  508.0 15.7 %collective-permute-done.29 = bf16[64,1024]{1,0:T(8,128)(2,1)S(1)} collective-permute-done((bf16[64,1024]{1,0:T(8,128)(2,1)S(1)}, bf16[64,1024]{1,0:T(8,128)(2,1)S(1)}, u32[]{:S(2)}, u32[]{:S(2)}) %collective-permute-start.29) | collective-permute-done | bytes 131104 | tf_op jit(solution)/shard_map/ppermute | solution.py:28
  527.5 7.2 collective-permute-done.32
  534.7 5.0 collective-permute-done.33
  547.5 24.5 %collective-permute-done.40 = bf16[64,2048]{1,0:T(8,128)(2,1)S(1)} collective-permute-done((bf16[64,2048]{1,0:T(8,128)(2,1)S(1)}, bf16[64,2048]{1,0:T(8,128)(2,1)S(1)}, u32[]{:S(2)}, u32[]{:S(2)}) %collective-permute-start.40) | collective-permute-done | bytes 262176 | tf_op jit(solution)/shard_map/ppermute | solution.py:28
  577.4 10.6 collective-permute-done.36
  590.9 15.7 %fusion.314 = f32[2048,1024]{0,1:T(8,128)} fusion(bf16[2048,2048]{0,1:T(8,128)(2,1)} %all-gather.7.cloned.1.call-done, bf16[2048,1024]{1,0:T(8,128)(2,1)} %bitcast.1403), kind=kOutput, calls=%fused_computation.782 | convolution fusion | flops 8589934592 | bytes 20971520 | tf_op jit(solution)/shard_map/dot_general | solution.py:137
  606.6 59.1 %all-gather.9.cloned.1.call-done = bf16[2048,2048]{1,0:T(8,128)(2,1)} async-done(((bf16[256,2048]{1,0:T(8,128)(2,1)}), bf16[2048,2048]{1,0:T(8,128)(2,1)}) %all-gather.9.cloned.1.call-update) | async-done | bytes 8388624 | tf_op jit(solution)/shard_map/all_gather | solution.py:266
  665.6 12.3 fusion.17
  679.2 13.3 convolution_convert_fusion.2
  692.6 88.3 %reduce-scatter.9.cloned.1.call-done = bf16[256,2048]{1,0:T(8,128)(2,1)} async-done(((bf16[2048,2048]{1,0:T(8,128)(2,1)}), bf16[256,2048]{1,0:T(8,128)(2,1)}) %reduce-scatter.9.cloned.1.call-update) | async-done | bytes 1048592 | tf_op jit(solution)/shard_map/reduce_scatter | solution.py:269
  796.2 3.9 fusion.111
  806.7 67.8 %all-gather.11.cloned.1.call-done = bf16[2048,2048]{1,0:T(8,128)(2,1)} async-done(((bf16[256,2048]{1,0:T(8,128)(2,1)}), bf16[2048,2048]{1,0:T(8,128)(2,1)}) %all-gather.11.cloned.1.call-update) | async-done | bytes 8388624 | tf_op jit(solution)/shard_map/all_gather | solution.py:266
  874.5 5.9 convolution_convert_fusion.8
  890.2 8.1 fusion.41
  914.1 5.1 multiply_reduce_fusion.5
  921.5 7.6 fusion.25
  935.3 4.4 fusion.28
  956.4 14.0 multiply_reduce_fusion.2
  970.5 8.1 multiply_reduce_fusion.3
  978.6 4.4 slice_multiply_fusion.1
  984.3 4.4 slice_multiply_fusion
  988.8 4.4 slice_multiply_fusion.2
  993.3 9.0 add_convert_fusion.1
  1023.7 19.2 %convolution_convert_fusion.1 = bf16[2048,2048]{1,0:T(8,128)(2,1)} fusion(bf16[2048,1792]{1,0:T(8,128)(2,1)} %constant_dynamic-update-slice_fusion.20, bf16[2048,1792]{1,0:T(8,128)(2,1)S(1)} %bitcast.1378), kind=kOutput, calls=%fused_computation.13 | convolution fusion | flops 15036579840 | bytes 23068672 | tf_op jit(solution)/shard_map/dot_general | solution.py:141
  1044.5 12.4 convolution_convert_fusion.4
  1063.1 8.2 convolution_convert_fusion.5
  1078.9 16.7 %collective-permute-done.85 = bf16[2,64,2048]{2,1,0:T(8,128)(2,1)} collective-permute-done((bf16[2,64,2048]{2,1,0:T(8,128)(2,1)}, bf16[2,64,2048]{2,1,0:T(8,128)(2,1)}, u32[]{:S(2)}, u32[]{:S(2)}) %collective-permute-start.85) | collective-permute-done | bytes 524320 | tf_op jit(solution)/shard_map/ppermute | solution.py:28
  1110.1 6.8 convolution_convert_fusion.3
  1133.0 5.2 collective-permute-done.79
  1140.6 4.8 collective-permute-done.83
  1168.2 4.1 convert_bitcast_fusion
  1176.1 4.9 convolution_convert_fusion.7
  1195.0 19.7 %convolution_convert_fusion = bf16[2048,1792]{1,0:T(8,128)(2,1)S(1)} fusion(bf16[2048,2048]{0,1:T(8,128)(2,1)} %all-gather.5.cloned.1.call-done, bf16[2048,1792]{1,0:T(8,128)(2,1)} %constant_dynamic-update-slice_fusion.20), kind=kOutput, calls=%fused_computation.12 | convolution fusion | flops 15036055552 | bytes 23068672 | tf_op jit(solution)/shard_map/dot_general | solution.py:145
  1222.5 4.0 fusion.58
  1232.1 18.7 %collective-permute-start.62 = (f32[23184]{0:T(1024)S(1)}, f32[23184]{0:T(1024)S(1)}, u32[]{:S(2)}, u32[]{:S(2)}) collective-permute-start(f32[23184]{0:T(1024)S(1)} %fusion.369), channel_id=1, source_target_pairs={{0,8},{4,12},{8,0},{12,4},{16,24},{20,28},{24,16},{28,20},{1,9},{5... | collective-permute-start | bytes 278216 | tf_op jit(solution)/shard_map/ppermute | solution.py:28
  1256.0 18.7 %collective-permute-done.71 = bf16[16,2048]{1,0:T(8,128)(2,1)S(1)} collective-permute-done((bf16[16,2048]{1,0:T(8,128)(2,1)S(1)}, bf16[16,2048]{1,0:T(8,128)(2,1)S(1)}, u32[]{:S(2)}, u32[]{:S(2)}) %collective-permute-start.71) | collective-permute-done | bytes 65568 | tf_op jit(solution)/shard_map/ppermute | solution.py:28
  1275.3 19.2 %collective-permute-start.63 = (f32[23184]{0:T(1024)S(1)}, f32[23184]{0:T(1024)S(1)}, u32[]{:S(2)}, u32[]{:S(2)}) collective-permute-start(f32[23184]{0:T(1024)S(1)} %add.558), channel_id=1, source_target_pairs={{0,16},{4,20},{8,24},{12,28},{16,0},{20,4},{24,8},{28,12},{1,17},{... | collective-permute-start | bytes 278216 | tf_op jit(solution)/shard_map/ppermute | solution.py:28
  1306.0 4.5 fusion.138
  1319.7 12.7 collective-permute-done.67
  1341.2 4.0 collective-permute-start.55
  1349.4 10.4 collective-permute-done.55
  1364.4 13.2 collective-permute-done.58
  1394.7 9.5 collective-permute-start.46
  1415.6 6.0 fusion.83
  (1188 shorter events, 460.8 us)
Async XLA Ops:
  7.2 213.9 %all-gather.5.cloned.1.call-start = ((), (), s32[]{:S(2)}) async-start(), calls=%async_computation.4 | async-start | bytes 9437184 | tf_op jit(solution)/shard_map/all_gather | solution.py:266
  7.2 140.0 %collective-permute-start.19 = (bf16[96,2048]{1,0:T(8,128)(2,1)}, bf16[96,2048]{1,0:T(8,128)(2,1)}, u32[]{:S(2)}, u32[]{:S(2)}) collective-permute-start(bf16[96,2048]{1,0:T(8,128)(2,1)} %param.23), channel_id=1, source_target_pairs={{0,1},{1,0},{2,3},{3,2},{4,5},{5,4},{6,7},{7,6},{8,9},{9,8},{10,11... | collective-permute-start | bytes 1179656 | tf_op jit(solution)/shard_map/ppermute | solution.py:28
  10.2 139.0 %collective-permute-start.20 = (bf16[96,2048]{1,0:T(8,128)(2,1)}, bf16[96,2048]{1,0:T(8,128)(2,1)}, u32[]{:S(2)}, u32[]{:S(2)}) collective-permute-start(bf16[96,2048]{1,0:T(8,128)(2,1)} %param.23), channel_id=1, source_target_pairs={{0,2},{1,3},{2,0},{3,1},{4,6},{5,7},{6,4},{7,5},{8,10},{9,11},{10,... | collective-permute-start | bytes 1179656 | tf_op jit(solution)/shard_map/ppermute | solution.py:28
  11.8 56.3 %collective-permute-start.23 = (bf16[32,2048]{1,0:T(8,128)(2,1)}, bf16[32,2048]{1,0:T(8,128)(2,1)}, u32[]{:S(2)}, u32[]{:S(2)}) collective-permute-start(bf16[32,2048]{1,0:T(8,128)(2,1)} %param.25), channel_id=1, source_target_pairs={{0,1},{1,0},{2,3},{3,2},{4,5},{5,4},{6,7},{7,6},{8,9},{9,8},{10,11... | collective-permute-start | bytes 393224 | tf_op jit(solution)/shard_map/ppermute | solution.py:28
  12.3 58.2 %collective-permute-start.24 = (bf16[32,2048]{1,0:T(8,128)(2,1)}, bf16[32,2048]{1,0:T(8,128)(2,1)}, u32[]{:S(2)}, u32[]{:S(2)}) collective-permute-start(bf16[32,2048]{1,0:T(8,128)(2,1)} %param.25), channel_id=1, source_target_pairs={{0,2},{1,3},{2,0},{3,1},{4,6},{5,7},{6,4},{7,5},{8,10},{9,11},{10,... | collective-permute-start | bytes 393224 | tf_op jit(solution)/shard_map/ppermute | solution.py:28
  15.9 27.8 %collective-permute-start = (bf16[1,784]{1,0:T(2,128)(2,1)S(1)}, bf16[1,784]{1,0:T(2,128)(2,1)S(1)}, u32[]{:S(2)}, u32[]{:S(2)}) collective-permute-start(bf16[1,784]{1,0:T(2,128)(2,1)S(1)} %broadcast_in_dim.75), channel_id=1, source_target_pairs={{0,1},{1,0},{2,3},{3,2},{4,5},{5,4},{6,7},{7,6},{8,9},{9,8},{10,11... | collective-permute-start | bytes 4712 | tf_op jit(solution)/shard_map/ppermute | solution.py:28
  62.0 17.1 %collective-permute-start.5 = (bf16[64,1792]{1,0:T(8,128)(2,1)}, bf16[64,1792]{1,0:T(8,128)(2,1)S(1)}, u32[]{:S(2)}, u32[]{:S(2)}) collective-permute-start(bf16[64,1792]{1,0:T(8,128)(2,1)} %get-tuple-element.259), channel_id=1, source_target_pairs={{0,4},{4,0},{8,12},{12,8},{16,20},{20,16},{24,28},{28,24},{1,5},{5... | collective-permute-start | bytes 688136 | tf_op jit(solution)/shard_map/ppermute | solution.py:28
  66.6 407.6 %reduce-scatter.5.cloned.1.call-start = ((), (), s32[]{:S(2)}) async-start(), calls=%async_computation.5 | async-start | bytes 9437184 | tf_op jit(solution)/shard_map/reduce_scatter | solution.py:269
  73.5 20.1 %collective-permute-start.6 = (bf16[64,1792]{1,0:T(8,128)(2,1)S(1)}, bf16[64,1792]{1,0:T(8,128)(2,1)S(1)}, u32[]{:S(2)}, u32[]{:S(2)}) collective-permute-start(bf16[64,1792]{1,0:T(8,128)(2,1)S(1)} %copy-done.133), channel_id=1, source_target_pairs={{0,8},{4,12},{8,0},{12,4},{16,24},{20,28},{24,16},{28,20},{1,9},{5... | collective-permute-start | bytes 688136 | tf_op jit(solution)/shard_map/ppermute | solution.py:28
  75.6 27.8 %collective-permute-start.7 = (bf16[64,1792]{1,0:T(8,128)(2,1)S(1)}, bf16[64,1792]{1,0:T(8,128)(2,1)S(1)}, u32[]{:S(2)}, u32[]{:S(2)}) collective-permute-start(bf16[64,1792]{1,0:T(8,128)(2,1)S(1)} %copy-done.132), channel_id=1, source_target_pairs={{0,12},{4,8},{8,4},{12,0},{16,28},{20,24},{24,20},{28,16},{1,13},{... | collective-permute-start | bytes 688136 | tf_op jit(solution)/shard_map/ppermute | solution.py:28
  79.1 31.5 %collective-permute-start.8 = (bf16[64,1792]{1,0:T(8,128)(2,1)S(1)}, bf16[64,1792]{1,0:T(8,128)(2,1)S(1)}, u32[]{:S(2)}, u32[]{:S(2)}) collective-permute-start(bf16[64,1792]{1,0:T(8,128)(2,1)S(1)} %copy-done.131), channel_id=1, source_target_pairs={{0,16},{4,20},{8,24},{12,28},{16,0},{20,4},{24,8},{28,12},{1,17},{... | collective-permute-start | bytes 688136 | tf_op jit(solution)/shard_map/ppermute | solution.py:28
  93.5 49.3 %collective-permute-start.9 = (bf16[64,1792]{1,0:T(8,128)(2,1)S(1)}, bf16[64,1792]{1,0:T(8,128)(2,1)S(1)}, u32[]{:S(2)}, u32[]{:S(2)}) collective-permute-start(bf16[64,1792]{1,0:T(8,128)(2,1)S(1)} %copy-done.130), channel_id=1, source_target_pairs={{0,20},{4,16},{8,28},{12,24},{16,4},{20,0},{24,12},{28,8},{1,21},{... | collective-permute-start | bytes 688136 | tf_op jit(solution)/shard_map/ppermute | solution.py:28
  103.3 39.5 %collective-permute-start.10 = (bf16[64,1792]{1,0:T(8,128)(2,1)S(1)}, bf16[64,1792]{1,0:T(8,128)(2,1)S(1)}, u32[]{:S(2)}, u32[]{:S(2)}) collective-permute-start(bf16[64,1792]{1,0:T(8,128)(2,1)S(1)} %copy-done.129), channel_id=1, source_target_pairs={{0,24},{4,28},{8,16},{12,20},{16,8},{20,12},{24,0},{28,4},{1,25},{... | collective-permute-start | bytes 688136 | tf_op jit(solution)/shard_map/ppermute | solution.py:28
  110.6 32.3 %collective-permute-start.11 = (bf16[64,1792]{1,0:T(8,128)(2,1)S(1)}, bf16[64,1792]{1,0:T(8,128)(2,1)S(1)}, u32[]{:S(2)}, u32[]{:S(2)}) collective-permute-start(bf16[64,1792]{1,0:T(8,128)(2,1)S(1)} %copy-done.128), channel_id=1, source_target_pairs={{0,28},{4,24},{8,20},{12,16},{16,12},{20,8},{24,4},{28,0},{1,29},{... | collective-permute-start | bytes 688136 | tf_op jit(solution)/shard_map/ppermute | solution.py:28
  144.9 49.9 %collective-permute-start.12 = (bf16[8,64,1792]{2,1,0:T(8,128)(2,1)S(1)}, bf16[8,64,1792]{2,1,0:T(8,128)(2,1)S(1)}, u32[]{:S(2)}, u32[]{:S(2)}) collective-permute-start(bf16[8,64,1792]{2,1,0:T(8,128)(2,1)S(1)} %fusion.101), channel_id=1, source_target_pairs={{0,1},{1,0},{2,3},{3,2},{4,5},{5,4},{6,7},{7,6},{8,9},{9,8},{10,11... | collective-permute-start | bytes 5505032 | tf_op jit(solution)/shard_map/ppermute | solution.py:28
  146.0 50.1 %collective-permute-start.13 = (bf16[8,64,1792]{2,1,0:T(8,128)(2,1)S(1)}, bf16[8,64,1792]{2,1,0:T(8,128)(2,1)S(1)}, u32[]{:S(2)}, u32[]{:S(2)}) collective-permute-start(bf16[8,64,1792]{2,1,0:T(8,128)(2,1)S(1)} %fusion.101), channel_id=1, source_target_pairs={{0,2},{1,3},{2,0},{3,1},{4,6},{5,7},{6,4},{7,5},{8,10},{9,11},{10,... | collective-permute-start | bytes 5505032 | tf_op jit(solution)/shard_map/ppermute | solution.py:28
  148.1 43.6 %collective-permute-start.21 = (bf16[48,2048]{1,0:T(8,128)(2,1)S(1)}, bf16[48,2048]{1,0:T(8,128)(2,1)S(1)}, u32[]{:S(2)}, u32[]{:S(2)}) collective-permute-start(bf16[48,2048]{1,0:T(8,128)(2,1)S(1)} %slice.1244), channel_id=1, source_target_pairs={{0,2},{1,3},{2,0},{3,1},{4,6},{5,7},{6,4},{7,5},{8,10},{9,11},{10,... | collective-permute-start | bytes 589832 | tf_op jit(solution)/shard_map/ppermute | solution.py:28
  150.2 41.6 %collective-permute-start.22 = (bf16[48,2048]{1,0:T(8,128)(2,1)S(1)}, bf16[48,2048]{1,0:T(8,128)(2,1)S(1)}, u32[]{:S(2)}, u32[]{:S(2)}) collective-permute-start(bf16[48,2048]{1,0:T(8,128)(2,1)S(1)} %slice.1245), channel_id=1, source_target_pairs={{0,1},{1,0},{2,3},{3,2},{4,5},{5,4},{6,7},{7,6},{8,9},{9,8},{10,11... | collective-permute-start | bytes 589832 | tf_op jit(solution)/shard_map/ppermute | solution.py:28
  194.9 21.1 %collective-permute-start.14 = (bf16[4,64,1792]{2,1,0:T(8,128)(2,1)S(1)}, bf16[4,64,1792]{2,1,0:T(8,128)(2,1)S(1)}, u32[]{:S(2)}, u32[]{:S(2)}) collective-permute-start(bf16[4,64,1792]{2,1,0:T(8,128)(2,1)S(1)} %slice.1198), channel_id=1, source_target_pairs={{0,2},{1,3},{2,0},{3,1},{4,6},{5,7},{6,4},{7,5},{8,10},{9,11},{10,... | collective-permute-start | bytes 2752520 | tf_op jit(solution)/shard_map/ppermute | solution.py:28
  196.2 21.0 %collective-permute-start.15 = (bf16[4,64,1792]{2,1,0:T(8,128)(2,1)S(1)}, bf16[4,64,1792]{2,1,0:T(8,128)(2,1)S(1)}, u32[]{:S(2)}, u32[]{:S(2)}) collective-permute-start(bf16[4,64,1792]{2,1,0:T(8,128)(2,1)S(1)} %slice.1199), channel_id=1, source_target_pairs={{0,1},{1,0},{2,3},{3,2},{4,5},{5,4},{6,7},{7,6},{8,9},{9,8},{10,11... | collective-permute-start | bytes 2752520 | tf_op jit(solution)/shard_map/ppermute | solution.py:28
  323.2 37.5 %collective-permute-start.17 = (f32[2048]{0:T(1024)S(1)}, f32[2048]{0:T(1024)S(1)}, u32[]{:S(2)}, u32[]{:S(2)}) collective-permute-start(f32[2048]{0:T(1024)S(1)} %add.512), channel_id=1, source_target_pairs={{0,8},{4,12},{8,0},{12,4},{16,24},{20,28},{24,16},{28,20},{1,9},{5... | collective-permute-start | bytes 24584 | tf_op jit(solution)/shard_map/ppermute | solution.py:28
  387.0 203.9 %all-gather.7.cloned.1.call-start = ((), (), s32[]{:S(2)}) async-start(), calls=%async_computation.6 | async-start | bytes 9437184 | tf_op jit(solution)/shard_map/all_gather | solution.py:266
  479.0 186.6 %all-gather.9.cloned.1.call-start = ((), (), s32[]{:S(2)}) async-start(), calls=%async_computation.8 | async-start | bytes 9437184 | tf_op jit(solution)/shard_map/all_gather | solution.py:266
  479.6 301.3 %reduce-scatter.9.cloned.1.call-start = ((), (), s32[]{:S(2)}) async-start(), calls=%async_computation.9 | async-start | bytes 9437184 | tf_op jit(solution)/shard_map/reduce_scatter | solution.py:269
  479.6 61.6 %collective-permute-start.38 = (bf16[128,2048]{1,0:T(8,128)(2,1)}, bf16[128,2048]{1,0:T(8,128)(2,1)}, u32[]{:S(2)}, u32[]{:S(2)}) collective-permute-start(bf16[128,2048]{1,0:T(8,128)(2,1)} %param.28), channel_id=1, source_target_pairs={{0,1},{1,0},{2,3},{3,2},{4,5},{5,4},{6,7},{7,6},{8,9},{9,8},{10,11... | collective-permute-start | bytes 1572872 | tf_op jit(solution)/shard_map/ppermute | solution.py:28
  481.1 63.1 %collective-permute-start.39 = (bf16[128,2048]{1,0:T(8,128)(2,1)}, bf16[128,2048]{1,0:T(8,128)(2,1)}, u32[]{:S(2)}, u32[]{:S(2)}) collective-permute-start(bf16[128,2048]{1,0:T(8,128)(2,1)} %param.28), channel_id=1, source_target_pairs={{0,2},{1,3},{2,0},{3,1},{4,6},{5,7},{6,4},{7,5},{8,10},{9,11},{10,... | collective-permute-start | bytes 1572872 | tf_op jit(solution)/shard_map/ppermute | solution.py:28
  493.3 14.7 %collective-permute-start.28 = (bf16[64,1024]{1,0:T(8,128)(2,1)S(1)}, bf16[64,1024]{1,0:T(8,128)(2,1)S(1)}, u32[]{:S(2)}, u32[]{:S(2)}) collective-permute-start(bf16[64,1024]{1,0:T(8,128)(2,1)S(1)} %get-tuple-element.333), channel_id=1, source_target_pairs={{0,8},{4,12},{8,0},{12,4},{16,24},{20,28},{24,16},{28,20},{1,9},{5... | collective-permute-start | bytes 393224 | tf_op jit(solution)/shard_map/ppermute | solution.py:28
  493.3 30.4 %collective-permute-start.29 = (bf16[64,1024]{1,0:T(8,128)(2,1)S(1)}, bf16[64,1024]{1,0:T(8,128)(2,1)S(1)}, u32[]{:S(2)}, u32[]{:S(2)}) collective-permute-start(bf16[64,1024]{1,0:T(8,128)(2,1)S(1)} %get-tuple-element.332), channel_id=1, source_target_pairs={{0,12},{4,8},{8,4},{12,0},{16,28},{20,24},{24,20},{28,16},{1,13},{... | collective-permute-start | bytes 393224 | tf_op jit(solution)/shard_map/ppermute | solution.py:28
  495.1 29.9 %collective-permute-start.30 = (bf16[64,1024]{1,0:T(8,128)(2,1)S(1)}, bf16[64,1024]{1,0:T(8,128)(2,1)S(1)}, u32[]{:S(2)}, u32[]{:S(2)}) collective-permute-start(bf16[64,1024]{1,0:T(8,128)(2,1)S(1)} %get-tuple-element.331), channel_id=1, source_target_pairs={{0,16},{4,20},{8,24},{12,28},{16,0},{20,4},{24,8},{28,12},{1,17},{... | collective-permute-start | bytes 393224 | tf_op jit(solution)/shard_map/ppermute | solution.py:28
  508.0 19.5 %collective-permute-start.31 = (bf16[64,1024]{1,0:T(8,128)(2,1)S(1)}, bf16[64,1024]{1,0:T(8,128)(2,1)S(1)}, u32[]{:S(2)}, u32[]{:S(2)}) collective-permute-start(bf16[64,1024]{1,0:T(8,128)(2,1)S(1)} %get-tuple-element.330), channel_id=1, source_target_pairs={{0,20},{4,16},{8,28},{12,24},{16,4},{20,0},{24,12},{28,8},{1,21},{... | collective-permute-start | bytes 393224 | tf_op jit(solution)/shard_map/ppermute | solution.py:28
  525.1 14.7 %collective-permute-start.33 = (bf16[64,1024]{1,0:T(8,128)(2,1)S(1)}, bf16[64,1024]{1,0:T(8,128)(2,1)S(1)}, u32[]{:S(2)}, u32[]{:S(2)}) collective-permute-start(bf16[64,1024]{1,0:T(8,128)(2,1)S(1)} %get-tuple-element.328), channel_id=1, source_target_pairs={{0,28},{4,24},{8,20},{12,16},{16,12},{20,8},{24,4},{28,0},{1,29},{... | collective-permute-start | bytes 393224 | tf_op jit(solution)/shard_map/ppermute | solution.py:28
  540.9 33.6 %collective-permute-start.34 = (bf16[8,64,1024]{2,1,0:T(8,128)(2,1)S(1)}, bf16[8,64,1024]{2,1,0:T(8,128)(2,1)S(1)}, u32[]{:S(2)}, u32[]{:S(2)}) collective-permute-start(bf16[8,64,1024]{2,1,0:T(8,128)(2,1)S(1)} %fusion.133), channel_id=1, source_target_pairs={{0,1},{1,0},{2,3},{3,2},{4,5},{5,4},{6,7},{7,6},{8,9},{9,8},{10,11... | collective-permute-start | bytes 3145736 | tf_op jit(solution)/shard_map/ppermute | solution.py:28
  541.0 34.0 %collective-permute-start.35 = (bf16[8,64,1024]{2,1,0:T(8,128)(2,1)S(1)}, bf16[8,64,1024]{2,1,0:T(8,128)(2,1)S(1)}, u32[]{:S(2)}, u32[]{:S(2)}) collective-permute-start(bf16[8,64,1024]{2,1,0:T(8,128)(2,1)S(1)} %fusion.133), channel_id=1, source_target_pairs={{0,2},{1,3},{2,0},{3,1},{4,6},{5,7},{6,4},{7,5},{8,10},{9,11},{10,... | collective-permute-start | bytes 3145736 | tf_op jit(solution)/shard_map/ppermute | solution.py:28
  542.2 29.8 %collective-permute-start.40 = (bf16[64,2048]{1,0:T(8,128)(2,1)S(1)}, bf16[64,2048]{1,0:T(8,128)(2,1)S(1)}, u32[]{:S(2)}, u32[]{:S(2)}) collective-permute-start(bf16[64,2048]{1,0:T(8,128)(2,1)S(1)} %slice.1292), channel_id=1, source_target_pairs={{0,2},{1,3},{2,0},{3,1},{4,6},{5,7},{6,4},{7,5},{8,10},{9,11},{10,... | collective-permute-start | bytes 786440 | tf_op jit(solution)/shard_map/ppermute | solution.py:28
  545.3 26.8 %collective-permute-start.41 = (bf16[64,2048]{1,0:T(8,128)(2,1)S(1)}, bf16[64,2048]{1,0:T(8,128)(2,1)S(1)}, u32[]{:S(2)}, u32[]{:S(2)}) collective-permute-start(bf16[64,2048]{1,0:T(8,128)(2,1)S(1)} %slice.1293), channel_id=1, source_target_pairs={{0,1},{1,0},{2,3},{3,2},{4,5},{5,4},{6,7},{7,6},{8,9},{9,8},{10,11... | collective-permute-start | bytes 786440 | tf_op jit(solution)/shard_map/ppermute | solution.py:28
  692.6 181.9 %all-gather.11.cloned.1.call-start = ((), (), s32[]{:S(2)}) async-start(), calls=%async_computation.10 | async-start | bytes 9437184 | tf_op jit(solution)/shard_map/all_gather | solution.py:266
  793.9 589.4 %reduce-scatter.11.cloned.1.call-start = ((), (), s32[]{:S(2)}) async-start(), calls=%async_computation.11 | async-start | bytes 9437184 | tf_op jit(solution)/shard_map/reduce_scatter | solution.py:269
  1042.9 372.6 %reduce-scatter.7.cloned.1.call-start = ((), (), s32[]{:S(2)}) async-start(), calls=%async_computation.7 | async-start | bytes 9437184 | tf_op jit(solution)/shard_map/reduce_scatter | solution.py:269
  1060.2 41.7 %collective-permute-start.74 = (bf16[2,256,1024]{2,1,0:T(8,128)(2,1)}, bf16[2,256,1024]{2,1,0:T(8,128)(2,1)}, u32[]{:S(2)}, u32[]{:S(2)}) collective-permute-start(bf16[2,256,1024]{2,1,0:T(8,128)(2,1)} %pad_maximum_fusion.43), channel_id=1, source_target_pairs={{0,1},{1,0},{2,3},{3,2},{4,5},{5,4},{6,7},{7,6},{8,9},{9,8},{10,11... | collective-permute-start | bytes 3145736 | tf_op jit(solution)/shard_map/ppermute | solution.py:28
  1061.7 41.8 %collective-permute-start.76 = (bf16[2,256,1024]{2,1,0:T(8,128)(2,1)}, bf16[2,256,1024]{2,1,0:T(8,128)(2,1)}, u32[]{:S(2)}, u32[]{:S(2)}) collective-permute-start(bf16[2,256,1024]{2,1,0:T(8,128)(2,1)} %slice.1389), channel_id=1, source_target_pairs={{0,2},{1,3},{2,0},{3,1},{4,6},{5,7},{6,4},{7,5},{8,10},{9,11},{10,... | collective-permute-start | bytes 3145736 | tf_op jit(solution)/shard_map/ppermute | solution.py:28
  1073.8 21.9 %collective-permute-start.85 = (bf16[2,64,2048]{2,1,0:T(8,128)(2,1)}, bf16[2,64,2048]{2,1,0:T(8,128)(2,1)}, u32[]{:S(2)}, u32[]{:S(2)}) collective-permute-start(bf16[2,64,2048]{2,1,0:T(8,128)(2,1)} %pad_maximum_fusion.59), channel_id=1, source_target_pairs={{0,1},{1,0},{2,3},{3,2},{4,5},{5,4},{6,7},{7,6},{8,9},{9,8},{10,11... | collective-permute-start | bytes 1572872 | tf_op jit(solution)/shard_map/ppermute | solution.py:28
  1075.2 21.6 %collective-permute-start.87 = (bf16[2,64,2048]{2,1,0:T(8,128)(2,1)}, bf16[2,64,2048]{2,1,0:T(8,128)(2,1)}, u32[]{:S(2)}, u32[]{:S(2)}) collective-permute-start(bf16[2,64,2048]{2,1,0:T(8,128)(2,1)} %slice.1424), channel_id=1, source_target_pairs={{0,2},{1,3},{2,0},{3,1},{4,6},{5,7},{6,4},{7,5},{8,10},{9,11},{10,... | collective-permute-start | bytes 1572872 | tf_op jit(solution)/shard_map/ppermute | solution.py:28
  1099.0 18.0 %collective-permute-start.86 = (bf16[64,2048]{1,0:T(8,128)(2,1)}, bf16[64,2048]{1,0:T(8,128)(2,1)S(1)}, u32[]{:S(2)}, u32[]{:S(2)}) collective-permute-start(bf16[64,2048]{1,0:T(8,128)(2,1)} %get-tuple-element.191), channel_id=1, source_target_pairs={{0,2},{1,3},{2,0},{3,1},{4,6},{5,7},{6,4},{7,5},{8,10},{9,11},{10,... | collective-permute-start | bytes 786440 | tf_op jit(solution)/shard_map/ppermute | solution.py:28
  1100.5 16.6 %collective-permute-start.88 = (bf16[64,2048]{1,0:T(8,128)(2,1)}, bf16[64,2048]{1,0:T(8,128)(2,1)}, u32[]{:S(2)}, u32[]{:S(2)}) collective-permute-start(bf16[64,2048]{1,0:T(8,128)(2,1)} %get-tuple-element.192), channel_id=1, source_target_pairs={{0,1},{1,0},{2,3},{3,2},{4,5},{5,4},{6,7},{7,6},{8,9},{9,8},{10,11... | collective-permute-start | bytes 786440 | tf_op jit(solution)/shard_map/ppermute | solution.py:28
  1182.9 67.9 %collective-permute-start.70 = (bf16[2,16,2048]{2,1,0:T(8,128)(2,1)}, bf16[2,16,2048]{2,1,0:T(8,128)(2,1)}, u32[]{:S(2)}, u32[]{:S(2)}) collective-permute-start(bf16[2,16,2048]{2,1,0:T(8,128)(2,1)} %pad_maximum_fusion.62), channel_id=1, source_target_pairs={{0,1},{1,0},{2,3},{3,2},{4,5},{5,4},{6,7},{7,6},{8,9},{9,8},{10,11... | collective-permute-start | bytes 393224 | tf_op jit(solution)/shard_map/ppermute | solution.py:28
  1184.3 67.4 %collective-permute-start.72 = (bf16[2,16,2048]{2,1,0:T(8,128)(2,1)}, bf16[2,16,2048]{2,1,0:T(8,128)(2,1)}, u32[]{:S(2)}, u32[]{:S(2)}) collective-permute-start(bf16[2,16,2048]{2,1,0:T(8,128)(2,1)} %slice.1377), channel_id=1, source_target_pairs={{0,2},{1,3},{2,0},{3,1},{4,6},{5,7},{6,4},{7,5},{8,10},{9,11},{10,... | collective-permute-start | bytes 393224 | tf_op jit(solution)/shard_map/ppermute | solution.py:28
  1230.5 73.5 %collective-permute-start.50 = (bf16[2,256,1792]{2,1,0:T(8,128)(2,1)S(1)}, bf16[2,256,1792]{2,1,0:T(8,128)(2,1)S(1)}, u32[]{:S(2)}, u32[]{:S(2)}) collective-permute-start(bf16[2,256,1792]{2,1,0:T(8,128)(2,1)S(1)} %pad_maximum_fusion.20), channel_id=1, source_target_pairs={{0,1},{1,0},{2,3},{3,2},{4,5},{5,4},{6,7},{7,6},{8,9},{9,8},{10,11... | collective-permute-start | bytes 5505032 | tf_op jit(solution)/shard_map/ppermute | solution.py:28
  1231.6 72.6 %collective-permute-start.52 = (bf16[2,256,1792]{2,1,0:T(8,128)(2,1)S(1)}, bf16[2,256,1792]{2,1,0:T(8,128)(2,1)S(1)}, u32[]{:S(2)}, u32[]{:S(2)}) collective-permute-start(bf16[2,256,1792]{2,1,0:T(8,128)(2,1)S(1)} %slice.1317), channel_id=1, source_target_pairs={{0,2},{1,3},{2,0},{3,1},{4,6},{5,7},{6,4},{7,5},{8,10},{9,11},{10,... | collective-permute-start | bytes 5505032 | tf_op jit(solution)/shard_map/ppermute | solution.py:28
  1232.1 21.9 %collective-permute-start.62 = (f32[23184]{0:T(1024)S(1)}, f32[23184]{0:T(1024)S(1)}, u32[]{:S(2)}, u32[]{:S(2)}) collective-permute-start(f32[23184]{0:T(1024)S(1)} %fusion.369), channel_id=1, source_target_pairs={{0,8},{4,12},{8,0},{12,4},{16,24},{20,28},{24,16},{28,20},{1,9},{5... | collective-permute-start | bytes 278216 | tf_op jit(solution)/shard_map/ppermute | solution.py:28
  1252.7 22.1 %collective-permute-start.71 = (bf16[16,2048]{1,0:T(8,128)(2,1)S(1)}, bf16[16,2048]{1,0:T(8,128)(2,1)S(1)}, u32[]{:S(2)}, u32[]{:S(2)}) collective-permute-start(bf16[16,2048]{1,0:T(8,128)(2,1)S(1)} %get-tuple-element.366), channel_id=1, source_target_pairs={{0,2},{1,3},{2,0},{3,1},{4,6},{5,7},{6,4},{7,5},{8,10},{9,11},{10,... | collective-permute-start | bytes 196616 | tf_op jit(solution)/shard_map/ppermute | solution.py:28
  1253.8 21.4 %collective-permute-start.73 = (bf16[16,2048]{1,0:T(8,128)(2,1)S(1)}, bf16[16,2048]{1,0:T(8,128)(2,1)S(1)}, u32[]{:S(2)}, u32[]{:S(2)}) collective-permute-start(bf16[16,2048]{1,0:T(8,128)(2,1)S(1)} %get-tuple-element.367), channel_id=1, source_target_pairs={{0,1},{1,0},{2,3},{3,2},{4,5},{5,4},{6,7},{7,6},{8,9},{9,8},{10,11... | collective-permute-start | bytes 196616 | tf_op jit(solution)/shard_map/ppermute | solution.py:28
  1254.0 45.2 %collective-permute-start.66 = (bf16[2,48,2048]{2,1,0:T(8,128)(2,1)S(1)}, bf16[2,48,2048]{2,1,0:T(8,128)(2,1)S(1)}, u32[]{:S(2)}, u32[]{:S(2)}) collective-permute-start(bf16[2,48,2048]{2,1,0:T(8,128)(2,1)S(1)} %pad_maximum_fusion.60), channel_id=1, source_target_pairs={{0,1},{1,0},{2,3},{3,2},{4,5},{5,4},{6,7},{7,6},{8,9},{9,8},{10,11... | collective-permute-start | bytes 1179656 | tf_op jit(solution)/shard_map/ppermute | solution.py:28
  1274.7 24.6 %collective-permute-start.68 = (bf16[2,48,2048]{2,1,0:T(8,128)(2,1)S(1)}, bf16[2,48,2048]{2,1,0:T(8,128)(2,1)S(1)}, u32[]{:S(2)}, u32[]{:S(2)}) collective-permute-start(bf16[2,48,2048]{2,1,0:T(8,128)(2,1)S(1)} %slice.1359), channel_id=1, source_target_pairs={{0,2},{1,3},{2,0},{3,1},{4,6},{5,7},{6,4},{7,5},{8,10},{9,11},{10,... | collective-permute-start | bytes 1179656 | tf_op jit(solution)/shard_map/ppermute | solution.py:28
  1275.3 22.8 %collective-permute-start.63 = (f32[23184]{0:T(1024)S(1)}, f32[23184]{0:T(1024)S(1)}, u32[]{:S(2)}, u32[]{:S(2)}) collective-permute-start(f32[23184]{0:T(1024)S(1)} %add.558), channel_id=1, source_target_pairs={{0,16},{4,20},{8,24},{12,28},{16,0},{20,4},{24,8},{28,12},{1,17},{... | collective-permute-start | bytes 278216 | tf_op jit(solution)/shard_map/ppermute | solution.py:28
  1310.5 23.7 %collective-permute-start.51 = (bf16[256,1792]{1,0:T(8,128)(2,1)}, bf16[256,1792]{1,0:T(8,128)(2,1)}, u32[]{:S(2)}, u32[]{:S(2)}) collective-permute-start(bf16[256,1792]{1,0:T(8,128)(2,1)} %get-tuple-element.173), channel_id=1, source_target_pairs={{0,2},{1,3},{2,0},{3,1},{4,6},{5,7},{6,4},{7,5},{8,10},{9,11},{10,... | collective-permute-start | bytes 2752520 | tf_op jit(solution)/shard_map/ppermute | solution.py:28
  1311.4 22.8 %collective-permute-start.53 = (bf16[256,1792]{1,0:T(8,128)(2,1)}, bf16[256,1792]{1,0:T(8,128)(2,1)}, u32[]{:S(2)}, u32[]{:S(2)}) collective-permute-start(bf16[256,1792]{1,0:T(8,128)(2,1)} %get-tuple-element.174), channel_id=1, source_target_pairs={{0,1},{1,0},{2,3},{3,2},{4,5},{5,4},{6,7},{7,6},{8,9},{9,8},{10,11... | collective-permute-start | bytes 2752520 | tf_op jit(solution)/shard_map/ppermute | solution.py:28
  1312.7 19.7 %collective-permute-start.67 = (bf16[48,2048]{1,0:T(8,128)(2,1)}, bf16[48,2048]{1,0:T(8,128)(2,1)S(1)}, u32[]{:S(2)}, u32[]{:S(2)}) collective-permute-start(bf16[48,2048]{1,0:T(8,128)(2,1)} %get-tuple-element.271), channel_id=1, source_target_pairs={{0,2},{1,3},{2,0},{3,1},{4,6},{5,7},{6,4},{7,5},{8,10},{9,11},{10,... | collective-permute-start | bytes 589832 | tf_op jit(solution)/shard_map/ppermute | solution.py:28
  1314.7 18.4 %collective-permute-start.69 = (bf16[48,2048]{1,0:T(8,128)(2,1)}, bf16[48,2048]{1,0:T(8,128)(2,1)}, u32[]{:S(2)}, u32[]{:S(2)}) collective-permute-start(bf16[48,2048]{1,0:T(8,128)(2,1)} %get-tuple-element.272), channel_id=1, source_target_pairs={{0,1},{1,0},{2,3},{3,2},{4,5},{5,4},{6,7},{7,6},{8,9},{9,8},{10,11... | collective-permute-start | bytes 589832 | tf_op jit(solution)/shard_map/ppermute | solution.py:28
  1341.2 18.6 %collective-permute-start.55 = (bf16[64,1792]{1,0:T(8,128)(2,1)S(1)}, bf16[64,1792]{1,0:T(8,128)(2,1)S(1)}, u32[]{:S(2)}, u32[]{:S(2)}) collective-permute-start(bf16[64,1792]{1,0:T(8,128)(2,1)S(1)} %get-tuple-element.234), channel_id=1, source_target_pairs={{0,8},{4,12},{8,0},{12,4},{16,24},{20,28},{24,16},{28,20},{1,9},{5... | collective-permute-start | bytes 688136 | tf_op jit(solution)/shard_map/ppermute | solution.py:28
  1345.2 19.1 %collective-permute-start.56 = (bf16[64,1792]{1,0:T(8,128)(2,1)S(1)}, bf16[64,1792]{1,0:T(8,128)(2,1)S(1)}, u32[]{:S(2)}, u32[]{:S(2)}) collective-permute-start(bf16[64,1792]{1,0:T(8,128)(2,1)S(1)} %get-tuple-element.233), channel_id=1, source_target_pairs={{0,12},{4,8},{8,4},{12,0},{16,28},{20,24},{24,20},{28,16},{1,13},{... | collective-permute-start | bytes 688136 | tf_op jit(solution)/shard_map/ppermute | solution.py:28
  1345.3 19.0 %collective-permute-start.57 = (bf16[64,1792]{1,0:T(8,128)(2,1)S(1)}, bf16[64,1792]{1,0:T(8,128)(2,1)S(1)}, u32[]{:S(2)}, u32[]{:S(2)}) collective-permute-start(bf16[64,1792]{1,0:T(8,128)(2,1)S(1)} %get-tuple-element.232), channel_id=1, source_target_pairs={{0,16},{4,20},{8,24},{12,28},{16,0},{20,4},{24,8},{28,12},{1,17},{... | collective-permute-start | bytes 688136 | tf_op jit(solution)/shard_map/ppermute | solution.py:28
  1346.5 31.1 %collective-permute-start.58 = (bf16[64,1792]{1,0:T(8,128)(2,1)S(1)}, bf16[64,1792]{1,0:T(8,128)(2,1)S(1)}, u32[]{:S(2)}, u32[]{:S(2)}) collective-permute-start(bf16[64,1792]{1,0:T(8,128)(2,1)S(1)} %get-tuple-element.231), channel_id=1, source_target_pairs={{0,20},{4,16},{8,28},{12,24},{16,4},{20,0},{24,12},{28,8},{1,21},{... | collective-permute-start | bytes 688136 | tf_op jit(solution)/shard_map/ppermute | solution.py:28
  1347.6 29.9 %collective-permute-start.59 = (bf16[64,1792]{1,0:T(8,128)(2,1)S(1)}, bf16[64,1792]{1,0:T(8,128)(2,1)S(1)}, u32[]{:S(2)}, u32[]{:S(2)}) collective-permute-start(bf16[64,1792]{1,0:T(8,128)(2,1)S(1)} %get-tuple-element.230), channel_id=1, source_target_pairs={{0,24},{4,28},{8,16},{12,20},{16,8},{20,12},{24,0},{28,4},{1,25},{... | collective-permute-start | bytes 688136 | tf_op jit(solution)/shard_map/ppermute | solution.py:28
  1359.8 17.8 %collective-permute-start.60 = (bf16[64,1792]{1,0:T(8,128)(2,1)S(1)}, bf16[64,1792]{1,0:T(8,128)(2,1)S(1)}, u32[]{:S(2)}, u32[]{:S(2)}) collective-permute-start(bf16[64,1792]{1,0:T(8,128)(2,1)S(1)} %get-tuple-element.229), channel_id=1, source_target_pairs={{0,28},{4,24},{8,20},{12,16},{16,12},{20,8},{24,4},{28,0},{1,29},{... | collective-permute-start | bytes 688136 | tf_op jit(solution)/shard_map/ppermute | solution.py:28
  (278 other events, 4597.6 us)
Sparse Core Ops, SparseCore 0:
  66.7 119.9 all-gather.4
  387.1 87.0 reduce-scatter.4
  479.1 102.9 all-gather.6
  583.5 82.0 all-gather.8
  692.7 88.1 reduce-scatter.8
  794.0 80.3 all-gather.10
  1043.0 89.3 reduce-scatter.10
  1134.8 93.6 reduce-scatter.6

commit v2 on v1

v2 whole, which is shorter than its diff:
```python
import jax
import jax.numpy as jnp
from jax import lax
from jax.experimental import pallas as pl
from jax.experimental.pallas import tpu as pltpu
from jax.sharding import PartitionSpec as P

D = 2048
FF = 4096
HEADS = 48
HEAD_DIM = 64
STATE = 256
ATT_HEADS = 8
KV_HEADS = 2
ATT_DIM = 128
INNER = HEADS * HEAD_DIM
CONV = 4
PROJ = 2 * INNER + 2 * STATE + HEADS
DT_PAD = 128

epsilon = 1e-05
rope_base = 10000.0
f32 = jnp.float32
bf16 = jnp.bfloat16


def after(value, *others):
    def nothing(*refs):
        pass

    return pl.pallas_call(
        nothing,
        out_shape=jax.ShapeDtypeStruct(value.shape, value.dtype),
        in_specs=[pl.BlockSpec(memory_space=pl.ANY)] * (1 + len(others)),
        out_specs=pl.BlockSpec(memory_space=pl.ANY),
        input_output_aliases={0: 0},
    )(value, *others)


def permuted(value, axis, by):
    pairs = [(i, i ^ by) for i in range(lax.axis_size(axis))]
    return lax.ppermute(value, axis, pairs)


def small_gather(value):
    rows = value[None]
    for axis in ("dp", "seq"):
        here = lax.axis_index(axis)
        by = 1
        while by < lax.axis_size(axis):
            other = permuted(rows, axis, by)
            upper = (here & by) != 0
            rows = jnp.where(
                upper, jnp.concatenate([other, rows]), jnp.concatenate([rows, other])
            )
            by *= 2
    return rows


def summed(value, axes):
    for axis in axes:
        by = 1
        while by < lax.axis_size(axis):
            value = value + permuted(value, axis, by)
            by *= 2
    return value


def exchanged(blocks, axis):
    return lax.all_to_all(blocks, axis, 0, 0, tiled=True)


def assembled(shape, kind, moves, *inputs):
    def kernel(*refs):
        out = refs[-1]
        for which, source, target in moves:
            out[target] = refs[which][source].astype(out.dtype)

    return pl.pallas_call(
        kernel,
        out_shape=jax.ShapeDtypeStruct(shape, kind),
        compiler_params=pltpu.CompilerParams(vmem_limit_bytes=40 * 1024 * 1024),
        cost_estimate=about(4),
    )(*inputs)


def about(microseconds):
    return pl.CostEstimate(
        flops=0, bytes_accessed=int(microseconds * 3.6e6), transcendentals=0
    )


def regrouped(value, outer, inner, width):
    rows, total = value.shape
    if width != 64 or outer % 2:
        split = value.reshape(rows, outer, inner, width)
        return jnp.swapaxes(split, 1, 2).reshape(rows, total)

    def kernel(in_ref, out_ref):
        for i in range(inner):
            for o in range(0, outer, 2):
                left = in_ref[:, (o * inner + i) * width : (o * inner + i + 1) * width]
                right = in_ref[:, ((o + 1) * inner + i) * width : ((o + 1) * inner + i + 1) * width]
                at = (i * outer + o) * width
                out_ref[:, at : at + 2 * width] = jnp.concatenate([left, right], axis=1)

    return pl.pallas_call(
        kernel,
        out_shape=jax.ShapeDtypeStruct(value.shape, value.dtype),
        compiler_params=pltpu.CompilerParams(vmem_limit_bytes=40 * 1024 * 1024),
        cost_estimate=about(2),
    )(value)


def dp_gather(value, forward=True):
    if lax.axis_size("dp") != 4:
        return lax.all_gather(value, "dp", axis=0)
    here = lax.axis_index("dp")
    half = value.shape[0] // 2
    one = permuted(value, "dp", 1)
    two = permuted(value, "dp", 2)
    if forward:
        three = jnp.concatenate([permuted(one[:half], "dp", 2), permuted(two[half:], "dp", 1)])
    else:
        three = permuted(value, "dp", 3)
    whole = jnp.zeros((4,) + value.shape, value.dtype)
    for k, piece in enumerate((value, one, two, three)):
        whole = lax.dynamic_update_index_in_dim(whole, piece, here ^ k, 0)
    return whole


def placed_pieces(pieces, here, cuts):
    count, (rows, width) = len(pieces), pieces[0].shape
    spans = list(zip(cuts[:-1], cuts[1:]))

    def kernel(here_ref, *refs):
        for k in range(count):
            owner = here_ref[0] ^ k
            for (low, high), out in zip(spans, refs[count:]):
                out[pl.ds(pl.multiple_of(owner * (high - low), 16), high - low)] = refs[k][low:high]

    return pl.pallas_call(
        kernel,
        out_shape=[
            jax.ShapeDtypeStruct((count * (high - low), width), pieces[0].dtype)
            for low, high in spans
        ],
        in_specs=[pl.BlockSpec(memory_space=pltpu.SMEM)]
        + [pl.BlockSpec(memory_space=pltpu.VMEM)] * count,
        out_specs=[pl.BlockSpec(memory_space=pltpu.VMEM)] * len(spans),
        compiler_params=pltpu.CompilerParams(vmem_limit_bytes=40 * 1024 * 1024),
        cost_estimate=about(2),
    )(here[None], *pieces)


def dp_scatter(total, forward=True, meanwhile=()):
    if lax.axis_size("dp") != 4:
        return lax.psum_scatter(total, "dp", scatter_dimension=0).astype(f32)
    here = lax.axis_index("dp")
    blocks = [lax.dynamic_index_in_dim(total, here ^ k, 0, False) for k in range(4)]
    if not forward:
        own = blocks[0].astype(f32)
        for k in range(1, 4):
            own = own + permuted(blocks[k], "dp", k).astype(f32)
        return own
    half = total.shape[1] // 2
    low, high = [b[:half] for b in blocks], [b[half:] for b in blocks]
    low_in = permuted(jnp.stack([low[1], low[3]]), "dp", 1)
    high_in = permuted(jnp.stack(high[2:]), "dp", 2)
    if meanwhile:
        low_in, high_in = after(low_in, *meanwhile), after(high_in, *meanwhile)
    low_in, high_in = low_in.astype(f32), high_in.astype(f32)
    low_on = (low[2].astype(f32) + low_in[1]).astype(bf16)
    high_on = (high[1].astype(f32) + high_in[1]).astype(bf16)
    low_own = low[0].astype(f32) + low_in[0] + permuted(low_on, "dp", 2).astype(f32)
    high_own = high[0].astype(f32) + high_in[0] + permuted(high_on, "dp", 1).astype(f32)
    return jnp.concatenate([low_own, high_own])


def row_sums(value):
    return other_pairs(value + permuted(value, "seq", 1))


def other_pairs(value):
    total = value
    for by in range(2, lax.axis_size("seq"), 2):
        total = total + permuted(value, "seq", by)
    return total


def segment_of(positions, end_points):
    counted = jnp.sum((end_points[None, :] <= positions[:, None]).astype(jnp.int32), axis=1)
    return jnp.where(positions < 0, -1, counted)


def rope_tables(positions):
    half = ATT_DIM // 2
    freqs = jnp.power(rope_base, -jnp.arange(half, dtype=f32) * (2.0 / ATT_DIM))
    angles = positions.astype(f32)[:, None] * freqs[None, :]
    cosine, sine = jnp.cos(angles), jnp.sin(angles)
    return jnp.concatenate([cosine, cosine], axis=1), jnp.concatenate([sine, sine], axis=1)


def rms_row(values):
    return lax.rsqrt(jnp.mean(values * values, axis=-1, keepdims=True) + epsilon)


def rms_back(grad, values, gain):
    r = rms_row(values)
    scaled = grad * gain
    along = jnp.mean(scaled * values, axis=-1, keepdims=True)
    return scaled * r - values * (r * r * r) * along, jnp.sum(grad * values * r, axis=0)


def dot(left, right):
    return jnp.dot(left, right, preferred_element_type=f32)


def dot_t(left, right):
    return lax.dot_general(left, right, (((1,), (1,)), ((), ())), preferred_element_type=f32)


def cross(left, right):
    return lax.dot_general(left, right, (((0,), (0,)), ((), ())), preferred_element_type=f32)


def halves(columns, pair, lanes):
    left, right = columns[:, 2 * pair : 2 * pair + 1], columns[:, 2 * pair + 1 : 2 * pair + 2]
    return jnp.where(lanes < HEAD_DIM, left, right)


def spread(columns, pairs, lanes):
    return jnp.concatenate([halves(columns, k, lanes) for k in range(pairs)], axis=1)


def counted(pattern, value, dims=(((1,), (0,)), ((), ())), terms=2, first=True):
    pattern = pattern.astype(bf16)
    total, rest = None, value
    for k in range(terms):
        term = rest.astype(bf16)
        pair = (pattern, term) if first else (term, pattern)
        part = lax.dot_general(*pair, dims, preferred_element_type=f32)
        total = part if total is None else total + part
        if k + 1 < terms:
            rest = rest - term.astype(f32)
    return total


def rough(left, right, dims=(((1,), (0,)), ((), ()))):
    return lax.dot_general(
        left.astype(bf16), right.astype(bf16), dims, preferred_element_type=f32
    )


ROWS = (((0,), (0,)), ((), ()))
LAST = (((1,), (1,)), ((), ()))


def block_start(mixed_ref, before_ref, aux_ref, conv_ref, head_ref, ext_ref, width):
    per = mixed_ref.shape[0]
    channels = width + 2 * STATE
    ext_ref[0:8] = before_ref[:, width : width + channels].astype(bf16).astype(f32)
    ext_ref[8 : 8 + per] = mixed_ref[:, width : width + channels].astype(bf16).astype(f32)
    aux = aux_ref[...]
    total = conv_ref[4:5] + ext_ref[8 : 8 + per] * conv_ref[3:4]
    for back in range(1, CONV):
        total = total + ext_ref[8 - back : 8 - back + per] * (
            aux[:, back : back + 1] * conv_ref[3 - back : 4 - back]
        )
    sig = jax.nn.sigmoid(total)
    shifted = mixed_ref[:, width + channels : width + channels + DT_PAD] + head_ref[1:2]
    step = jnp.maximum(shifted, 0.0) + jnp.log1p(jnp.exp(-jnp.abs(shifted)))
    rate = -jnp.exp(head_ref[0:1])
    rows_at = lax.broadcasted_iota(jnp.int32, (per, per), 0)
    cols_at = lax.broadcasted_iota(jnp.int32, (per, per), 1)
    tril = (rows_at >= cols_at).astype(f32)
    cum = counted(tril, step * rate, terms=3)
    return aux, total, sig, shifted, step, rate, tril, cum


def ssd_forward_kernel(
    mixed_ref,
    before_ref,
    aux_ref,
    seg_ref,
    conv_ref,
    head_ref,
    skip_ref,
    y_ref,
    gated_ref,
    enter_ref,
    ext_ref,
    state_ref,
):
    per, width = y_ref.shape
    pairs = width // 128

    @pl.when(pl.program_id(1) == 0)
    def _():
        state_ref[...] = jnp.zeros_like(state_ref)

    aux, total, sig, _, step, _, tril, cum = block_start(
        mixed_ref, before_ref, aux_ref, conv_ref, head_ref, ext_ref, width
    )
    conv = total * sig
    x = conv[:, :width]
    b = conv[:, width : width + STATE].astype(bf16)
    c = conv[:, width + STATE :].astype(bf16)
    lanes = lax.broadcasted_iota(jnp.int32, (per, 128), 1)
    mask = (tril > 0) & (aux[:, 0:1] == seg_ref[0])
    both = rough(c, b, LAST)
    cum_t, step_t = cum.T, step.T
    state = state_ref[...]
    enter_ref[0] = state.astype(bf16)
    carried = rough(c, state)
    grown = jnp.exp(cum) * aux[:, 4:5]
    last = cum[per - 1 : per]
    keep = jnp.exp(last - cum) * aux[:, 5:6] * step
    gate = mixed_ref[:, :width]
    silu_gate = gate * jax.nn.sigmoid(gate)
    scaled = []
    for k in range(pairs):
        at = slice(128 * k, 128 * k + 128)
        x_pair = x[:, at]
        x_low = x_pair.astype(bf16)
        sides = []
        for h in (2 * k, 2 * k + 1):
            gap = jnp.where(mask, cum[:, h : h + 1] - cum_t[h : h + 1], -1e30)
            mixing = both * jnp.exp(gap) * step_t[h : h + 1]
            sides.append(rough(mixing, x_low))
        y = jnp.where(lanes < HEAD_DIM, sides[0], sides[1])
        y = y + carried[:, at] * halves(grown, k, lanes) + skip_ref[:, at] * x_pair
        y_ref[:, at] = y
        gated_ref[:, at] = y * silu_gate[:, at]
        scaled.append(x_pair * halves(keep, k, lanes))
    passed = spread(jnp.exp(last) * aux[0:1, 6:7], pairs, lanes[0:1])
    state_ref[...] = state * passed + rough(b, jnp.concatenate(scaled, axis=1), ROWS)


def ssd_backward_kernel(
    mixed_ref,
    before_ref,
    aux_ref,
    seg_ref,
    conv_ref,
    head_ref,
    skip_ref,
    y_ref,
    enter_ref,
    grad_ref,
    qkv_ref,
    out_ref,
    conv_grad_ref,
    head_grad_ref,
    skip_grad_ref,
    ext_ref,
    next_ref,
    col_ref,
    state_ref,
):
    per, width = y_ref.shape
    pairs = width // 128
    channels = width + 2 * STATE

    @pl.when(pl.program_id(1) == 0)
    def _():
        state_ref[...] = jnp.zeros_like(state_ref)
        next_ref[...] = jnp.zeros_like(next_ref)

    @pl.when((pl.program_id(0) == 0) & (pl.program_id(1) == 0))
    def _():
        conv_grad_ref[...] = jnp.zeros_like(conv_grad_ref)
        head_grad_ref[...] = jnp.zeros_like(head_grad_ref)
        skip_grad_ref[...] = jnp.zeros_like(skip_grad_ref)
        col_ref[...] = jnp.zeros_like(col_ref)

    aux, total, sig, shifted, step, rate, tril, cum = block_start(
        mixed_ref, before_ref, aux_ref, conv_ref, head_ref, ext_ref, width
    )
    conv = total * sig
    x = conv[:, :width]
    b = conv[:, width : width + STATE].astype(bf16)
    c = conv[:, width + STATE :].astype(bf16)
    lanes = lax.broadcasted_iota(jnp.int32, (per, 128), 1)
    mask = (tril > 0) & (aux[:, 0:1] == seg_ref[0])
    both = rough(c, b, LAST)
    cum_t, step_t = cum.T, step.T
    enter = enter_ref[0]
    growth = jnp.exp(cum) * aux[:, 4:5]
    last = cum[per - 1 : per]
    fade = jnp.exp(last - cum) * aux[:, 5:6]
    keep = fade * step
    passed_row = jnp.exp(last) * aux[0:1, 6:7]

    gate = mixed_ref[:, :width]
    gate_sig = jax.nn.sigmoid(gate)
    grad = grad_ref[...]
    dy = grad * gate * gate_sig
    out_ref[:, :width] = (
        grad * y_ref[...] * (gate_sig * (1.0 + gate * (1.0 - gate_sig)))
    ).astype(bf16)

    d_out = state_ref[...]
    wide_growth = spread(growth, pairs, lanes)
    wide_keep = spread(keep, pairs, lanes)
    carried = rough(c, enter)
    dq = dy * wide_growth
    d_c = rough(dq, enter, LAST)
    xk = x * wide_keep
    d_b = rough(xk, d_out, LAST)
    dxk = rough(b, d_out)
    of_head = (
        lax.broadcasted_iota(jnp.int32, (width, 128), 0) // HEAD_DIM
        == lax.broadcasted_iota(jnp.int32, (width, 128), 1)
    ).astype(f32)
    d_growth = counted(of_head, dq * carried, first=False)
    d_keep = counted(of_head, dxk * x, first=False)
    d_passed = jnp.sum(d_out * enter.astype(f32), axis=0, keepdims=True)
    d_passed = counted(of_head, jnp.broadcast_to(d_passed, (16, width)), first=False)[0:1]
    d_x = dxk * wide_keep + dy * skip_ref[...]
    skip_grad_ref[0:1] += jnp.sum(dy * x, axis=0, keepdims=True)
    state_ref[...] = d_out * spread(passed_row, pairs, lanes[0:1]) + rough(c, dq, ROWS)

    d_both = jnp.zeros((per, per), f32)
    row_sums = jnp.zeros((per, 128), f32)
    within = []
    for k in range(pairs):
        at = slice(128 * k, 128 * k + 128)
        x_low = x[:, at].astype(bf16)
        dy_pair = dy[:, at]
        dy_low = dy_pair.astype(bf16)
        sides = []
        for h in (2 * k, 2 * k + 1):
            mine = (lanes >= HEAD_DIM) if h % 2 else (lanes < HEAD_DIM)
            gap = jnp.where(mask, cum[:, h : h + 1] - cum_t[h : h + 1], -1e30)
            level = jnp.exp(gap)
            step_row = step_t[h : h + 1]
            weighted = level * step_row
            sides.append(rough(both * weighted, dy_low, ROWS))
            d_mix = rough(jnp.where(mine, dy_pair, 0.0), x_low, LAST)
            d_both = d_both + d_mix * weighted
            flow = d_mix * both * level
            col_ref[h : h + 1] = jnp.sum(flow, axis=0, keepdims=True)
            row_sum = jnp.sum(flow * step_row, axis=1, keepdims=True)
            row_sums = jnp.where(lanes == h, row_sum, row_sums)
        within.append(jnp.where(lanes < HEAD_DIM, sides[0], sides[1]))
    d_x = d_x + jnp.concatenate(within, axis=1)
    d_c = d_c + rough(d_both, b)
    d_b = d_b + rough(d_both, c, ROWS)
    col_sums = col_ref[...].T
    d_step = col_sums + d_keep * fade
    kept = d_keep * keep
    d_cum = row_sums - col_sums * step + d_growth - kept
    d_last = jnp.sum(kept, axis=0, keepdims=True) + d_passed * passed_row
    at_end = lax.broadcasted_iota(jnp.int32, (per, 128), 0) == per - 1
    d_cum = d_cum + jnp.where(at_end, d_last, 0.0)
    d_decay = counted(tril, d_cum, ROWS)
    d_step = d_step + d_decay * rate
    d_shifted = d_step * jax.nn.sigmoid(shifted)
    head_grad_ref[0:1] += jnp.sum(d_decay * step, axis=0, keepdims=True) * rate
    head_grad_ref[1:2] += jnp.sum(d_shifted, axis=0, keepdims=True)
    out_ref[:, width + channels : width + channels + DT_PAD] = d_shifted.astype(bf16)
    out_ref[:, width + channels + DT_PAD :] = qkv_ref[...]

    d_conv = jnp.concatenate([d_x, d_b, d_c], axis=1)
    d_total = d_conv * (sig * (1.0 + total * (1.0 - sig)))
    conv_grad_ref[4:5] += jnp.sum(d_total, axis=0, keepdims=True)
    conv_grad_ref[3:4] += jnp.sum(d_total * ext_ref[8 : 8 + per], axis=0, keepdims=True)
    for back in range(1, CONV):
        conv_grad_ref[3 - back : 4 - back] += jnp.sum(
            d_total * aux[:, back : back + 1] * ext_ref[8 - back : 8 - back + per],
            axis=0,
            keepdims=True,
        )
    d_in = d_total * conv_ref[3:4]
    for back in range(1, CONV):
        masked = d_total * aux[:, back : back + 1]
        ext_ref[0:per] = masked
        ext_ref[per : per + 8] = next_ref[back - 1]
        d_in = d_in + ext_ref[back : back + per] * conv_ref[3 - back : 4 - back]
        next_ref[back - 1] = masked[0:8]
    out_ref[:, width : width + channels] = d_in.astype(bf16)


def ssd_specs(n, micro, per, width, used, order):
    eighths = per // 8
    return [
        pl.BlockSpec((per, used), lambda m, k: (order(k) * micro + m, 0)),
        pl.BlockSpec(
            (8, used),
            lambda m, k: (
                (jnp.maximum(order(k) - 1, 0) * micro + m) * eighths + eighths - 1,
                0,
            ),
        ),
        pl.BlockSpec((per, 8), lambda m, k: (order(k) * micro + m, 0)),
        pl.BlockSpec((1, 1, per), lambda m, k: (order(k) * micro + m, 0, 0)),
        pl.BlockSpec((8, width + 2 * STATE), lambda m, k: (0, 0)),
        pl.BlockSpec((8, DT_PAD), lambda m, k: (0, 0)),
        pl.BlockSpec((1, width), lambda m, k: (0, 0)),
    ]


def ssd_forward(mixed, aux, seg_rows, conv_rows, head_rows, skip_row, n, micro):
    rows = mixed.shape[0]
    per = rows // (n * micro)
    width = skip_row.shape[1]
    channels = width + 2 * STATE
    used = width + channels + DT_PAD
    specs = ssd_specs(n, micro, per, width, used, lambda k: k)
    by_block = pl.BlockSpec((per, width), lambda m, k: (k * micro + m, 0))
    return pl.pallas_call(
        ssd_forward_kernel,
        grid=(micro, n),
        out_shape=(
            jax.ShapeDtypeStruct((rows, width), f32),
            jax.ShapeDtypeStruct((rows, width), f32),
            jax.ShapeDtypeStruct((n * micro, STATE, width), bf16),
        ),
        in_specs=specs,
        out_specs=(
            by_block,
            by_block,
            pl.BlockSpec((1, STATE, width), lambda m, k: (k * micro + m, 0, 0)),
        ),
        scratch_shapes=[
            pltpu.VMEM((per + 8, channels), f32),
            pltpu.VMEM((STATE, width), f32),
        ],
        compiler_params=pltpu.CompilerParams(vmem_limit_bytes=40 * 1024 * 1024),
        cost_estimate=about(20),
    )(mixed, mixed, aux, seg_rows, conv_rows, head_rows, skip_row)


def ssd_backward(
    mixed, aux, seg_rows, conv_rows, head_rows, skip_row, y, enter, grad, qkv, n, micro
):
    rows = mixed.shape[0]
    per = rows // (n * micro)
    width = skip_row.shape[1]
    channels = width + 2 * STATE
    used = width + channels + DT_PAD

    def order(k):
        return n - 1 - k

    specs = ssd_specs(n, micro, per, width, used, order)
    by_block = pl.BlockSpec((per, width), lambda m, k: (order(k) * micro + m, 0))
    return pl.pallas_call(
        ssd_backward_kernel,
        grid=(micro, n),
        out_shape=(
            jax.ShapeDtypeStruct(mixed.shape, bf16),
            jax.ShapeDtypeStruct((8, channels), f32),
            jax.ShapeDtypeStruct((8, DT_PAD), f32),
            jax.ShapeDtypeStruct((8, width), f32),
        ),
        in_specs=specs
        + [
            by_block,
            pl.BlockSpec((1, STATE, width), lambda m, k: (order(k) * micro + m, 0, 0)),
            by_block,
            pl.BlockSpec((per, qkv.shape[1]), lambda m, k: (order(k) * micro + m, 0)),
        ],
        out_specs=(
            pl.BlockSpec((per, mixed.shape[1]), lambda m, k: (order(k) * micro + m, 0)),
            pl.BlockSpec((8, channels), lambda m, k: (0, 0)),
            pl.BlockSpec((8, DT_PAD), lambda m, k: (0, 0)),
            pl.BlockSpec((8, width), lambda m, k: (0, 0)),
        ),
        scratch_shapes=[
            pltpu.VMEM((per + 8, channels), f32),
            pltpu.VMEM((CONV - 1, 8, channels), f32),
            pltpu.VMEM((128, per), f32),
            pltpu.VMEM((STATE, width), f32),
        ],
        compiler_params=pltpu.CompilerParams(vmem_limit_bytes=40 * 1024 * 1024),
        cost_estimate=about(43),
    )(mixed, mixed, aux, seg_rows, conv_rows, head_rows, skip_row, y, enter, grad, qkv)


def turn(values, cosine, sine):
    half = ATT_DIM // 2
    swapped = jnp.concatenate([-values[:, half:], values[:, :half]], axis=1)
    return values * cosine + swapped * sine


def attention_start(k_ref, v_ref, table_ref, keys_ref, values_ref):
    blocks, per, _ = k_ref.shape
    for b in range(blocks):
        at = slice(b * per, b * per + per)
        keys_ref[at] = turn(k_ref[b], table_ref[b, :, :ATT_DIM], table_ref[b, :, ATT_DIM:]).astype(
            bf16
        )
        values_ref[at] = v_ref[b].astype(bf16)


def attention_probs(q_ref, q_table_ref, q_aux_ref, seg_ref, keys_ref):
    scale = ATT_DIM ** (-0.5)
    table = q_table_ref[0]
    queries = turn(q_ref[0], table[:, :ATT_DIM], table[:, ATT_DIM:]).astype(bf16)
    scores = rough(queries, keys_ref[...], LAST) * scale
    q_aux = q_aux_ref[0]
    positions = lax.broadcasted_iota(jnp.int32, scores.shape, 1)
    seen = (positions <= q_aux[:, 1:2].astype(jnp.int32)) & (q_aux[:, 0:1] == seg_ref[0])
    scores = jnp.where(seen, scores, -1e30)
    raised = jnp.exp(scores - jnp.max(scores, axis=1, keepdims=True))
    return queries, raised / jnp.sum(raised, axis=1, keepdims=True)


def attention_forward_kernel(
    q_ref, k_ref, v_ref, table_ref, q_table_ref, q_aux_ref, seg_ref, out_ref, keys_ref, values_ref
):
    @pl.when(pl.program_id(1) == 0)
    def _():
        attention_start(k_ref, v_ref, table_ref, keys_ref, values_ref)

    _, probs = attention_probs(q_ref, q_table_ref, q_aux_ref, seg_ref, keys_ref)
    out_ref[0] = rough(probs, values_ref[...]).astype(bf16)


def attention_backward_kernel(
    q_ref,
    k_ref,
    v_ref,
    table_ref,
    q_table_ref,
    q_aux_ref,
    seg_ref,
    grad_ref,
    q_grad_ref,
    k_grad_ref,
    v_grad_ref,
    keys_ref,
    values_ref,
    k_sum_ref,
    v_sum_ref,
):
    blocks, per, _ = k_ref.shape

    @pl.when(pl.program_id(1) == 0)
    def _():
        attention_start(k_ref, v_ref, table_ref, keys_ref, values_ref)
        k_sum_ref[...] = jnp.zeros_like(k_sum_ref)
        v_sum_ref[...] = jnp.zeros_like(v_sum_ref)

    scale = ATT_DIM ** (-0.5)
    queries, probs = attention_probs(q_ref, q_table_ref, q_aux_ref, seg_ref, keys_ref)
    grad = grad_ref[0]
    probs_grad = rough(grad, values_ref[...], LAST)
    along = jnp.sum(probs * probs_grad, axis=1, keepdims=True)
    scores_grad = (probs * (probs_grad - along)).astype(bf16)
    table = q_table_ref[0]
    q_grad = rough(scores_grad, keys_ref[...]) * scale
    q_grad_ref[0] = turn(q_grad, table[:, :ATT_DIM], -table[:, ATT_DIM:]).astype(bf16)
    k_sum_ref[...] += rough(scores_grad, queries, ROWS)
    v_sum_ref[...] += rough(probs, grad, ROWS)

    @pl.when(pl.program_id(1) == pl.num_programs(1) - 1)
    def _():
        for b in range(blocks):
            at = slice(b * per, b * per + per)
            k_grad_ref[b] = turn(
                k_sum_ref[at] * scale, table_ref[b, :, :ATT_DIM], -table_ref[b, :, ATT_DIM:]
            ).astype(bf16)
            v_grad_ref[b] = v_sum_ref[at].astype(bf16)


def attention_specs(n, micro, per, q_at, k_at, v_at):
    return [
        pl.BlockSpec((1, per, ATT_DIM), lambda m, k: (k, m, q_at)),
        pl.BlockSpec((n, per, ATT_DIM), lambda m, k: (0, m, k_at)),
        pl.BlockSpec((n, per, ATT_DIM), lambda m, k: (0, m, v_at)),
        pl.BlockSpec((n, per, 2 * ATT_DIM), lambda m, k: (0, 0, 0)),
        pl.BlockSpec((1, per, 2 * ATT_DIM), lambda m, k: (k, 0, 0)),
        pl.BlockSpec((1, per, 8), lambda m, k: (k, m, 0)),
        pl.BlockSpec((1, 1, n * per), lambda m, k: (m, 0, 0)),
    ]


def attention_forward(q, mixed, table, q_table, q_aux, seg, q_at, k_at):
    n, both, _ = mixed.shape
    micro = seg.shape[0]
    per = both // micro
    block = pl.BlockSpec((1, per, ATT_DIM), lambda m, k: (k, m, 0))
    return pl.pallas_call(
        attention_forward_kernel,
        grid=(micro, q_table.shape[0]),
        out_shape=jax.ShapeDtypeStruct((q_table.shape[0], both, ATT_DIM), bf16),
        in_specs=attention_specs(n, micro, per, q_at, k_at, k_at + 1),
        out_specs=block,
        scratch_shapes=[pltpu.VMEM((n * per, ATT_DIM), bf16)] * 2,
        compiler_params=pltpu.CompilerParams(vmem_limit_bytes=40 * 1024 * 1024),
        cost_estimate=about(14),
    )(q, mixed, mixed, table, q_table, q_aux, seg)


def attention_backward(q, mixed, table, q_table, q_aux, seg, grad, q_at, k_at):
    n, both, _ = mixed.shape
    micro = seg.shape[0]
    per = both // micro
    block = pl.BlockSpec((1, per, ATT_DIM), lambda m, k: (k, m, 0))
    whole = pl.BlockSpec((n, per, ATT_DIM), lambda m, k: (0, m, 0))
    return pl.pallas_call(
        attention_backward_kernel,
        grid=(micro, q_table.shape[0]),
        out_shape=(
            jax.ShapeDtypeStruct((q_table.shape[0], both, ATT_DIM), bf16),
            jax.ShapeDtypeStruct((n, both, ATT_DIM), bf16),
            jax.ShapeDtypeStruct((n, both, ATT_DIM), bf16),
        ),
        in_specs=attention_specs(n, micro, per, q_at, k_at, k_at + 1) + [block],
        out_specs=(block, whole, whole),
        scratch_shapes=[pltpu.VMEM((n * per, ATT_DIM), bf16)] * 2
        + [pltpu.VMEM((n * per, ATT_DIM), f32)] * 2,
        compiler_params=pltpu.CompilerParams(vmem_limit_bytes=40 * 1024 * 1024),
        cost_estimate=about(19),
    )(q, mixed, mixed, table, q_table, q_aux, seg, grad)


def ffn_kernel(rows_ref, weight_ref, turned_ref, grad_ref, act_ref, gate_grad_ref, back_ref):
    half = grad_ref.shape[1]
    values = rough(rows_ref[...], weight_ref[...])
    gate, up = values[:, :half], values[:, half:]
    grad = grad_ref[...]
    sig = jax.nn.sigmoid(gate)
    silu = gate * sig
    act_ref[...] = (silu * up).astype(bf16)
    gate_grad_ref[:, :half] = (grad * up * (sig * (1.0 + gate * (1.0 - sig)))).astype(bf16)
    gate_grad_ref[:, half:] = (grad * silu).astype(bf16)
    back_ref[...] = rough(gate_grad_ref[...], turned_ref[...]).astype(bf16)


def ffn_both(rows, weight, turned_weight, act_grad):
    count, depth = rows.shape
    block, wide = 256, weight.shape[1]

    def by_block(columns):
        return pl.BlockSpec((block, columns), lambda k: (k, 0))

    def whole(array):
        return pl.BlockSpec(array.shape, lambda k: (0, 0))

    return pl.pallas_call(
        ffn_kernel,
        grid=(count // block,),
        out_shape=(
            jax.ShapeDtypeStruct((count, wide // 2), bf16),
            jax.ShapeDtypeStruct((count, wide), bf16),
            jax.ShapeDtypeStruct((count, depth), bf16),
        ),
        in_specs=[by_block(depth), whole(weight), whole(turned_weight), by_block(wide // 2)],
        out_specs=(by_block(wide // 2), by_block(wide), by_block(depth)),
        compiler_params=pltpu.CompilerParams(vmem_limit_bytes=48 * 1024 * 1024),
        cost_estimate=about(22),
    )(rows, weight, turned_weight, act_grad)


def local(
    tokens,
    doc_ends,
    input_gain,
    mixer_in,
    conv_weight,
    conv_bias,
    head_params,
    mixer_gain,
    mixer_out,
    attn_qkv,
    attn_out,
    ffn_gain,
    gate_up,
    down_proj,
    out_grad,
):
    n = lax.axis_size("seq")
    nd = lax.axis_size("dp")
    s = lax.axis_index("seq")
    d = lax.axis_index("dp")
    micro, _, per, _ = tokens.shape
    own = micro * per
    length = n * per
    rows = n * own
    owner = mixer_in.shape[0]
    inner = INNER // n
    width = -(-inner // 128) * 128
    heads = HEADS // n
    ffl = FF // n
    parts = n // ATT_HEADS
    group = ATT_HEADS // KV_HEADS
    conv_ch = INNER + 2 * STATE

    def mixed_order(value):
        if value.ndim == 1:
            return jnp.swapaxes(value.reshape(n, nd, owner), 0, 1).reshape(D)
        return regrouped(value, n, nd, owner)

    def plain_order(value):
        if value.ndim == 1:
            return jnp.swapaxes(value.reshape(nd, n, owner), 0, 1).reshape(D)
        return regrouped(value, nd, n, owner)

    def widened(value):
        return jnp.pad(value, [(0, 0)] * (value.ndim - 1) + [(0, width - inner)])

    def from_seq(value):
        return value.reshape(micro, n, per, -1).transpose(1, 0, 2, 3).reshape(rows, -1)

    def gathered(value):
        return lax.all_gather(value, "seq", axis=0, tiled=True)

    def scattered(value, *others):
        total = lax.psum_scatter(value.astype(bf16), "seq", scatter_dimension=0, tiled=True)
        return (after(total, *others) if others else total).astype(f32)

    token_b = mixed_order(tokens.reshape(own, D))
    token_rows = token_b.astype(f32)
    grad_rows = mixed_order(out_grad.reshape(own, D))

    tap_count = conv_weight.shape[1]
    small_own = jnp.concatenate(
        [input_gain, conv_weight.reshape(-1), conv_bias, mixer_gain, ffn_gain]
    )
    small_count = small_own.shape[0]
    small_cols = -(-small_count // owner)
    small_own = jnp.pad(small_own, (0, small_cols * owner - small_count)).reshape(owner, small_cols)

    steps_own = jnp.pad(
        jnp.concatenate(
            [
                mixer_in[:, 2 * INNER + 2 * STATE :].reshape(owner, n, heads).transpose(1, 0, 2),
                jnp.broadcast_to(small_own[None], (n,) + small_own.shape),
            ],
            axis=2,
        ),
        ((0, 0), (0, 0), (0, DT_PAD - heads - small_cols)),
    )
    q_of = [k // parts for k in range(n)]
    kv_of = [ATT_HEADS + q // group for q in q_of]
    sizes = [width, width, 2 * STATE, DT_PAD, ATT_DIM, ATT_DIM, ATT_DIM]
    starts = [sum(sizes[:k]) for k in range(len(sizes) + 1)]
    every = slice(None)
    moves = []
    for k in range(n):
        for which, source, target, wide in (
            (0, k * inner, starts[0], inner),
            (0, INNER + k * inner, starts[1], inner),
            (0, 2 * INNER, starts[2], 2 * STATE),
            (1, q_of[k] * ATT_DIM, starts[4], ATT_DIM),
            (1, kv_of[k] * ATT_DIM, starts[5], ATT_DIM),
            (1, (kv_of[k] + KV_HEADS) * ATT_DIM, starts[6], ATT_DIM),
        ):
            moves.append(
                (which, (every, slice(source, source + wide)), (k, every, slice(target, target + wide)))
            )
        moves.append((2, (k,), (k, every, slice(starts[3], starts[4]))))
        if width != inner:
            gap = slice(0, width - inner)
            for target in (starts[1], starts[2]):
                hole = slice(target - width + inner, target)
                moves.append((3, (every, gap), (k, every, hole)))
    blank = jnp.zeros((owner, 128), bf16)
    packed = assembled(
        (n, owner, starts[-1]), bf16, moves, mixer_in, attn_qkv, steps_own, blank
    )
    sent_in = exchanged(packed, "seq")
    positions = jnp.arange(length, dtype=jnp.int32)
    seg = jnp.stack([segment_of(positions, doc_ends[m, 0]) for m in range(micro)])

    blocks = seg.reshape(micro, n, per)
    columns = [seg.astype(f32)]
    for back in range(1, CONV):
        moved = jnp.pad(seg[:, : length - back], ((0, 0), (back, 0)), constant_values=-1)
        columns.append((moved == seg).astype(f32))
    prior = jnp.concatenate(
        [jnp.full((micro, 1), -1, jnp.int32), blocks[:, :-1, per - 1]], axis=1
    )
    last = blocks[:, :, per - 1]
    for flag in (
        blocks == prior[:, :, None],
        blocks == last[:, :, None],
        jnp.broadcast_to((last == prior)[:, :, None], blocks.shape),
        jnp.zeros_like(blocks),
    ):
        columns.append(flag.astype(f32).reshape(micro, length))
    aux = from_seq(jnp.stack(columns, axis=-1))
    seg_blocks = blocks.transpose(1, 0, 2).reshape(n * micro, 1, per).astype(f32)
    cosine, sine = rope_tables(positions)
    table = jnp.concatenate([cosine, sine], axis=1).reshape(n, per, 2 * ATT_DIM)
    part = s % parts

    def taken(value):
        if parts == 1:
            return value
        split = value.reshape(n // parts, parts, *value.shape[1:])
        return lax.dynamic_index_in_dim(split, part, 1, False)

    def put_back(value):
        if parts == 1:
            return value
        here = (jnp.arange(parts) == part).reshape(1, parts, 1, 1)
        return jnp.where(here, value[:, None], 0).reshape(n, *value.shape[1:])

    q_aux = jnp.stack(
        [seg.astype(f32), jnp.broadcast_to(positions.astype(f32), seg.shape)], axis=-1
    )
    q_aux = jnp.pad(from_seq(q_aux), ((0, 0), (0, 6))).reshape(n, own, 8)
    q_aux, q_table = taken(q_aux), taken(table)
    w_in = after(dp_gather(sent_in), aux, seg_blocks, table, q_aux)
    small = w_in[:, :, :, starts[3] + heads : starts[3] + heads + small_cols]
    small = jnp.swapaxes(small, 0, 1).reshape(n * nd, -1)[:, :small_count]
    w_in = w_in.reshape(D, starts[-1])
    gu_moves = []
    for k in range(n):
        for half in range(2):
            gu_moves.append(
                (
                    (every, slice(half * FF + k * ffl, half * FF + (k + 1) * ffl)),
                    (k, every, slice(half * ffl, (half + 1) * ffl)),
                )
            )
    gu_own = assembled(
        (n, owner, 2 * ffl), bf16, [(0, flat, cube) for flat, cube in gu_moves], gate_up
    )
    sent_gu = exchanged(after(gu_own, w_in), "seq")
    cuts = [owner, CONV * tap_count, tap_count, mixer_gain.shape[0], owner]
    at = [sum(cuts[:k]) for k in range(len(cuts) + 1)]
    small = small.astype(f32)
    gain_in = mixed_order(small[:, at[0] : at[1]].reshape(-1))
    taps = (
        small[:, at[1] : at[2]].reshape(-1, CONV, tap_count).transpose(1, 0, 2).reshape(CONV, -1)
    )
    shift = small[:, at[2] : at[3]].reshape(-1)
    gain_mix = widened(
        lax.dynamic_slice_in_dim(small[:, at[3] : at[4]].reshape(-1), s * inner, inner)
    )
    gain_ffn = mixed_order(small[:, at[4] : at[5]].reshape(-1))
    conv_rows = jnp.concatenate([taps, shift[None], jnp.zeros((3, conv_ch), f32)])
    conv_rows = jnp.concatenate(
        [
            widened(lax.dynamic_slice_in_dim(conv_rows, s * inner, inner, axis=1)),
            conv_rows[:, INNER:],
        ],
        axis=1,
    )
    head = lax.dynamic_slice_in_dim(head_params, s * heads, heads, axis=1)
    head_rows = jnp.pad(head, ((0, 5), (0, DT_PAD - heads)))
    skip_row = widened(jnp.repeat(head[2], HEAD_DIM)[None])

    token_all = gathered(after(token_b, sent_in))
    token_f32 = token_all.astype(f32)
    normed = (token_f32 * rms_row(token_f32) * gain_in).astype(bf16)
    grads = gathered(after(grad_rows, token_all, w_in))
    mixed = dot(normed, w_in)
    out_own = after(mixed_order(jnp.concatenate([mixer_out, attn_out])), w_in)
    out_cut = mixer_out.shape[0]
    if nd == 4 and out_cut % 16 == 0:
        pieces = [after(permuted(out_own, "dp", k), mixed) for k in range(1, nd)]
        w_mix, w_att = placed_pieces([out_own, *pieces], d, [0, out_cut, out_own.shape[0]])
    else:
        out_parts = dp_gather(out_own, forward=False)
        w_mix = out_parts[:, :out_cut].reshape(-1, D)
        w_att = out_parts[:, out_cut:].reshape(-1, D)
    w_mix = jnp.pad(w_mix, ((0, width - inner), (0, 0)))
    if parts > 1:
        other = permuted(w_att, "seq", 1)
        w_att = jnp.where(
            (s & 1) != 0, jnp.concatenate([other, w_att]), jnp.concatenate([w_att, other])
        )
    w_gu = dp_gather(after(sent_gu, mixed), forward=False).reshape(D, 2 * ffl)
    w_down = dp_gather(after(mixed_order(down_proj), mixed), forward=False).reshape(ffl, D)
    ssd_args = (mixed, aux, seg_blocks, conv_rows, head_rows, skip_row)
    y, gated, enter = ssd_forward(*ssd_args, n, micro)
    squares = row_sums(jnp.sum(gated * gated, axis=1)) / INNER
    r_mix = lax.rsqrt(squares + epsilon)[:, None]
    mixer_b = (gated * r_mix * gain_mix).astype(bf16)

    q_at = starts[4] // ATT_DIM
    mixed_blocks = mixed.reshape(n, own, starts[-1])
    queries, own_q_at = mixed_blocks, q_at
    if parts > 1:
        queries, own_q_at = taken(mixed_blocks[:, :, starts[4] : starts[5]]), 0
    q_aux = after(q_aux, sent_gu, gated)
    att_args = (queries, mixed_blocks, table, q_table, q_aux)
    att_args = att_args + (seg.astype(f32)[:, None],)
    attended_b = put_back(attention_forward(*att_args, own_q_at, q_at + 1)).reshape(rows, ATT_DIM)
    branch_b = jnp.concatenate([mixer_b, attended_b], axis=1)
    w_out = jnp.concatenate([w_mix, w_att])
    branches = dot(branch_b, w_out)
    branches = after(branches.astype(bf16), grads)
    hidden = token_rows + scattered(branches, w_gu, w_down)
    ffn_own = (hidden * rms_row(hidden) * gain_ffn).astype(bf16)
    ffn_in = gathered(ffn_own)

    act_grad = after(dot_t(grads, w_down), branches)
    turned_gu = after(w_gu.T, branches)
    activated_b, gate_grad, ffn_back = ffn_both(ffn_in, w_gu, turned_gu, act_grad)
    gu_total = cross(ffn_in, gate_grad).astype(bf16)
    down_total = cross(activated_b, grads).astype(bf16)
    ffn_in_grad = scattered(ffn_back, gu_total, down_total)

    def over_dp(total, forward, meanwhile=()):
        return dp_scatter(total.reshape(nd, n * owner, -1), forward, meanwhile).astype(bf16)

    def to_owners(part_sum):
        return exchanged(part_sum.reshape(n, owner, -1), "seq")

    gu_part = over_dp(gu_total, False)
    down_grad = dp_scatter(down_total.reshape(nd, -1, D), False)
    hidden_part, ffn_gain_grad = rms_back(ffn_in_grad, hidden, gain_ffn)
    hidden_grad = hidden_part + grad_rows.astype(f32)
    hidden_b = after(gathered(hidden_grad.astype(bf16)), gu_part, down_grad)
    gu_sum = to_owners(gu_part)

    ffn_out = after(dot(activated_b, w_down).astype(bf16), hidden_b)
    ffn_sum = scattered(ffn_out)
    layer_out = plain_order((hidden + ffn_sum).astype(bf16))

    branch_total = cross(branch_b, hidden_b).astype(bf16)
    mix_total, att_total = branch_total[:width], branch_total[width:]
    if parts > 1:
        half = att_total.shape[0] // 2
        low, high = att_total[:half], att_total[half:]
        odd = (s & 1) != 0
        other = permuted(jnp.where(odd, low, high), "seq", 1)
        att_total = (jnp.where(odd, high, low).astype(f32) + other.astype(f32)).astype(bf16)
    out_total = jnp.concatenate(
        [mix_total[:inner].reshape(nd, -1, D), att_total.reshape(nd, -1, D)], axis=1
    )
    out_sum = dp_scatter(out_total, False)

    branch_grad = dot_t(hidden_b, w_out)
    mix_grad = branch_grad[:, :width]
    scaled = mix_grad * gain_mix
    along = jnp.sum(scaled * gated, axis=1)
    along = along + permuted(along, "seq", 1)
    att_grad = taken(branch_grad[:, width:].astype(bf16).reshape(n, own, ATT_DIM))
    att_grad = after(att_grad, along)
    q_grad, k_grad, v_grad = attention_backward(*att_args, att_grad, own_q_at, q_at + 1)
    qkv_grad = jnp.concatenate([put_back(q_grad), k_grad, v_grad], axis=2).reshape(rows, -1)

    along = other_pairs(along)[:, None] / INNER
    mix_gain_grad = jnp.sum(mix_grad * gated * r_mix, axis=0)
    gated_grad = scaled * r_mix - gated * (r_mix * r_mix * r_mix) * along
    mixed_grad, conv_g, head_g, skip_g = ssd_backward(
        *ssd_args, y, enter, gated_grad, qkv_grad, n, micro
    )
    mixed_grad = after(mixed_grad, out_sum, gu_sum)

    def placed(value, full):
        whole = jnp.zeros(value.shape[:-1] + (full,), f32)
        return lax.dynamic_update_slice_in_dim(
            whole, value, s * value.shape[-1], axis=value.ndim - 1
        )

    def by_owner(value):
        return value.reshape(-1, n * nd, value.shape[-1] // (n * nd)).transpose(1, 0, 2)

    conv_full = jnp.concatenate(
        [placed(conv_g[: CONV + 1, :inner], INNER), conv_g[: CONV + 1, width:]], axis=1
    )
    vectors = [
        by_owner(conv_full),
        by_owner(placed(mix_gain_grad[:inner], INNER)[None]),
        by_owner(plain_order(ffn_gain_grad)[None]),
    ]
    vectors = jnp.concatenate([v.reshape(n * nd, -1) for v in vectors], axis=1)
    vector_count = vectors.shape[1]
    vector_cols = -(-vector_count // owner)
    vectors = jnp.pad(vectors, ((0, 0), (0, vector_cols * owner - vector_count)))
    vectors = vectors.reshape(n, nd, owner, vector_cols).transpose(1, 0, 2, 3)
    vectors = vectors.reshape(D, vector_cols)

    in_back = after(dot_t(mixed_grad, w_in).astype(bf16), ffn_sum)
    mixed_grad = after(mixed_grad, in_back)
    zx_total = cross(normed, mixed_grad[:, : starts[2]]).astype(bf16)
    at_steps, at_heads = starts[3] - starts[2], starts[4] - starts[2]
    spare = starts[-1] - starts[2] - at_steps - heads - vector_cols
    rest_total = cross(normed, mixed_grad[:, starts[2] :])
    rest_total = (
        rest_total + jnp.pad(vectors, ((0, 0), (at_steps + heads, spare)))
    ).astype(bf16)
    zx_part = over_dp(zx_total, True, (rest_total,))
    zx_sum = to_owners(zx_part)
    rest_sum = to_owners(over_dp(rest_total, True, (zx_total,)))
    gate_up_grad = assembled(
        (owner, 2 * FF), f32, [(0, cube, flat) for flat, cube in gu_moves], gu_sum
    )
    out_plain = plain_order(out_sum)
    mixer_out_grad = out_plain[: mixer_out.shape[0]]
    attn_out_grad = out_plain[mixer_out.shape[0] :]
    down_grad = plain_order(down_grad)
    normed_grad = scattered(
        in_back, gate_up_grad, mixer_out_grad, attn_out_grad, down_grad, layer_out
    )
    head_g = jnp.concatenate(
        [head_g[:2, :heads], skip_g[:1, :inner].reshape(1, heads, HEAD_DIM).sum(axis=2)]
    )
    head_g = after(placed(head_g, HEADS).reshape(-1), normed_grad)
    head_g = summed(head_g, ("dp",))
    head_g = head_g + permuted(head_g, "seq", 1)
    others = [head_g] + [permuted(head_g, "seq", by) for by in range(2, n, 2)]
    head_g = jnp.sum(jnp.stack(others)[jnp.arange(n // 2) ^ (s // 2)], axis=0)
    token_part, _ = rms_back(normed_grad, token_rows, gain_in)
    token_grad = plain_order(token_part + hidden_grad)
    zx_sum = after(zx_sum, token_grad, head_g)

    bc_sum = jnp.sum(rest_sum[:, :, :at_steps].astype(f32), axis=0)
    step_sum = (
        rest_sum[:, :, at_steps : at_steps + heads]
        .transpose(1, 0, 2)
        .reshape(owner, HEADS)
    )
    moves = []
    for k in range(n):
        for half in range(2):
            source = slice(half * width, half * width + inner)
            target = slice(half * INNER + k * inner, half * INNER + (k + 1) * inner)
            moves.append((0, (k, every, source), (every, target)))
    moves.append((1, (every, every), (every, slice(2 * INNER, 2 * INNER + 2 * STATE))))
    moves.append((2, (every, every), (every, slice(2 * INNER + 2 * STATE, PROJ))))
    mixer_in_grad = assembled((owner, PROJ), f32, moves, zx_sum, bc_sum, step_sum)
    head_sum = rest_sum[:, :, at_heads:].astype(f32)
    head_sum = [head_sum[:, :, k * ATT_DIM : (k + 1) * ATT_DIM] for k in range(3)]
    q_sum = head_sum[0].reshape(ATT_HEADS, parts, owner, ATT_DIM).sum(axis=1)
    k_sum = head_sum[1].reshape(KV_HEADS, n // KV_HEADS, owner, ATT_DIM).sum(axis=1)
    v_sum = head_sum[2].reshape(KV_HEADS, n // KV_HEADS, owner, ATT_DIM).sum(axis=1)
    attn_qkv_grad = (
        jnp.concatenate([q_sum, k_sum, v_sum]).transpose(1, 0, 2).reshape(owner, -1)
    )

    vectors = jnp.sum(
        rest_sum[:, :, at_steps + heads : at_steps + heads + vector_cols].astype(f32), axis=0
    ).reshape(-1)[:vector_count]
    ends = [(CONV + 1) * tap_count, (CONV + 1) * tap_count + mixer_gain.shape[0]]
    conv_own = vectors[: ends[0]].reshape(CONV + 1, tap_count)
    in_gain_grad = (
        jnp.sum(mixer_in.astype(f32) * mixer_in_grad, axis=1)
        + jnp.sum(attn_qkv.astype(f32) * attn_qkv_grad, axis=1)
    ) / input_gain.astype(f32)
    return (
        layer_out.reshape(micro, 1, per, D),
        token_grad.reshape(micro, 1, per, D),
        in_gain_grad,
        mixer_in_grad,
        conv_own[:CONV],
        conv_own[CONV],
        head_g.reshape(3, HEADS),
        vectors[ends[0] : ends[1]],
        mixer_out_grad,
        attn_qkv_grad,
        attn_out_grad,
        vectors[ends[1] :],
        gate_up_grad,
        down_grad,
    )


def solution(mesh):
    rows = P(("seq", "dp"), None)
    vector = P(("seq", "dp"))
    activations = P(None, "dp", "seq", None)
    return jax.shard_map(
        local,
        mesh=mesh,
        in_specs=(
            activations,
            P(None, "dp", None),
            vector,
            rows,
            P(None, ("seq", "dp")),
            vector,
            P(),
            vector,
            rows,
            rows,
            rows,
            vector,
            rows,
            rows,
            activations,
        ),
        out_specs=(
            activations,
            activations,
            vector,
            rows,
            P(None, ("seq", "dp")),
            vector,
            P(),
            vector,
            rows,
            rows,
            rows,
            vector,
            rows,
            rows,
        ),
        check_vma=False,
    )
```

time: 1440 us -> 926 us (0.64)
  waiting for transfers between devices: 611 us -> 386 us
  other arithmetic: 220 us -> 68.7 us
  Pallas kernels: 0 us -> 133 us
  local copies, waits for them, and re-layouts: 199 us -> 95.1 us
  starting transfers between devices: 168 us -> 82.4 us
  matrix products: 212 us -> 136 us
    ppermute x89 -> x44, waiting for transfers between devices: 309 us -> 169 us  [permuted(): return lax.ppermute(value, axis, pairs)]
    pallas_call x0 -> x47, Pallas kernels: none -> 133 us  [the longest x1 41.4 us: ssd_backward(): pl.pallas_call(ssd_backward_kernel, grid=(micro, n), out_shape=(jax.Shape...]
    ppermute x89 -> x44, starting transfers between devices: 168 us -> 57.3 us  [permuted(): return lax.ppermute(value, axis, pairs)]
    reduce_scatter x4, waiting for transfers between devices: 175 us -> 79.1 us  [scattered(): lax.psum_scatter(value.astype(bf16), 'seq', scatter_dimension=0, tiled=True)]
    all_to_all x0 -> x5, waiting for transfers between devices: none -> 53.7 us  [exchanged(): return lax.all_to_all(blocks, axis, 0, 0, tiled=True)]
    all_gather x4, waiting for transfers between devices: 127 us -> 84.1 us  [gathered(): return lax.all_gather(value, 'seq', axis=0, tiled=True)]
    reduce_sum x12 -> x10, other arithmetic: 46.1 us -> 8.05 us  [the longest x1 1.78 us: local(): jnp.sum(mixer_in.astype(f32) * mixer_in_grad, axis=1)]
    dot_general x19 -> x0, matrix products: 34.9 us -> none  [the longest x3 14.7 us: mixer_core(): y = jnp.einsum('btsh,bshp->bthp', mixing, x, preferred_element_type=f32)]
  transfers between devices with their start and end apart: 97 -> 57, of which waited for: 43 -> 28; matrix products, arithmetic and copies ran while one was open for 21% -> 27% of each run, Pallas kernels for 0% -> 11%
where the time goes in v2:
time: 926 us; the launch traced here: 917 us
  waiting for transfers between devices  386 us (42%)
  matrix products  136 us (15%)
  Pallas kernels  133 us (14%)
  local copies, waits for them, and re-layouts  95.1 us (10%)
  starting transfers between devices  82.4 us (9%)
  other arithmetic  68.7 us (7%)
  between operations  16.1 us (2%)
    ppermute x44, waiting for transfers between devices, permuted(): return lax.ppermute(value, axis, pairs)  169 us
    all_gather x4, waiting for transfers between devices, gathered(): return lax.all_gather(value, 'seq', axis=0, tiled=True)  84.1 us
    reduce_scatter x4, waiting for transfers between devices, scattered(): lax.psum_scatter(value.astype(bf16), 'seq', scatter_dimension=0, tiled=True)  79.1 us
    dot_general x5, matrix products, cross(): lax.dot_general(left, right, (((0,), (0,)), ((), ())), preferred_element_...  58 us
    ppermute x44, starting transfers between devices, permuted(): return lax.ppermute(value, axis, pairs)  57.3 us
    all_to_all x5, waiting for transfers between devices, exchanged(): return lax.all_to_all(blocks, axis, 0, 0, tiled=True)  53.7 us
    pallas_call x1, Pallas kernels, ssd_backward(): pl.pallas_call(ssd_backward_kernel, grid=(micro, n), out_shape=(jax.Shape...  41.4 us
    dot_general x3, matrix products, dot_t(): lax.dot_general(left, right, (((1,), (1,)), ((), ())), preferred_element_...  41.1 us
  transfers between devices with their start and end apart: 57, of which 28 were waited for; matrix products, arithmetic and copies ran while one was open for 27% of the time, Pallas kernels for 11%

profile of v2, /device:TPU:0, one launch (start us, length us, event | category | flops | bytes accessed | tf_op | source)
XLA Modules:
  0.0 916.7 jit_solution(7273560798388328231)
XLA Ops:
  9.0 2.8 concatenate.92
  15.5 6.5 all-to-all-start
  24.4 41.1 %all-to-all-done.refs_1_ = bf16[8,64,1792]{2,1,0:T(8,128)(2,1)S(1)} async-done(((bf16[8,64,1792]{2,1,0:T(8,128)(2,1)}), bf16[8,64,1792]{2,1,0:T(8,128)(2,1)S(1)}, u32[]{:S(2)}, u32[]{:S(2)}) %all-to-all-start) | async-done | bytes 1835040 | tf_op jit(solution)/shard_map/all_to_all | solution.py:70
  80.0 3.8 broadcast_in_dim.103
  85.1 24.6 %collective-permute-done = bf16[8,64,1792]{2,1,0:T(8,128)(2,1)} collective-permute-done((bf16[8,64,1792]{2,1,0:T(8,128)(2,1)}, bf16[8,64,1792]{2,1,0:T(8,128)(2,1)}, u32[]{:S(2)}, u32[]{:S(2)}) %collective-permute-start) | collective-permute-done | bytes 1835040 | tf_op jit(solution)/shard_map/ppermute | solution.py:42
  115.3 2.9 bitcast_dynamic-update-slice_fusion.1
  118.2 2.9 bitcast_dynamic-update-slice_fusion
  121.1 10.9 %collective-permute-done.2 = bf16[4,64,1792]{2,1,0:T(8,128)(2,1)S(1)} collective-permute-done((bf16[4,64,1792]{2,1,0:T(8,128)(2,1)S(1)}, bf16[4,64,1792]{2,1,0:T(8,128)(2,1)S(1)}, u32[]{:S(2)}, u32[]{:S(2)}) %collective-permute-start.2) | collective-permute-done | bytes 917536 | tf_op jit(solution)/shard_map/ppermute | solution.py:42
  132.0 2.5 collective-permute-done.3
  135.9 11.9 %all-gather.5.cloned.1.call-done.refs_1_ = bf16[2048,2048]{1,0:T(8,128)(2,1)} async-done(((bf16[256,2048]{1,0:T(8,128)(2,1)}), bf16[2048,2048]{1,0:T(8,128)(2,1)}) %all-gather.5.cloned.1.call-update) | async-done | bytes 8388624 | tf_op jit(solution)/shard_map/all_gather | solution.py:810
  153.4 2.4 collective-permute-start.10
  157.6 4.3 all-to-all-start.1
  162.1 5.2 fusion
  167.9 21.9 %fusion.78.mixed_ref.before_ref.refs_1_ = f32[2048,1792]{1,0:T(8,128)} fusion(bf16[2048,1792]{1,0:T(8,128)(2,1)} %bitcast.26.refs_1_.refs_2_, bf16[2048,2048]{1,0:T(8,128)(2,1)} %all-gather.5.cloned.1.call-done.refs_1_, f32[2048]{0:T(1024)S(1)} %mul.295, f32[2048]{0:T(1024)S(1)} %add_rsqrt_fusion.1), kind=kOutput, calls=%fused_computation.240 | convolution fusion | flops 15049162752 | bytes 30425088 | tf_op jit(solution)/shard_map/dot_general | solution.py:216
  189.9 19.0 %shard_map.258 = (f32[2048,384]{1,0:T(8,128)S(1)}, f32[2048,384]{1,0:T(8,128)S(1)}, bf16[16,256,384]{2,1,0:T(8,128)(2,1)S(1)}) custom-call(f32[2048,1792]{1,0:T(8,128)} %fusion.78.mixed_ref.before_ref.refs_1_, f32[2048,1792]{1,0:T(8,128)} %fusion.78.mixed_ref.before_ref.refs_1_, f32[2048,8]{1,0:T(8,128)S(1)} %bitcast.237, f32[16,1,128]{2,1,0:T(1,128)S(1)} %bitcast.246, ...), custom_call_target="tpu_custom_call" | custom-call | bytes 72000000 | tf_op jit(solution)/shard_map/pallas_call | solution.py:512
  225.7 14.7 %shard_map.262 = bf16[8,256,128]{2,1,0:T(8,128)(2,1)S(1)} custom-call(f32[8,256,1792]{2,1,0:T(8,128)} %bitcast.248, f32[8,256,1792]{2,1,0:T(8,128)} %bitcast.249, f32[8,256,1792]{2,1,0:T(8,128)} %bitcast.250, f32[8,128,256]{2,1,0:T(8,128)S(1)} %copy-done.8, f32[8,128,256]{2,1,0:T(8,128)S(1)} %copy-done.8, f32[8,256,8]{2,1,0:T(8,128)S(1)} %copy-done.10, ...), custom_call_target="tpu_custom_call" | custom-call | bytes 50400000 | tf_op jit(solution)/shard_map/pallas_call | solution.py:686
  242.6 8.3 convolution_convert_fusion.2.refs_0_
  250.9 2.6 all-gather.7.cloned.1.call-done.refs_1_
  262.4 2.5 broadcast_in_dim.111
  267.2 3.4 collective-permute-done.14
  270.7 2.4 collective-permute-start.13
  274.2 9.3 %collective-permute-done.15 = bf16[128,2048]{1,0:T(8,128)(2,1)} collective-permute-done((bf16[128,2048]{1,0:T(8,128)(2,1)}, bf16[128,2048]{1,0:T(8,128)(2,1)}, u32[]{:S(2)}, u32[]{:S(2)}) %collective-permute-start.15) | collective-permute-done | bytes 524320 | tf_op jit(solution)/shard_map/ppermute | solution.py:42
  284.6 19.7 %collective-permute-done.11 = bf16[8,64,1024]{2,1,0:T(8,128)(2,1)S(1)} collective-permute-done((bf16[8,64,1024]{2,1,0:T(8,128)(2,1)}, bf16[8,64,1024]{2,1,0:T(8,128)(2,1)S(1)}, u32[]{:S(2)}, u32[]{:S(2)}) %collective-permute-start.11) | collective-permute-done | bytes 1048608 | tf_op jit(solution)/shard_map/ppermute | solution.py:42
  305.4 21.9 %collective-permute-done.12 = bf16[8,64,1024]{2,1,0:T(8,128)(2,1)S(1)} collective-permute-done((bf16[8,64,1024]{2,1,0:T(8,128)(2,1)}, bf16[8,64,1024]{2,1,0:T(8,128)(2,1)S(1)}, u32[]{:S(2)}, u32[]{:S(2)}) %collective-permute-start.12) | collective-permute-done | bytes 1048608 | tf_op jit(solution)/shard_map/ppermute | solution.py:42
  329.5 14.3 %reduce-scatter.5.cloned.1.call-done.refs_0_ = bf16[256,2048]{1,0:T(8,128)(2,1)} async-done(((bf16[2048,2048]{1,0:T(8,128)(2,1)}), bf16[256,2048]{1,0:T(8,128)(2,1)}) %reduce-scatter.5.cloned.1.call-update) | async-done | bytes 1048592 | tf_op jit(solution)/shard_map/reduce_scatter | solution.py:813
  348.4 6.6 copy.145.refs_0_
  355.0 11.3 %fusion.81.refs_0_ = f32[2048,512]{1,0:T(8,128)} fusion(bf16[2048,2048]{1,0:T(8,128)(2,1)} %all-gather.7.cloned.1.call-done.refs_1_, bf16[512,2048]{1,0:T(8,128)(2,1)} %bitcast.268), kind=kOutput, calls=%fused_computation.242 | convolution fusion | flops 4294967296 | bytes 14680064 | tf_op jit(solution)/shard_map/dot_general | solution.py:220
  366.3 62.6 %all-gather.9.cloned.1.call-done.rows_ref = bf16[2048,2048]{1,0:T(8,128)(2,1)} async-done(((bf16[256,2048]{1,0:T(8,128)(2,1)}), bf16[2048,2048]{1,0:T(8,128)(2,1)}) %all-gather.9.cloned.1.call-update) | async-done | bytes 8388624 | tf_op jit(solution)/shard_map/all_gather | solution.py:810
  428.9 25.1 %shard_map.278 = (bf16[2048,512]{1,0:T(8,128)(2,1)S(1)}, bf16[2048,1024]{1,0:T(8,128)(2,1)}, bf16[2048,2048]{1,0:T(8,128)(2,1)}) custom-call(bf16[2048,2048]{1,0:T(8,128)(2,1)} %all-gather.9.cloned.1.call-done.rows_ref, bf16[2048,1024]{1,0:T(8,128)(2,1)} %bitcast.39.refs_1_.weight_ref, bf16[1024,2048]{1,0:T(8,128)(2,1)} %shard_map.276.turned_ref, ...), custom_call_target="tpu_custom_call" | custom-call | bytes 79200000 | tf_op jit(solution)/shard_map/pallas_call | solution.py:744
  455.8 10.1 %convolution_convert_fusion.6.refs_2_ = bf16[512,2048]{1,0:T(8,128)(2,1)} fusion(bf16[2048,512]{1,0:T(8,128)(2,1)} %copy-done.45, bf16[2048,2048]{1,0:T(8,128)(2,1)} %all-gather.7.cloned.1.call-done.refs_1_), kind=kOutput, calls=%fused_computation.29 | convolution fusion | flops 4296015872 | bytes 12582912 | tf_op jit(solution)/shard_map/dot_general | solution.py:224
  465.9 12.9 %convolution_convert_fusion.3.refs_1_ = bf16[2048,1024]{1,0:T(8,128)(2,1)} fusion(bf16[2048,2048]{1,0:T(8,128)(2,1)} %all-gather.9.cloned.1.call-done.rows_ref, bf16[2048,1024]{1,0:T(8,128)(2,1)S(1)} %copy-done.89), kind=kOutput, calls=%fused_computation.12 | convolution fusion | flops 8592031744 | bytes 16777216 | tf_op jit(solution)/shard_map/dot_general | solution.py:224
  478.9 64.8 %reduce-scatter.7.cloned.1.call-done.refs_0_ = bf16[256,2048]{1,0:T(8,128)(2,1)} async-done(((bf16[2048,2048]{1,0:T(8,128)(2,1)}), bf16[256,2048]{1,0:T(8,128)(2,1)}) %reduce-scatter.7.cloned.1.call-update) | async-done | bytes 1048592 | tf_op jit(solution)/shard_map/reduce_scatter | solution.py:813
  543.7 2.9 fusion.14
  553.6 2.6 dynamic-slice_bitcast_fusion.2
  559.2 5.7 collective-permute-done.20
  565.0 2.4 collective-permute-start.19
  567.3 6.7 convolution_convert_fusion.1.refs_0_
  574.1 3.6 collective-permute-done.21
  577.7 2.4 fusion.35.refs_2_.in_ref
  580.0 18.7 %collective-permute-done.17 = bf16[512,1024]{1,0:T(8,128)(2,1)S(1)} collective-permute-done((bf16[512,1024]{1,0:T(8,128)(2,1)S(1)}, bf16[512,1024]{1,0:T(8,128)(2,1)S(1)}, u32[]{:S(2)}, u32[]{:S(2)}) %collective-permute-start.17) | collective-permute-done | bytes 1048608 | tf_op jit(solution)/shard_map/ppermute | solution.py:42
  598.7 20.3 %collective-permute-done.18 = bf16[512,1024]{1,0:T(8,128)(2,1)S(1)} collective-permute-done((bf16[512,1024]{1,0:T(8,128)(2,1)S(1)}, bf16[512,1024]{1,0:T(8,128)(2,1)S(1)}, u32[]{:S(2)}, u32[]{:S(2)}) %collective-permute-start.18) | collective-permute-done | bytes 1048608 | tf_op jit(solution)/shard_map/ppermute | solution.py:42
  619.0 3.1 fusion.22.refs_1_
  622.1 7.0 all-gather.11.cloned.1.call-done.refs_0_
  629.1 4.4 all-to-all-start.2
  633.7 9.0 convolution_convert_fusion.5
  643.0 8.3 fusion.82
  660.3 2.4 collective-permute-start.25
  666.5 19.2 %shard_map.284 = (bf16[8,256,128]{2,1,0:T(8,128)(2,1)S(1)}, bf16[8,256,128]{2,1,0:T(8,128)(2,1)S(1)}, bf16[8,256,128]{2,1,0:T(8,128)(2,1)S(1)}) custom-call(f32[8,256,1792]{2,1,0:T(8,128)} %bitcast.251, f32[8,256,1792]{2,1,0:T(8,128)} %bitcast.252, f32[8,256,1792]{2,1,0:T(8,128)} %bitcast.253, f32[8,128,256]{2,1,0:T(8,128)S(1)} %copy-done.9, ...), custom_call_target="tpu_custom_call" | custom-call | bytes 68400000 | tf_op jit(solution)/shard_map/pallas_call | solution.py:704
  691.3 41.4 %shard_map.285 = (bf16[2048,1792]{1,0:T(8,128)(2,1)}, f32[8,896]{1,0:T(8,128)S(1)}, f32[8,128]{1,0:T(8,128)S(1)}, f32[8,384]{1,0:T(8,128)S(1)}) custom-call(f32[2048,1792]{1,0:T(8,128)} %fusion.78.mixed_ref.before_ref.refs_1_, f32[2048,1792]{1,0:T(8,128)} %fusion.78.mixed_ref.before_ref.refs_1_, f32[2048,8]{1,0:T(8,128)S(1)} %bitcast.238, ...), custom_call_target="tpu_custom_call" | custom-call | bytes 154800000 | tf_op jit(solution)/shard_map/pallas_call | solution.py:549
  732.8 2.4 fusion.33.refs_1_.in_ref
  735.2 21.5 %convolution_convert_fusion.refs_0_ = bf16[2048,2048]{1,0:T(8,128)(2,1)} fusion(bf16[2048,1792]{1,0:T(8,128)(2,1)} %shard_map.286.refs_0_, bf16[2048,1792]{1,0:T(8,128)(2,1)} %bitcast.26.refs_1_.refs_2_), kind=kOutput, calls=%fused_computation.7 | convolution fusion | flops 15036579840 | bytes 23068672 | tf_op jit(solution)/shard_map/dot_general | solution.py:220
  756.7 2.8 convert_element_type.350.refs_1_
  762.3 13.7 %add_convert_fusion.refs_1_ = bf16[2048,1024]{1,0:T(8,128)(2,1)S(1)} fusion(f32[2048,12]{1,0:T(8,128)S(1)} %bitcast.275, bf16[2048,1792]{1,0:T(8,128)(2,1)} %shard_map.293, bf16[2048,2048]{1,0:T(8,128)(2,1)} %all-gather.5.cloned.1.call-done.refs_1_, f32[2048]{0:T(1024)S(1)} %copy-done.75, f32[2048]{0:T(1024)S(1)} %copy-done.85), kind=kOutput, calls=%fused_computation.6 | convolution fusion | flops 8610906112 | bytes 16891904 | tf_op jit(solution)/shard_map/dot_general | solution.py:224
  782.2 12.3 %convolution_convert_fusion.4.refs_1_ = bf16[2048,768]{1,0:T(8,128)(2,1)} fusion(bf16[2048,1792]{1,0:T(8,128)(2,1)} %shard_map.293, bf16[2048,2048]{1,0:T(8,128)(2,1)} %all-gather.5.cloned.1.call-done.refs_1_, f32[2048]{0:T(1024)S(1)} %copy-done.75, f32[2048]{0:T(1024)S(1)} %copy-done.85), kind=kOutput, calls=%fused_computation.21 | convolution fusion | flops 6460801024 | bytes 14696448 | tf_op jit(solution)/shard_map/dot_general | solution.py:224
  794.5 7.3 collective-permute-done.42.refs_0_
  813.9 8.7 collective-permute-done.41
  826.8 4.7 all-to-all-start.4
  832.9 2.8 shard_map.288.refs_1_
  847.7 7.6 collective-permute-done.31
  858.1 12.7 %all-to-all-done.4 = bf16[8,64,1024]{2,1,0:T(8,128)(2,1)} async-done(((bf16[8,64,1024]{2,1,0:T(8,128)(2,1)}), bf16[8,64,1024]{2,1,0:T(8,128)(2,1)}, u32[]{:S(2)}, u32[]{:S(2)}) %all-to-all-start.4) | async-done | bytes 1048608 | tf_op jit(solution)/shard_map/all_to_all | solution.py:70
  870.7 4.0 all-to-all-start.3
  878.8 2.8 convert_element_type.359.refs_1_
  894.5 2.4 collective-permute-start.38
  897.0 2.9 fusion.18.in_ref
  (491 shorter events, 176.7 us)
Async XLA Ops:
  7.2 140.7 %copy-start = (f32[3,48]{1,0:T(4,128)S(1)}, f32[3,48]{1,0:T(4,128)}, u32[]{:S(2)}) copy-start(f32[3,48]{1,0:T(4,128)} %param.21) | copy-start | bytes 1732
  15.5 49.9 %all-to-all-start = ((bf16[8,64,1792]{2,1,0:T(8,128)(2,1)}), bf16[8,64,1792]{2,1,0:T(8,128)(2,1)S(1)}, u32[]{:S(2)}, u32[]{:S(2)}) async-start(bf16[8,64,1792]{2,1,0:T(8,128)(2,1)} %shard_map.255), calls=%async_computation | async-start | bytes 3670016 | tf_op jit(solution)/shard_map/all_to_all | solution.py:70
  22.0 125.8 %all-gather.5.cloned.1.call-start = ((), (), s32[]{:S(2)}) async-start(), calls=%async_computation.9 | async-start | bytes 9437184 | tf_op jit(solution)/shard_map/all_gather | solution.py:810
  24.4 42.4 %copy-start.88 = (s32[2,1,18]{2,1,0:T(1,128)S(1)}, s32[2,1,18]{2,1,0:T(1,128)}, u32[]{:S(2)}) copy-start(s32[2,1,18]{2,1,0:T(1,128)} %param.16) | copy-start | bytes 436
  66.7 186.8 %all-gather.7.cloned.1.call-start = ((), (), s32[]{:S(2)}) async-start(), calls=%async_computation.10 | async-start | bytes 9437184 | tf_op jit(solution)/shard_map/all_gather | solution.py:810
  67.8 41.9 %collective-permute-start = (bf16[8,64,1792]{2,1,0:T(8,128)(2,1)}, bf16[8,64,1792]{2,1,0:T(8,128)(2,1)}, u32[]{:S(2)}, u32[]{:S(2)}) collective-permute-start(bf16[8,64,1792]{2,1,0:T(8,128)(2,1)} %copy-done.54), channel_id=1, source_target_pairs={{0,1},{1,0},{2,3},{3,2},{4,5},{5,4},{6,7},{7,6},{8,9},{9,8},{10,11... | collective-permute-start | bytes 5505032 | tf_op jit(solution)/shard_map/ppermute | solution.py:42
  69.3 43.2 %collective-permute-start.1 = (bf16[8,64,1792]{2,1,0:T(8,128)(2,1)}, bf16[8,64,1792]{2,1,0:T(8,128)(2,1)}, u32[]{:S(2)}, u32[]{:S(2)}) collective-permute-start(bf16[8,64,1792]{2,1,0:T(8,128)(2,1)} %copy-done.54), channel_id=1, source_target_pairs={{0,2},{1,3},{2,0},{3,1},{4,6},{5,7},{6,4},{7,5},{8,10},{9,11},{10,... | collective-permute-start | bytes 5505032 | tf_op jit(solution)/shard_map/ppermute | solution.py:42
  110.9 21.1 %collective-permute-start.2 = (bf16[4,64,1792]{2,1,0:T(8,128)(2,1)S(1)}, bf16[4,64,1792]{2,1,0:T(8,128)(2,1)S(1)}, u32[]{:S(2)}, u32[]{:S(2)}) collective-permute-start(bf16[4,64,1792]{2,1,0:T(8,128)(2,1)S(1)} %slice.301), channel_id=1, source_target_pairs={{0,2},{1,3},{2,0},{3,1},{4,6},{5,7},{6,4},{7,5},{8,10},{9,11},{10,... | collective-permute-start | bytes 2752520 | tf_op jit(solution)/shard_map/ppermute | solution.py:42
  113.8 20.8 %collective-permute-start.3 = (bf16[4,64,1792]{2,1,0:T(8,128)(2,1)S(1)}, bf16[4,64,1792]{2,1,0:T(8,128)(2,1)S(1)}, u32[]{:S(2)}, u32[]{:S(2)}) collective-permute-start(bf16[4,64,1792]{2,1,0:T(8,128)(2,1)S(1)} %slice.302), channel_id=1, source_target_pairs={{0,1},{1,0},{2,3},{3,2},{4,5},{5,4},{6,7},{7,6},{8,9},{9,8},{10,11... | collective-permute-start | bytes 2752520 | tf_op jit(solution)/shard_map/ppermute | solution.py:42
  148.0 41.9 %copy-start.43 = (f32[8,128]{1,0:T(8,128)}, f32[8,128]{1,0:T(8,128)S(1)}, u32[]{:S(2)}) copy-start(f32[8,128]{1,0:T(8,128)S(1)} %pad.43.head_ref) | copy-start | bytes 12292
  153.4 59.9 %collective-permute-start.10 = (bf16[128,2048]{1,0:T(8,128)(2,1)}, bf16[128,2048]{1,0:T(8,128)(2,1)}, u32[]{:S(2)}, u32[]{:S(2)}) collective-permute-start(bf16[128,2048]{1,0:T(8,128)(2,1)} %shard_map.264.refs_0_), channel_id=1, source_target_pairs={{0,3},{1,2},{2,1},{3,0},{4,7},{5,6},{6,5},{7,4},{8,11},{9,10},{10,... | collective-permute-start | bytes 1572872 | tf_op jit(solution)/shard_map/ppermute | solution.py:42
  155.9 58.2 %collective-permute-start.9 = (bf16[128,2048]{1,0:T(8,128)(2,1)}, bf16[128,2048]{1,0:T(8,128)(2,1)}, u32[]{:S(2)}, u32[]{:S(2)}) collective-permute-start(bf16[128,2048]{1,0:T(8,128)(2,1)} %shard_map.264.refs_0_), channel_id=1, source_target_pairs={{0,2},{1,3},{2,0},{3,1},{4,6},{5,7},{6,4},{7,5},{8,10},{9,11},{10,... | collective-permute-start | bytes 1572872 | tf_op jit(solution)/shard_map/ppermute | solution.py:42
  156.4 57.6 %collective-permute-start.8 = (bf16[128,2048]{1,0:T(8,128)(2,1)}, bf16[128,2048]{1,0:T(8,128)(2,1)}, u32[]{:S(2)}, u32[]{:S(2)}) collective-permute-start(bf16[128,2048]{1,0:T(8,128)(2,1)} %shard_map.264.refs_0_), channel_id=1, source_target_pairs={{0,1},{1,0},{2,3},{3,2},{4,5},{5,4},{6,7},{7,6},{8,9},{9,8},{10,11... | collective-permute-start | bytes 1572872 | tf_op jit(solution)/shard_map/ppermute | solution.py:42
  157.6 65.6 %all-to-all-start.1 = ((bf16[8,64,1024]{2,1,0:T(8,128)(2,1)}), bf16[8,64,1024]{2,1,0:T(8,128)(2,1)}, u32[]{:S(2)}, u32[]{:S(2)}) async-start(bf16[8,64,1024]{2,1,0:T(8,128)(2,1)} %shard_map.260), calls=%async_computation.1 | async-start | bytes 2097152 | tf_op jit(solution)/shard_map/all_to_all | solution.py:70
  161.8 182.0 %reduce-scatter.5.cloned.1.call-start = ((), (), s32[]{:S(2)}) async-start(), calls=%async_computation.11 | async-start | bytes 9437184 | tf_op jit(solution)/shard_map/reduce_scatter | solution.py:813
  212.7 5.1 collective-permute-start.4
  217.9 22.5 %collective-permute-start.5 = (f32[2048]{0:T(1024)S(1)}, f32[2048]{0:T(1024)S(1)}, u32[]{:S(2)}, u32[]{:S(2)}) collective-permute-start(f32[2048]{0:T(1024)S(1)} %add.275), channel_id=1, source_target_pairs={{0,8},{4,12},{8,0},{12,4},{16,24},{20,28},{24,16},{28,20},{1,9},{5... | collective-permute-start | bytes 24584 | tf_op jit(solution)/shard_map/ppermute | solution.py:42
  219.9 20.5 %collective-permute-start.6 = (f32[2048]{0:T(1024)S(1)}, f32[2048]{0:T(1024)S(1)}, u32[]{:S(2)}, u32[]{:S(2)}) collective-permute-start(f32[2048]{0:T(1024)S(1)} %add.275), channel_id=1, source_target_pairs={{0,16},{4,20},{8,24},{12,28},{16,0},{20,4},{24,8},{28,12},{1,17},{... | collective-permute-start | bytes 24584 | tf_op jit(solution)/shard_map/ppermute | solution.py:42
  222.2 18.2 %collective-permute-start.7 = (f32[2048]{0:T(1024)S(1)}, f32[2048]{0:T(1024)S(1)}, u32[]{:S(2)}, u32[]{:S(2)}) collective-permute-start(f32[2048]{0:T(1024)S(1)} %add.275), channel_id=1, source_target_pairs={{0,24},{4,28},{8,16},{12,20},{16,8},{20,12},{24,0},{28,4},{1,25},{... | collective-permute-start | bytes 24584 | tf_op jit(solution)/shard_map/ppermute | solution.py:42
  253.5 175.4 %all-gather.9.cloned.1.call-start = ((), (), s32[]{:S(2)}) async-start(), calls=%async_computation.12 | async-start | bytes 9437184 | tf_op jit(solution)/shard_map/all_gather | solution.py:810
  255.6 291.0 %copy-start.71 = (f32[2048]{0:T(1024)}, f32[2048]{0:T(1024)S(1)}, u32[]{:S(2)}) copy-start(f32[2048]{0:T(1024)S(1)} %mul.308) | copy-start | bytes 24580
  255.6 15.1 %collective-permute-start.14 = (bf16[128,2048]{1,0:T(8,128)(2,1)}, bf16[128,2048]{1,0:T(8,128)(2,1)}, u32[]{:S(2)}, u32[]{:S(2)}) collective-permute-start(bf16[128,2048]{1,0:T(8,128)(2,1)} %shard_map.274), channel_id=1, source_target_pairs={{0,1},{1,0},{2,3},{3,2},{4,5},{5,4},{6,7},{7,6},{8,9},{9,8},{10,11... | collective-permute-start | bytes 1572872 | tf_op jit(solution)/shard_map/ppermute | solution.py:42
  257.1 26.3 %collective-permute-start.15 = (bf16[128,2048]{1,0:T(8,128)(2,1)}, bf16[128,2048]{1,0:T(8,128)(2,1)}, u32[]{:S(2)}, u32[]{:S(2)}) collective-permute-start(bf16[128,2048]{1,0:T(8,128)(2,1)} %shard_map.274), channel_id=1, source_target_pairs={{0,2},{1,3},{2,0},{3,1},{4,6},{5,7},{6,4},{7,5},{8,10},{9,11},{10,... | collective-permute-start | bytes 1572872 | tf_op jit(solution)/shard_map/ppermute | solution.py:42
  258.6 26.0 %collective-permute-start.16 = (bf16[128,2048]{1,0:T(8,128)(2,1)}, bf16[128,2048]{1,0:T(8,128)(2,1)S(1)}, u32[]{:S(2)}, u32[]{:S(2)}) collective-permute-start(bf16[128,2048]{1,0:T(8,128)(2,1)} %shard_map.274), channel_id=1, source_target_pairs={{0,3},{1,2},{2,1},{3,0},{4,7},{5,6},{6,5},{7,4},{8,11},{9,10},{10,... | collective-permute-start | bytes 1572872 | tf_op jit(solution)/shard_map/ppermute | solution.py:42
  259.1 45.2 %collective-permute-start.11 = (bf16[8,64,1024]{2,1,0:T(8,128)(2,1)}, bf16[8,64,1024]{2,1,0:T(8,128)(2,1)S(1)}, u32[]{:S(2)}, u32[]{:S(2)}) collective-permute-start(bf16[8,64,1024]{2,1,0:T(8,128)(2,1)} %shard_map.272), channel_id=1, source_target_pairs={{0,1},{1,0},{2,3},{3,2},{4,5},{5,4},{6,7},{7,6},{8,9},{9,8},{10,11... | collective-permute-start | bytes 3145736 | tf_op jit(solution)/shard_map/ppermute | solution.py:42
  260.6 66.7 %collective-permute-start.12 = (bf16[8,64,1024]{2,1,0:T(8,128)(2,1)}, bf16[8,64,1024]{2,1,0:T(8,128)(2,1)S(1)}, u32[]{:S(2)}, u32[]{:S(2)}) collective-permute-start(bf16[8,64,1024]{2,1,0:T(8,128)(2,1)} %shard_map.272), channel_id=1, source_target_pairs={{0,2},{1,3},{2,0},{3,1},{4,6},{5,7},{6,4},{7,5},{8,10},{9,11},{10,... | collective-permute-start | bytes 3145736 | tf_op jit(solution)/shard_map/ppermute | solution.py:42
  270.7 57.7 %collective-permute-start.13 = (bf16[8,64,1024]{2,1,0:T(8,128)(2,1)}, bf16[8,64,1024]{2,1,0:T(8,128)(2,1)S(1)}, u32[]{:S(2)}, u32[]{:S(2)}) collective-permute-start(bf16[8,64,1024]{2,1,0:T(8,128)(2,1)} %shard_map.272), channel_id=1, source_target_pairs={{0,3},{1,2},{2,1},{3,0},{4,7},{5,6},{6,5},{7,4},{8,11},{9,10},{10,... | collective-permute-start | bytes 3145736 | tf_op jit(solution)/shard_map/ppermute | solution.py:42
  284.6 43.8 %copy-start.60 = (bf16[4,128,2048]{2,1,0:T(8,128)(2,1)}, bf16[4,128,2048]{2,1,0:T(8,128)(2,1)S(1)}, u32[]{:S(2)}) copy-start(bf16[4,128,2048]{2,1,0:T(8,128)(2,1)S(1)} %bitcast_dynamic-update-slice_fusion.7) | copy-start | bytes 6291460
  346.8 199.8 %copy-start.77 = (f32[256]{0:T(256)}, f32[256]{0:T(256)S(1)}, u32[]{:S(2)}) copy-start(f32[256]{0:T(256)S(1)} %get-tuple-element.160) | copy-start | bytes 3076
  346.8 199.8 %copy-start.80 = (f32[256]{0:T(256)}, f32[256]{0:T(256)S(1)}, u32[]{:S(2)}) copy-start(f32[256]{0:T(256)S(1)} %get-tuple-element.159) | copy-start | bytes 3076
  348.3 195.3 %reduce-scatter.7.cloned.1.call-start = ((), (), s32[]{:S(2)}) async-start(), calls=%async_computation.13 | async-start | bytes 9437184 | tf_op jit(solution)/shard_map/reduce_scatter | solution.py:813
  455.3 173.7 %all-gather.11.cloned.1.call-start = ((), (), s32[]{:S(2)}) async-start(), calls=%async_computation.14 | async-start | bytes 9437184 | tf_op jit(solution)/shard_map/all_gather | solution.py:810
  548.5 208.2 %reduce-scatter.9.cloned.1.call-start = ((), (), s32[]{:S(2)}) async-start(), calls=%async_computation.15 | async-start | bytes 9437184 | tf_op jit(solution)/shard_map/reduce_scatter | solution.py:813
  550.0 14.9 %collective-permute-start.20 = (bf16[128,2048]{1,0:T(8,128)(2,1)S(1)}, bf16[128,2048]{1,0:T(8,128)(2,1)S(1)}, u32[]{:S(2)}, u32[]{:S(2)}) collective-permute-start(bf16[128,2048]{1,0:T(8,128)(2,1)S(1)} %get-tuple-element.147), channel_id=1, source_target_pairs={{0,1},{1,0},{2,3},{3,2},{4,5},{5,4},{6,7},{7,6},{8,9},{9,8},{10,11... | collective-permute-start | bytes 1572872 | tf_op jit(solution)/shard_map/ppermute | solution.py:42
  551.6 26.1 %collective-permute-start.21 = (bf16[128,2048]{1,0:T(8,128)(2,1)S(1)}, bf16[128,2048]{1,0:T(8,128)(2,1)S(1)}, u32[]{:S(2)}, u32[]{:S(2)}) collective-permute-start(bf16[128,2048]{1,0:T(8,128)(2,1)S(1)} %get-tuple-element.149), channel_id=1, source_target_pairs={{0,2},{1,3},{2,0},{3,1},{4,6},{5,7},{6,4},{7,5},{8,10},{9,11},{10,... | collective-permute-start | bytes 1572872 | tf_op jit(solution)/shard_map/ppermute | solution.py:42
  553.0 24.6 %collective-permute-start.22 = (bf16[128,2048]{1,0:T(8,128)(2,1)S(1)}, bf16[128,2048]{1,0:T(8,128)(2,1)S(1)}, u32[]{:S(2)}, u32[]{:S(2)}) collective-permute-start(bf16[128,2048]{1,0:T(8,128)(2,1)S(1)} %get-tuple-element.148), channel_id=1, source_target_pairs={{0,3},{1,2},{2,1},{3,0},{4,7},{5,6},{6,5},{7,4},{8,11},{9,10},{10,... | collective-permute-start | bytes 1572872 | tf_op jit(solution)/shard_map/ppermute | solution.py:42
  556.3 42.5 %collective-permute-start.17 = (bf16[512,1024]{1,0:T(8,128)(2,1)S(1)}, bf16[512,1024]{1,0:T(8,128)(2,1)S(1)}, u32[]{:S(2)}, u32[]{:S(2)}) collective-permute-start(bf16[512,1024]{1,0:T(8,128)(2,1)S(1)} %get-tuple-element.133), channel_id=1, source_target_pairs={{0,1},{1,0},{2,3},{3,2},{4,5},{5,4},{6,7},{7,6},{8,9},{9,8},{10,11... | collective-permute-start | bytes 3145736 | tf_op jit(solution)/shard_map/ppermute | solution.py:42
  557.8 61.2 %collective-permute-start.18 = (bf16[512,1024]{1,0:T(8,128)(2,1)S(1)}, bf16[512,1024]{1,0:T(8,128)(2,1)S(1)}, u32[]{:S(2)}, u32[]{:S(2)}) collective-permute-start(bf16[512,1024]{1,0:T(8,128)(2,1)S(1)} %get-tuple-element.135), channel_id=1, source_target_pairs={{0,2},{1,3},{2,0},{3,1},{4,6},{5,7},{6,4},{7,5},{8,10},{9,11},{10,... | collective-permute-start | bytes 3145736 | tf_op jit(solution)/shard_map/ppermute | solution.py:42
  565.0 54.0 %collective-permute-start.19 = (bf16[512,1024]{1,0:T(8,128)(2,1)S(1)}, bf16[512,1024]{1,0:T(8,128)(2,1)S(1)}, u32[]{:S(2)}, u32[]{:S(2)}) collective-permute-start(bf16[512,1024]{1,0:T(8,128)(2,1)S(1)} %get-tuple-element.134), channel_id=1, source_target_pairs={{0,3},{1,2},{2,1},{3,0},{4,7},{5,6},{6,5},{7,4},{8,11},{9,10},{10,... | collective-permute-start | bytes 3145736 | tf_op jit(solution)/shard_map/ppermute | solution.py:42
  629.1 106.1 %all-to-all-start.2 = ((bf16[8,64,1024]{2,1,0:T(8,128)(2,1)}), bf16[8,64,1024]{2,1,0:T(8,128)(2,1)}, u32[]{:S(2)}, u32[]{:S(2)}) async-start(bf16[8,64,1024]{2,1,0:T(8,128)(2,1)} %bitcast.68), calls=%async_computation.5 | async-start | bytes 2097152 | tf_op jit(solution)/shard_map/all_to_all | solution.py:70
  633.5 245.3 %reduce-scatter.11.cloned.1.call-start = ((), (), s32[]{:S(2)}) async-start(), calls=%async_computation.16 | async-start | bytes 9437184 | tf_op jit(solution)/shard_map/reduce_scatter | solution.py:813
  652.5 5.6 collective-permute-start.23
  655.1 77.7 %collective-permute-start.27 = (bf16[128,2048]{1,0:T(8,128)(2,1)}, bf16[128,2048]{1,0:T(8,128)(2,1)}, u32[]{:S(2)}, u32[]{:S(2)}) collective-permute-start(bf16[128,2048]{1,0:T(8,128)(2,1)} %get-tuple-element.144), channel_id=1, source_target_pairs={{0,1},{1,0},{2,3},{3,2},{4,5},{5,4},{6,7},{7,6},{8,9},{9,8},{10,11... | collective-permute-start | bytes 1572872 | tf_op jit(solution)/shard_map/ppermute | solution.py:42
  656.6 76.2 %collective-permute-start.28 = (bf16[128,2048]{1,0:T(8,128)(2,1)}, bf16[128,2048]{1,0:T(8,128)(2,1)}, u32[]{:S(2)}, u32[]{:S(2)}) collective-permute-start(bf16[128,2048]{1,0:T(8,128)(2,1)} %get-tuple-element.145), channel_id=1, source_target_pairs={{0,2},{1,3},{2,0},{3,1},{4,6},{5,7},{6,4},{7,5},{8,10},{9,11},{10,... | collective-permute-start | bytes 1572872 | tf_op jit(solution)/shard_map/ppermute | solution.py:42
  658.6 27.4 %collective-permute-start.24 = (f32[2048]{0:T(1024)}, f32[2048]{0:T(1024)S(1)}, u32[]{:S(2)}, u32[]{:S(2)}) collective-permute-start(f32[2048]{0:T(1024)} %add.291.refs_1_), channel_id=1, source_target_pairs={{0,8},{4,12},{8,0},{12,4},{16,24},{20,28},{24,16},{28,20},{1,9},{5... | collective-permute-start | bytes 24584 | tf_op jit(solution)/shard_map/ppermute | solution.py:42
  660.3 27.1 %collective-permute-start.25 = (f32[2048]{0:T(1024)}, f32[2048]{0:T(1024)S(1)}, u32[]{:S(2)}, u32[]{:S(2)}) collective-permute-start(f32[2048]{0:T(1024)} %add.291.refs_1_), channel_id=1, source_target_pairs={{0,16},{4,20},{8,24},{12,28},{16,0},{20,4},{24,8},{28,12},{1,17},{... | collective-permute-start | bytes 24584 | tf_op jit(solution)/shard_map/ppermute | solution.py:42
  662.7 24.7 %collective-permute-start.26 = (f32[2048]{0:T(1024)}, f32[2048]{0:T(1024)S(1)}, u32[]{:S(2)}, u32[]{:S(2)}) collective-permute-start(f32[2048]{0:T(1024)} %add.291.refs_1_), channel_id=1, source_target_pairs={{0,24},{4,28},{8,16},{12,20},{16,8},{20,12},{24,0},{28,4},{1,25},{... | collective-permute-start | bytes 24584 | tf_op jit(solution)/shard_map/ppermute | solution.py:42
  686.8 45.9 %collective-permute-start.29 = (bf16[128,2048]{1,0:T(8,128)(2,1)S(1)}, bf16[128,2048]{1,0:T(8,128)(2,1)S(1)}, u32[]{:S(2)}, u32[]{:S(2)}) collective-permute-start(bf16[128,2048]{1,0:T(8,128)(2,1)S(1)} %copy-done.69), channel_id=1, source_target_pairs={{0,3},{1,2},{2,1},{3,0},{4,7},{5,6},{6,5},{7,4},{8,11},{9,10},{10,... | collective-permute-start | bytes 1572872 | tf_op jit(solution)/shard_map/ppermute | solution.py:42
  778.1 23.7 %collective-permute-start.42 = (bf16[2,256,1024]{2,1,0:T(8,128)(2,1)S(1)}, bf16[2,256,1024]{2,1,0:T(8,128)(2,1)S(1)}, u32[]{:S(2)}, u32[]{:S(2)}) collective-permute-start(bf16[2,256,1024]{2,1,0:T(8,128)(2,1)S(1)} %pad_maximum_fusion.6), channel_id=1, source_target_pairs={{0,2},{1,3},{2,0},{3,1},{4,6},{5,7},{6,4},{7,5},{8,10},{9,11},{10,... | collective-permute-start | bytes 3145736 | tf_op jit(solution)/shard_map/ppermute | solution.py:42
  780.8 23.7 %collective-permute-start.40 = (bf16[2,256,1024]{2,1,0:T(8,128)(2,1)}, bf16[2,256,1024]{2,1,0:T(8,128)(2,1)}, u32[]{:S(2)}, u32[]{:S(2)}) collective-permute-start(bf16[2,256,1024]{2,1,0:T(8,128)(2,1)} %pad_maximum_fusion.5), channel_id=1, source_target_pairs={{0,1},{1,0},{2,3},{3,2},{4,5},{5,4},{6,7},{7,6},{8,9},{9,8},{10,11... | collective-permute-start | bytes 3145736 | tf_op jit(solution)/shard_map/ppermute | solution.py:42
  807.7 14.9 %collective-permute-start.41 = (bf16[256,1024]{1,0:T(8,128)(2,1)S(1)}, bf16[256,1024]{1,0:T(8,128)(2,1)S(1)}, u32[]{:S(2)}, u32[]{:S(2)}) collective-permute-start(bf16[256,1024]{1,0:T(8,128)(2,1)S(1)} %get-tuple-element.127), channel_id=1, source_target_pairs={{0,2},{1,3},{2,0},{3,1},{4,6},{5,7},{6,4},{7,5},{8,10},{9,11},{10,... | collective-permute-start | bytes 1572872 | tf_op jit(solution)/shard_map/ppermute | solution.py:42
  809.2 14.9 %collective-permute-start.43 = (bf16[256,1024]{1,0:T(8,128)(2,1)S(1)}, bf16[256,1024]{1,0:T(8,128)(2,1)S(1)}, u32[]{:S(2)}, u32[]{:S(2)}) collective-permute-start(bf16[256,1024]{1,0:T(8,128)(2,1)S(1)} %get-tuple-element.128), channel_id=1, source_target_pairs={{0,1},{1,0},{2,3},{3,2},{4,5},{5,4},{6,7},{7,6},{8,9},{9,8},{10,11... | collective-permute-start | bytes 1572872 | tf_op jit(solution)/shard_map/ppermute | solution.py:42
  811.7 27.0 %collective-permute-start.32 = (bf16[2,256,768]{2,1,0:T(8,128)(2,1)}, bf16[2,256,768]{2,1,0:T(8,128)(2,1)}, u32[]{:S(2)}, u32[]{:S(2)}) collective-permute-start(bf16[2,256,768]{2,1,0:T(8,128)(2,1)} %pad_maximum_fusion.9), channel_id=1, source_target_pairs={{0,2},{1,3},{2,0},{3,1},{4,6},{5,7},{6,4},{7,5},{8,10},{9,11},{10,... | collective-permute-start | bytes 2359304 | tf_op jit(solution)/shard_map/ppermute | solution.py:42
  813.3 26.6 %collective-permute-start.30 = (bf16[2,256,768]{2,1,0:T(8,128)(2,1)}, bf16[2,256,768]{2,1,0:T(8,128)(2,1)S(1)}, u32[]{:S(2)}, u32[]{:S(2)}) collective-permute-start(bf16[2,256,768]{2,1,0:T(8,128)(2,1)} %pad_maximum_fusion.8), channel_id=1, source_target_pairs={{0,1},{1,0},{2,3},{3,2},{4,5},{5,4},{6,7},{7,6},{8,9},{9,8},{10,11... | collective-permute-start | bytes 2359304 | tf_op jit(solution)/shard_map/ppermute | solution.py:42
  826.8 43.9 %all-to-all-start.4 = ((bf16[8,64,1024]{2,1,0:T(8,128)(2,1)}), bf16[8,64,1024]{2,1,0:T(8,128)(2,1)}, u32[]{:S(2)}, u32[]{:S(2)}) async-start(bf16[8,64,1024]{2,1,0:T(8,128)(2,1)} %bitcast.93), calls=%async_computation.8 | async-start | bytes 2097152 | tf_op jit(solution)/shard_map/all_to_all | solution.py:70
  843.6 11.7 %collective-permute-start.31 = (bf16[256,768]{1,0:T(8,128)(2,1)S(1)}, bf16[256,768]{1,0:T(8,128)(2,1)S(1)}, u32[]{:S(2)}, u32[]{:S(2)}) collective-permute-start(bf16[256,768]{1,0:T(8,128)(2,1)S(1)} %get-tuple-element.138), channel_id=1, source_target_pairs={{0,2},{1,3},{2,0},{3,1},{4,6},{5,7},{6,4},{7,5},{8,10},{9,11},{10,... | collective-permute-start | bytes 1179656 | tf_op jit(solution)/shard_map/ppermute | solution.py:42
  844.4 11.3 %collective-permute-start.33 = (bf16[256,768]{1,0:T(8,128)(2,1)S(1)}, bf16[256,768]{1,0:T(8,128)(2,1)S(1)}, u32[]{:S(2)}, u32[]{:S(2)}) collective-permute-start(bf16[256,768]{1,0:T(8,128)(2,1)S(1)} %get-tuple-element.139), channel_id=1, source_target_pairs={{0,1},{1,0},{2,3},{3,2},{4,5},{5,4},{6,7},{7,6},{8,9},{9,8},{10,11... | collective-permute-start | bytes 1179656 | tf_op jit(solution)/shard_map/ppermute | solution.py:42
  870.7 32.8 %all-to-all-start.3 = ((bf16[8,64,768]{2,1,0:T(8,128)(2,1)}), bf16[8,64,768]{2,1,0:T(8,128)(2,1)S(1)}, u32[]{:S(2)}, u32[]{:S(2)}) async-start(bf16[8,64,768]{2,1,0:T(8,128)(2,1)} %bitcast.81), calls=%async_computation.7 | async-start | bytes 1572864 | tf_op jit(solution)/shard_map/all_to_all | solution.py:70
  881.6 5.4 collective-permute-start.34
  887.8 3.6 collective-permute-start.35
  891.4 1.1 collective-permute-start.36
  892.5 9.3 %collective-permute-start.37 = (f32[144]{0:T(256)S(1)}, f32[144]{0:T(256)S(1)}, u32[]{:S(2)}, u32[]{:S(2)}) collective-permute-start(f32[144]{0:T(256)S(1)} %add.311), channel_id=1, source_target_pairs={{0,8},{4,12},{8,0},{12,4},{16,24},{20,28},{24,16},{28,20},{1,9},{5... | collective-permute-start | bytes 1736 | tf_op jit(solution)/shard_map/ppermute | solution.py:42
  894.5 7.3 collective-permute-start.38
  896.9 5.4 collective-permute-start.39
  (83 other events, 504.2 us)
Sparse Core Ops, SparseCore 0:
  66.8 80.9 all-gather.4
  150.0 103.4 all-gather.6
  255.8 87.9 reduce-scatter.4
  348.5 80.4 all-gather.8
  455.5 88.1 reduce-scatter.6
  548.6 80.3 all-gather.10
  631.4 104.4 reduce-scatter.8
  759.6 102.9 reduce-scatter.10

commit v3 on v2

--- a/solution.py
+++ b/solution.py
@@ -840,28 +840,30 @@
     sizes = [width, width, 2 * STATE, DT_PAD, ATT_DIM, ATT_DIM, ATT_DIM]
     starts = [sum(sizes[:k]) for k in range(len(sizes) + 1)]
     every = slice(None)
+    sent_sizes = [width, width, STATE, DT_PAD, ATT_DIM, ATT_DIM]
+    sent_at = [sum(sent_sizes[:k]) for k in range(len(sent_sizes) + 1)]
     moves = []
     for k in range(n):
+        odd = k % 2
         for which, source, target, wide in (
-            (0, k * inner, starts[0], inner),
-            (0, INNER + k * inner, starts[1], inner),
-            (0, 2 * INNER, starts[2], 2 * STATE),
-            (1, q_of[k] * ATT_DIM, starts[4], ATT_DIM),
-            (1, kv_of[k] * ATT_DIM, starts[5], ATT_DIM),
-            (1, (kv_of[k] + KV_HEADS) * ATT_DIM, starts[6], ATT_DIM),
+            (0, k * inner, sent_at[0], inner),
+            (0, INNER + k * inner, sent_at[1], inner),
+            (0, 2 * INNER + odd * STATE, sent_at[2], STATE),
+            (1, q_of[k] * ATT_DIM, sent_at[4], ATT_DIM),
+            (1, (kv_of[k] + odd * KV_HEADS) * ATT_DIM, sent_at[5], ATT_DIM),
         ):
             moves.append(
                 (which, (every, slice(source, source + wide)), (k, every, slice(target, target + wide)))
             )
-        moves.append((2, (k,), (k, every, slice(starts[3], starts[4]))))
+        moves.append((2, (k,), (k, every, slice(sent_at[3], sent_at[4]))))
         if width != inner:
             gap = slice(0, width - inner)
-            for target in (starts[1], starts[2]):
+            for target in (sent_at[1], sent_at[2]):
                 hole = slice(target - width + inner, target)
                 moves.append((3, (every, gap), (k, every, hole)))
     blank = jnp.zeros((owner, 128), bf16)
     packed = assembled(
-        (n, owner, starts[-1]), bf16, moves, mixer_in, attn_qkv, steps_own, blank
+        (n, owner, sent_at[-1]), bf16, moves, mixer_in, attn_qkv, steps_own, blank
     )
     sent_in = exchanged(packed, "seq")
     positions = jnp.arange(length, dtype=jnp.int32)
@@ -906,10 +908,30 @@
     )
     q_aux = jnp.pad(from_seq(q_aux), ((0, 0), (0, 6))).reshape(n, own, 8)
     q_aux, q_table = taken(q_aux), taken(table)
-    w_in = after(dp_gather(sent_in), aux, seg_blocks, table, q_aux)
-    small = w_in[:, :, :, starts[3] + heads : starts[3] + heads + small_cols]
+    w_half = dp_gather(sent_in)
+    small = w_half[:, :, :, sent_at[3] + heads : sent_at[3] + heads + small_cols]
     small = jnp.swapaxes(small, 0, 1).reshape(n * nd, -1)[:, :small_count]
-    w_in = w_in.reshape(D, starts[-1])
+    w_half = w_half.reshape(D, sent_at[-1])
+    w_cut = [w_half[:, sent_at[k] : sent_at[k + 1]] for k in range(6)]
+    own_side = jnp.concatenate([w_cut[2], w_cut[5]], axis=1)
+    other_side = permuted(own_side, "seq", 1)
+    odd_place = (s & 1) != 0
+    first_side = jnp.where(odd_place, other_side, own_side)
+    second_side = jnp.where(odd_place, own_side, other_side)
+    w_in = jnp.concatenate(
+        [
+            w_cut[0],
+            w_cut[1],
+            first_side[:, :STATE],
+            second_side[:, :STATE],
+            w_cut[3],
+            w_cut[4],
+            first_side[:, STATE:],
+            second_side[:, STATE:],
+        ],
+        axis=1,
+    )
+    w_in = after(w_in, aux, seg_blocks, table, q_aux)
     gu_moves = []
     for k in range(n):
         for half in range(2):
@@ -1013,8 +1035,8 @@
     gu_sum = to_owners(gu_part)
 
     ffn_out = after(dot(activated_b, w_down).astype(bf16), hidden_b)
-    ffn_sum = scattered(ffn_out)
-    layer_out = plain_order((hidden + ffn_sum).astype(bf16))
+    ffn_sum = lax.psum_scatter(ffn_out, "seq", scatter_dimension=0, tiled=True)
+    layer_out = plain_order((hidden + ffn_sum.astype(f32)).astype(bf16))
 
     branch_total = cross(branch_b, hidden_b).astype(bf16)
     mix_total, att_total = branch_total[:width], branch_total[width:]
@@ -1027,7 +1049,15 @@
     out_total = jnp.concatenate(
         [mix_total[:inner].reshape(nd, -1, D), att_total.reshape(nd, -1, D)], axis=1
     )
-    out_sum = dp_scatter(out_total, False)
+    if nd == 4:
+        out_blocks = [lax.dynamic_index_in_dim(out_total, d ^ k, 0, False) for k in range(nd)]
+        out_pieces = [permuted(out_blocks[k], "dp", k) for k in range(1, nd)]
+        out_sum = out_blocks[0].astype(f32)
+        for piece in out_pieces:
+            out_sum = out_sum + piece.astype(f32)
+    else:
+        out_sum = dp_scatter(out_total, False)
+        out_pieces = [out_sum]
 
     branch_grad = dot_t(hidden_b, w_out)
     mix_grad = branch_grad[:, :width]
@@ -1045,7 +1075,7 @@
     mixed_grad, conv_g, head_g, skip_g = ssd_backward(
         *ssd_args, y, enter, gated_grad, qkv_grad, n, micro
     )
-    mixed_grad = after(mixed_grad, out_sum, gu_sum)
+    mixed_grad = after(mixed_grad, gu_sum, *out_pieces)
 
     def placed(value, full):
         whole = jnp.zeros(value.shape[:-1] + (full,), f32)
@@ -1090,13 +1120,15 @@
     mixer_out_grad = out_plain[: mixer_out.shape[0]]
     attn_out_grad = out_plain[mixer_out.shape[0] :]
     down_grad = plain_order(down_grad)
-    normed_grad = scattered(
-        in_back, gate_up_grad, mixer_out_grad, attn_out_grad, down_grad, layer_out
-    )
+    normed_sum = lax.psum_scatter(in_back, "seq", scatter_dimension=0, tiled=True)
+    normed_sum = after(
+        normed_sum, gate_up_grad, mixer_out_grad, attn_out_grad, down_grad, layer_out
+    )
+    normed_grad = normed_sum.astype(f32)
     head_g = jnp.concatenate(
         [head_g[:2, :heads], skip_g[:1, :inner].reshape(1, heads, HEAD_DIM).sum(axis=2)]
     )
-    head_g = after(placed(head_g, HEADS).reshape(-1), normed_grad)
+    head_g = after(placed(head_g, HEADS).reshape(-1), normed_sum)
     head_g = summed(head_g, ("dp",))
     head_g = head_g + permuted(head_g, "seq", 1)
     others = [head_g] + [permuted(head_g, "seq", by) for by in range(2, n, 2)]

time: 926 us -> 913 us (0.986)
  waiting for transfers between devices: 386 us -> 367 us
    all_to_all x5, waiting for transfers between devices: 53.7 us -> 37.4 us  [exchanged(): return lax.all_to_all(blocks, axis, 0, 0, tiled=True)]
    unnamed x188 -> x195, local copies, waits for them, and re-layouts: 37.8 us -> 51.2 us
    ppermute x44 -> x45, waiting for transfers between devices: 169 us -> 173 us  [permuted(): return lax.ppermute(value, axis, pairs)]
    ppermute x44 -> x45, starting transfers between devices: 57.3 us -> 58.3 us  [permuted(): return lax.ppermute(value, axis, pairs)]
    reduce_scatter x4 -> x2, waiting for transfers between devices: 79.1 us -> 79.1 us  [scattered(): lax.psum_scatter(value.astype(bf16), 'seq', scatter_dimension=0, tiled=True)]
  transfers between devices with their start and end apart: 57 -> 58, of which waited for: 28 -> 28; matrix products, arithmetic and copies ran while one was open for 27% -> 27% of each run, Pallas kernels for 11% -> 12%
where the time goes in v3:
time: 913 us; the launch traced here: 903 us
  waiting for transfers between devices  367 us (40%)
  matrix products  137 us (15%)
  Pallas kernels  132 us (14%)
  local copies, waits for them, and re-layouts  99.1 us (11%)
  starting transfers between devices  83 us (9%)
  other arithmetic  67.5 us (7%)
  between operations  16.2 us (2%)
    ppermute x45, waiting for transfers between devices, permuted(): return lax.ppermute(value, axis, pairs)  173 us
    reduce_scatter x2, waiting for transfers between devices, scattered(): lax.psum_scatter(value.astype(bf16), 'seq', scatter_dimension=0, tiled=True)  79.1 us
    all_gather x4, waiting for transfers between devices, gathered(): return lax.all_gather(value, 'seq', axis=0, tiled=True)  77.8 us
    dot_general x5, matrix products, cross(): lax.dot_general(left, right, (((0,), (0,)), ((), ())), preferred_element_...  58.9 us
    ppermute x45, starting transfers between devices, permuted(): return lax.ppermute(value, axis, pairs)  58.3 us
    unnamed x195, local copies, waits for them, and re-layouts  51.2 us
    pallas_call x1, Pallas kernels, ssd_backward(): pl.pallas_call(ssd_backward_kernel, grid=(micro, n), out_shape=(jax.Shape...  41.3 us
    dot_general x3, matrix products, dot_t(): lax.dot_general(left, right, (((1,), (1,)), ((), ())), preferred_element_...  41.3 us
  transfers between devices with their start and end apart: 58, of which 28 were waited for; matrix products, arithmetic and copies ran while one was open for 27% of the time, Pallas kernels for 12%

profile of v3, /device:TPU:0, one launch (start us, length us, event | category | flops | bytes accessed | tf_op | source)
XLA Modules:
  0.0 902.5 jit_solution(14524092799576097676)
XLA Ops:
  9.0 2.8 concatenate.98
  15.4 6.3 all-to-all-start
  24.1 32.6 %all-to-all-done.refs_1_ = bf16[8,64,1408]{2,1,0:T(8,128)(2,1)S(1)} async-done(((bf16[8,64,1408]{2,1,0:T(8,128)(2,1)}), bf16[8,64,1408]{2,1,0:T(8,128)(2,1)S(1)}, u32[]{:S(2)}, u32[]{:S(2)}) %all-to-all-start) | async-done | bytes 1441824 | tf_op jit(solution)/shard_map/all_to_all | solution.py:70
  63.1 29.1 %collective-permute-done = bf16[8,64,1408]{2,1,0:T(8,128)(2,1)S(1)} collective-permute-done((bf16[8,64,1408]{2,1,0:T(8,128)(2,1)}, bf16[8,64,1408]{2,1,0:T(8,128)(2,1)S(1)}, u32[]{:S(2)}, u32[]{:S(2)}) %collective-permute-start) | collective-permute-done | bytes 1441824 | tf_op jit(solution)/shard_map/ppermute | solution.py:42
  95.9 13.3 %collective-permute-done.2 = bf16[4,64,1408]{2,1,0:T(8,128)(2,1)S(1)} collective-permute-done((bf16[4,64,1408]{2,1,0:T(8,128)(2,1)S(1)}, bf16[4,64,1408]{2,1,0:T(8,128)(2,1)S(1)}, u32[]{:S(2)}, u32[]{:S(2)}) %collective-permute-start.2) | collective-permute-done | bytes 720928 | tf_op jit(solution)/shard_map/ppermute | solution.py:42
  127.3 2.1 broadcast_select_fusion
  134.5 4.5 all-gather.5.cloned.1.call-done.refs_1_
  144.3 2.5 collective-permute-start.11
  147.8 4.3 all-to-all-start.1
  152.3 5.1 fusion
  158.1 21.9 %fusion.78.mixed_ref.before_ref.refs_1_ = f32[2048,1792]{1,0:T(8,128)} fusion(bf16[2048,1792]{1,0:T(8,128)(2,1)} %shard_map.257.refs_1_.refs_2_, bf16[2048,2048]{1,0:T(8,128)(2,1)} %all-gather.5.cloned.1.call-done.refs_1_, f32[2048]{0:T(1024)S(1)} %mul.290, f32[2048]{0:T(1024)S(1)} %add_rsqrt_fusion.1), kind=kOutput, calls=%fused_computation.250 | convolution fusion | flops 15049162752 | bytes 30425088 | tf_op jit(solution)/shard_map/dot_general | solution.py:216
  180.1 19.0 %shard_map.258 = (f32[2048,384]{1,0:T(8,128)S(1)}, f32[2048,384]{1,0:T(8,128)S(1)}, bf16[16,256,384]{2,1,0:T(8,128)(2,1)S(1)}) custom-call(f32[2048,1792]{1,0:T(8,128)} %fusion.78.mixed_ref.before_ref.refs_1_, f32[2048,1792]{1,0:T(8,128)} %fusion.78.mixed_ref.before_ref.refs_1_, f32[2048,8]{1,0:T(8,128)S(1)} %bitcast.245, f32[16,1,128]{2,1,0:T(1,128)S(1)} %bitcast.254, ...), custom_call_target="tpu_custom_call" | custom-call | bytes 72000000 | tf_op jit(solution)/shard_map/pallas_call | solution.py:512
  209.9 2.3 collective-permute-start.7
  215.7 14.7 %shard_map.262 = bf16[8,256,128]{2,1,0:T(8,128)(2,1)S(1)} custom-call(f32[8,256,1792]{2,1,0:T(8,128)} %bitcast.256, f32[8,256,1792]{2,1,0:T(8,128)} %bitcast.257, f32[8,256,1792]{2,1,0:T(8,128)} %bitcast.258, f32[8,128,256]{2,1,0:T(8,128)S(1)} %copy-done.8, f32[8,128,256]{2,1,0:T(8,128)S(1)} %copy-done.8, f32[8,256,8]{2,1,0:T(8,128)S(1)} %copy-done.10, ...), custom_call_target="tpu_custom_call" | custom-call | bytes 50400000 | tf_op jit(solution)/shard_map/pallas_call | solution.py:686
  232.7 8.3 convolution_convert_fusion.2.refs_0_
  241.0 3.7 all-gather.7.cloned.1.call-done.refs_1_
  253.5 2.5 broadcast_in_dim.111
  256.1 2.3 bitcast_dynamic-update-slice_fusion.6
  258.4 3.5 collective-permute-done.15
  261.9 2.4 collective-permute-start.14
  265.3 9.3 %collective-permute-done.16 = bf16[128,2048]{1,0:T(8,128)(2,1)} collective-permute-done((bf16[128,2048]{1,0:T(8,128)(2,1)}, bf16[128,2048]{1,0:T(8,128)(2,1)}, u32[]{:S(2)}, u32[]{:S(2)}) %collective-permute-start.16) | collective-permute-done | bytes 524320 | tf_op jit(solution)/shard_map/ppermute | solution.py:42
  276.8 18.7 %collective-permute-done.12 = bf16[8,64,1024]{2,1,0:T(8,128)(2,1)S(1)} collective-permute-done((bf16[8,64,1024]{2,1,0:T(8,128)(2,1)}, bf16[8,64,1024]{2,1,0:T(8,128)(2,1)S(1)}, u32[]{:S(2)}, u32[]{:S(2)}) %collective-permute-start.12) | collective-permute-done | bytes 1048608 | tf_op jit(solution)/shard_map/ppermute | solution.py:42
  296.6 21.8 %collective-permute-done.13 = bf16[8,64,1024]{2,1,0:T(8,128)(2,1)S(1)} collective-permute-done((bf16[8,64,1024]{2,1,0:T(8,128)(2,1)}, bf16[8,64,1024]{2,1,0:T(8,128)(2,1)S(1)}, u32[]{:S(2)}, u32[]{:S(2)}) %collective-permute-start.13) | collective-permute-done | bytes 1048608 | tf_op jit(solution)/shard_map/ppermute | solution.py:42
  320.6 14.3 %reduce-scatter.5.cloned.1.call-done.refs_0_ = bf16[256,2048]{1,0:T(8,128)(2,1)} async-done(((bf16[2048,2048]{1,0:T(8,128)(2,1)}), bf16[256,2048]{1,0:T(8,128)(2,1)}) %reduce-scatter.5.cloned.1.call-update) | async-done | bytes 1048592 | tf_op jit(solution)/shard_map/reduce_scatter | solution.py:813
  337.9 2.6 multiply_convert_fusion.1
  340.6 6.6 copy.162.refs_0_
  347.2 11.3 %fusion.81.refs_0_ = f32[2048,512]{1,0:T(8,128)} fusion(bf16[2048,2048]{1,0:T(8,128)(2,1)} %all-gather.7.cloned.1.call-done.refs_1_, bf16[512,2048]{1,0:T(8,128)(2,1)} %bitcast.280), kind=kOutput, calls=%fused_computation.252 | convolution fusion | flops 4294967296 | bytes 14680064 | tf_op jit(solution)/shard_map/dot_general | solution.py:220
  358.5 62.6 %all-gather.9.cloned.1.call-done.rows_ref = bf16[2048,2048]{1,0:T(8,128)(2,1)} async-done(((bf16[256,2048]{1,0:T(8,128)(2,1)}), bf16[2048,2048]{1,0:T(8,128)(2,1)}) %all-gather.9.cloned.1.call-update) | async-done | bytes 8388624 | tf_op jit(solution)/shard_map/all_gather | solution.py:810
  421.1 25.1 %shard_map.278 = (bf16[2048,512]{1,0:T(8,128)(2,1)S(1)}, bf16[2048,1024]{1,0:T(8,128)(2,1)}, bf16[2048,2048]{1,0:T(8,128)(2,1)}) custom-call(bf16[2048,2048]{1,0:T(8,128)(2,1)} %all-gather.9.cloned.1.call-done.rows_ref, bf16[2048,1024]{1,0:T(8,128)(2,1)} %bitcast.43.refs_1_.weight_ref, bf16[1024,2048]{1,0:T(8,128)(2,1)} %shard_map.276.turned_ref, ...), custom_call_target="tpu_custom_call" | custom-call | bytes 79200000 | tf_op jit(solution)/shard_map/pallas_call | solution.py:744
  448.0 10.1 %convolution_convert_fusion.6.refs_2_ = bf16[512,2048]{1,0:T(8,128)(2,1)} fusion(bf16[2048,512]{1,0:T(8,128)(2,1)} %copy-done.42, bf16[2048,2048]{1,0:T(8,128)(2,1)} %all-gather.7.cloned.1.call-done.refs_1_), kind=kOutput, calls=%fused_computation.30 | convolution fusion | flops 4296015872 | bytes 12582912 | tf_op jit(solution)/shard_map/dot_general | solution.py:224
  458.1 12.9 %convolution_convert_fusion.3.refs_1_ = bf16[2048,1024]{1,0:T(8,128)(2,1)} fusion(bf16[2048,2048]{1,0:T(8,128)(2,1)} %all-gather.9.cloned.1.call-done.rows_ref, bf16[2048,1024]{1,0:T(8,128)(2,1)S(1)} %copy-done.90), kind=kOutput, calls=%fused_computation.12 | convolution fusion | flops 8592031744 | bytes 16777216 | tf_op jit(solution)/shard_map/dot_general | solution.py:224
  471.0 64.8 %reduce-scatter.7.cloned.1.call-done.refs_0_ = bf16[256,2048]{1,0:T(8,128)(2,1)} async-done(((bf16[2048,2048]{1,0:T(8,128)(2,1)}), bf16[256,2048]{1,0:T(8,128)(2,1)}) %reduce-scatter.7.cloned.1.call-update) | async-done | bytes 1048592 | tf_op jit(solution)/shard_map/reduce_scatter | solution.py:813
  535.8 2.3 fusion.14
  545.2 2.6 dynamic-slice_bitcast_fusion.2
  550.8 5.7 collective-permute-done.21
  556.6 2.4 collective-permute-start.20
  558.9 6.8 convolution_convert_fusion.1.refs_0_
  565.7 3.5 collective-permute-done.22
  569.3 2.4 fusion.35.refs_2_.in_ref
  571.6 18.7 %collective-permute-done.18 = bf16[512,1024]{1,0:T(8,128)(2,1)S(1)} collective-permute-done((bf16[512,1024]{1,0:T(8,128)(2,1)S(1)}, bf16[512,1024]{1,0:T(8,128)(2,1)S(1)}, u32[]{:S(2)}, u32[]{:S(2)}) %collective-permute-start.18) | collective-permute-done | bytes 1048608 | tf_op jit(solution)/shard_map/ppermute | solution.py:42
  590.3 20.3 %collective-permute-done.19 = bf16[512,1024]{1,0:T(8,128)(2,1)S(1)} collective-permute-done((bf16[512,1024]{1,0:T(8,128)(2,1)S(1)}, bf16[512,1024]{1,0:T(8,128)(2,1)S(1)}, u32[]{:S(2)}, u32[]{:S(2)}) %collective-permute-start.19) | collective-permute-done | bytes 1048608 | tf_op jit(solution)/shard_map/ppermute | solution.py:42
  610.6 3.1 fusion.22.refs_1_
  613.7 7.0 all-gather.11.cloned.1.call-done.refs_0_
  620.7 4.3 all-to-all-start.2
  625.2 8.4 fusion.82
  633.6 9.8 %convolution_convert_fusion.5 = bf16[512,2048]{1,0:T(8,128)(2,1)S(1)} fusion(bf16[2048,2048]{1,0:T(8,128)(2,1)} %shard_map.280.refs_1_, bf16[2048,128]{1,0:T(8,128)(2,1)S(1)} %bitcast.252, bf16[2048,384]{1,0:T(8,128)(2,1)S(1)} %copy-done.71), kind=kOutput, calls=%fused_computation.29 | convolution fusion | flops 4300210176 | bytes 12582912 | tf_op jit(solution)/shard_map/dot_general | solution.py:224
  643.7 2.2 copy-done.7
  654.7 2.4 collective-permute-start.26
  660.8 19.3 %shard_map.284 = (bf16[8,256,128]{2,1,0:T(8,128)(2,1)S(1)}, bf16[8,256,128]{2,1,0:T(8,128)(2,1)S(1)}, bf16[8,256,128]{2,1,0:T(8,128)(2,1)S(1)}) custom-call(f32[8,256,1792]{2,1,0:T(8,128)} %bitcast.259, f32[8,256,1792]{2,1,0:T(8,128)} %bitcast.260, f32[8,256,1792]{2,1,0:T(8,128)} %bitcast.261, f32[8,128,256]{2,1,0:T(8,128)S(1)} %copy-done.9, ...), custom_call_target="tpu_custom_call" | custom-call | bytes 68400000 | tf_op jit(solution)/shard_map/pallas_call | solution.py:704
  685.1 41.3 %shard_map.285 = (bf16[2048,1792]{1,0:T(8,128)(2,1)}, f32[8,896]{1,0:T(8,128)S(1)}, f32[8,128]{1,0:T(8,128)S(1)}, f32[8,384]{1,0:T(8,128)S(1)}) custom-call(f32[2048,1792]{1,0:T(8,128)} %fusion.78.mixed_ref.before_ref.refs_1_, f32[2048,1792]{1,0:T(8,128)} %fusion.78.mixed_ref.before_ref.refs_1_, f32[2048,8]{1,0:T(8,128)S(1)} %bitcast.246, ...), custom_call_target="tpu_custom_call" | custom-call | bytes 154800000 | tf_op jit(solution)/shard_map/pallas_call | solution.py:549
  726.4 21.5 %convolution_convert_fusion.refs_0_ = bf16[2048,2048]{1,0:T(8,128)(2,1)} fusion(bf16[2048,1792]{1,0:T(8,128)(2,1)} %shard_map.286.refs_0_, bf16[2048,1792]{1,0:T(8,128)(2,1)} %shard_map.257.refs_1_.refs_2_), kind=kOutput, calls=%fused_computation.7 | convolution fusion | flops 15036579840 | bytes 23068672 | tf_op jit(solution)/shard_map/dot_general | solution.py:220
  750.4 2.7 shard_map.288.refs_1_
  755.9 13.7 %add_convert_fusion.refs_1_ = bf16[2048,1024]{1,0:T(8,128)(2,1)S(1)} fusion(f32[2048,12]{1,0:T(8,128)S(1)} %bitcast.287, bf16[2048,1792]{1,0:T(8,128)(2,1)} %shard_map.293, bf16[2048,2048]{1,0:T(8,128)(2,1)} %all-gather.5.cloned.1.call-done.refs_1_, f32[2048]{0:T(1024)S(1)} %copy-done.77, f32[2048]{0:T(1024)S(1)} %copy-done.87), kind=kOutput, calls=%fused_computation.6 | convolution fusion | flops 8610906112 | bytes 16891904 | tf_op jit(solution)/shard_map/dot_general | solution.py:224
  774.7 12.3 %convolution_convert_fusion.4.refs_1_ = bf16[2048,768]{1,0:T(8,128)(2,1)} fusion(bf16[2048,1792]{1,0:T(8,128)(2,1)} %shard_map.293, bf16[2048,2048]{1,0:T(8,128)(2,1)} %all-gather.5.cloned.1.call-done.refs_1_, f32[2048]{0:T(1024)S(1)} %copy-done.77, f32[2048]{0:T(1024)S(1)} %copy-done.87), kind=kOutput, calls=%fused_computation.21 | convolution fusion | flops 6460801024 | bytes 14696448 | tf_op jit(solution)/shard_map/dot_general | solution.py:224
  787.0 8.8 collective-permute-done.43.refs_0_
  796.9 2.8 convert_element_type.383
  803.5 2.9 fusion.44
  812.8 8.8 collective-permute-done.42
  826.4 4.8 all-to-all-start.4
  845.9 6.5 collective-permute-done.32
  854.8 4.8 all-to-all-done.4
  859.6 3.8 all-to-all-start.3
  880.3 2.4 collective-permute-start.39
  882.8 3.5 fusion.18.in_ref
  (503 shorter events, 181.2 us)
Async XLA Ops:
  7.2 131.8 %copy-start = (f32[3,48]{1,0:T(4,128)S(1)}, f32[3,48]{1,0:T(4,128)}, u32[]{:S(2)}) copy-start(f32[3,48]{1,0:T(4,128)} %param.21) | copy-start | bytes 1732
  15.4 41.3 %all-to-all-start = ((bf16[8,64,1408]{2,1,0:T(8,128)(2,1)}), bf16[8,64,1408]{2,1,0:T(8,128)(2,1)S(1)}, u32[]{:S(2)}, u32[]{:S(2)}) async-start(bf16[8,64,1408]{2,1,0:T(8,128)(2,1)} %shard_map.255), calls=%async_computation | async-start | bytes 2883584 | tf_op jit(solution)/shard_map/all_to_all | solution.py:70
  21.7 117.3 %all-gather.5.cloned.1.call-start = ((), (), s32[]{:S(2)}) async-start(), calls=%async_computation.9 | async-start | bytes 9437184 | tf_op jit(solution)/shard_map/all_gather | solution.py:810
  57.9 186.8 %all-gather.7.cloned.1.call-start = ((), (), s32[]{:S(2)}) async-start(), calls=%async_computation.10 | async-start | bytes 9437184 | tf_op jit(solution)/shard_map/all_gather | solution.py:810
  58.8 33.4 %collective-permute-start = (bf16[8,64,1408]{2,1,0:T(8,128)(2,1)}, bf16[8,64,1408]{2,1,0:T(8,128)(2,1)S(1)}, u32[]{:S(2)}, u32[]{:S(2)}) collective-permute-start(bf16[8,64,1408]{2,1,0:T(8,128)(2,1)} %copy-done.54), channel_id=1, source_target_pairs={{0,1},{1,0},{2,3},{3,2},{4,5},{5,4},{6,7},{7,6},{8,9},{9,8},{10,11... | collective-permute-start | bytes 4325384 | tf_op jit(solution)/shard_map/ppermute | solution.py:42
  60.3 33.5 %collective-permute-start.1 = (bf16[8,64,1408]{2,1,0:T(8,128)(2,1)}, bf16[8,64,1408]{2,1,0:T(8,128)(2,1)S(1)}, u32[]{:S(2)}, u32[]{:S(2)}) collective-permute-start(bf16[8,64,1408]{2,1,0:T(8,128)(2,1)} %copy-done.54), channel_id=1, source_target_pairs={{0,2},{1,3},{2,0},{3,1},{4,6},{5,7},{6,4},{7,5},{8,10},{9,11},{10,... | collective-permute-start | bytes 4325384 | tf_op jit(solution)/shard_map/ppermute | solution.py:42
  92.2 17.0 %collective-permute-start.2 = (bf16[4,64,1408]{2,1,0:T(8,128)(2,1)S(1)}, bf16[4,64,1408]{2,1,0:T(8,128)(2,1)S(1)}, u32[]{:S(2)}, u32[]{:S(2)}) collective-permute-start(bf16[4,64,1408]{2,1,0:T(8,128)(2,1)S(1)} %slice.337), channel_id=1, source_target_pairs={{0,2},{1,3},{2,0},{3,1},{4,6},{5,7},{6,4},{7,5},{8,10},{9,11},{10,... | collective-permute-start | bytes 2162696 | tf_op jit(solution)/shard_map/ppermute | solution.py:42
  93.9 16.7 %collective-permute-start.3 = (bf16[4,64,1408]{2,1,0:T(8,128)(2,1)S(1)}, bf16[4,64,1408]{2,1,0:T(8,128)(2,1)S(1)}, u32[]{:S(2)}, u32[]{:S(2)}) collective-permute-start(bf16[4,64,1408]{2,1,0:T(8,128)(2,1)S(1)} %slice.338), channel_id=1, source_target_pairs={{0,1},{1,0},{2,3},{3,2},{4,5},{5,4},{6,7},{7,6},{8,9},{9,8},{10,11... | collective-permute-start | bytes 2162696 | tf_op jit(solution)/shard_map/ppermute | solution.py:42
  116.3 11.1 %collective-permute-start.4 = (bf16[2048,384]{1,0:T(8,128)(2,1)}, bf16[2048,384]{1,0:T(8,128)(2,1)}, u32[]{:S(2)}, u32[]{:S(2)}) collective-permute-start(bf16[2048,384]{1,0:T(8,128)(2,1)} %pad_maximum_fusion.1), channel_id=1, source_target_pairs={{0,4},{4,0},{8,12},{12,8},{16,20},{20,16},{24,28},{28,24},{1,5},{5... | collective-permute-start | bytes 4718600 | tf_op jit(solution)/shard_map/ppermute | solution.py:42
  144.3 59.0 %collective-permute-start.11 = (bf16[128,2048]{1,0:T(8,128)(2,1)}, bf16[128,2048]{1,0:T(8,128)(2,1)}, u32[]{:S(2)}, u32[]{:S(2)}) collective-permute-start(bf16[128,2048]{1,0:T(8,128)(2,1)} %shard_map.264.refs_0_), channel_id=1, source_target_pairs={{0,3},{1,2},{2,1},{3,0},{4,7},{5,6},{6,5},{7,4},{8,11},{9,10},{10,... | collective-permute-start | bytes 1572872 | tf_op jit(solution)/shard_map/ppermute | solution.py:42
  146.8 57.4 %collective-permute-start.10 = (bf16[128,2048]{1,0:T(8,128)(2,1)}, bf16[128,2048]{1,0:T(8,128)(2,1)}, u32[]{:S(2)}, u32[]{:S(2)}) collective-permute-start(bf16[128,2048]{1,0:T(8,128)(2,1)} %shard_map.264.refs_0_), channel_id=1, source_target_pairs={{0,2},{1,3},{2,0},{3,1},{4,6},{5,7},{6,4},{7,5},{8,10},{9,11},{10,... | collective-permute-start | bytes 1572872 | tf_op jit(solution)/shard_map/ppermute | solution.py:42
  147.3 56.9 %collective-permute-start.9 = (bf16[128,2048]{1,0:T(8,128)(2,1)}, bf16[128,2048]{1,0:T(8,128)(2,1)}, u32[]{:S(2)}, u32[]{:S(2)}) collective-permute-start(bf16[128,2048]{1,0:T(8,128)(2,1)} %shard_map.264.refs_0_), channel_id=1, source_target_pairs={{0,1},{1,0},{2,3},{3,2},{4,5},{5,4},{6,7},{7,6},{8,9},{9,8},{10,11... | collective-permute-start | bytes 1572872 | tf_op jit(solution)/shard_map/ppermute | solution.py:42
  147.8 65.4 %all-to-all-start.1 = ((bf16[8,64,1024]{2,1,0:T(8,128)(2,1)}), bf16[8,64,1024]{2,1,0:T(8,128)(2,1)}, u32[]{:S(2)}, u32[]{:S(2)}) async-start(bf16[8,64,1024]{2,1,0:T(8,128)(2,1)} %shard_map.260), calls=%async_computation.1 | async-start | bytes 2097152 | tf_op jit(solution)/shard_map/all_to_all | solution.py:70
  152.1 182.9 %reduce-scatter.5.cloned.1.call-start = ((), (), s32[]{:S(2)}) async-start(), calls=%async_computation.11 | async-start | bytes 9437184 | tf_op jit(solution)/shard_map/reduce_scatter | solution.py:813
  202.9 5.1 collective-permute-start.5
  208.0 22.4 %collective-permute-start.6 = (f32[2048]{0:T(1024)S(1)}, f32[2048]{0:T(1024)S(1)}, u32[]{:S(2)}, u32[]{:S(2)}) collective-permute-start(f32[2048]{0:T(1024)S(1)} %add.275), channel_id=1, source_target_pairs={{0,8},{4,12},{8,0},{12,4},{16,24},{20,28},{24,16},{28,20},{1,9},{5... | collective-permute-start | bytes 24584 | tf_op jit(solution)/shard_map/ppermute | solution.py:42
  209.9 20.6 %collective-permute-start.7 = (f32[2048]{0:T(1024)S(1)}, f32[2048]{0:T(1024)S(1)}, u32[]{:S(2)}, u32[]{:S(2)}) collective-permute-start(f32[2048]{0:T(1024)S(1)} %add.275), channel_id=1, source_target_pairs={{0,16},{4,20},{8,24},{12,28},{16,0},{20,4},{24,8},{28,12},{1,17},{... | collective-permute-start | bytes 24584 | tf_op jit(solution)/shard_map/ppermute | solution.py:42
  212.2 18.3 %collective-permute-start.8 = (f32[2048]{0:T(1024)S(1)}, f32[2048]{0:T(1024)S(1)}, u32[]{:S(2)}, u32[]{:S(2)}) collective-permute-start(f32[2048]{0:T(1024)S(1)} %add.275), channel_id=1, source_target_pairs={{0,24},{4,28},{8,16},{12,20},{16,8},{20,12},{24,0},{28,4},{1,25},{... | collective-permute-start | bytes 24584 | tf_op jit(solution)/shard_map/ppermute | solution.py:42
  244.7 176.4 %all-gather.9.cloned.1.call-start = ((), (), s32[]{:S(2)}) async-start(), calls=%async_computation.12 | async-start | bytes 9437184 | tf_op jit(solution)/shard_map/all_gather | solution.py:810
  246.8 291.4 %copy-start.73 = (f32[2048]{0:T(1024)}, f32[2048]{0:T(1024)S(1)}, u32[]{:S(2)}) copy-start(f32[2048]{0:T(1024)S(1)} %mul.308) | copy-start | bytes 24580
  246.8 15.1 %collective-permute-start.15 = (bf16[128,2048]{1,0:T(8,128)(2,1)}, bf16[128,2048]{1,0:T(8,128)(2,1)}, u32[]{:S(2)}, u32[]{:S(2)}) collective-permute-start(bf16[128,2048]{1,0:T(8,128)(2,1)} %shard_map.274), channel_id=1, source_target_pairs={{0,1},{1,0},{2,3},{3,2},{4,5},{5,4},{6,7},{7,6},{8,9},{9,8},{10,11... | collective-permute-start | bytes 1572872 | tf_op jit(solution)/shard_map/ppermute | solution.py:42
  248.3 26.3 %collective-permute-start.16 = (bf16[128,2048]{1,0:T(8,128)(2,1)}, bf16[128,2048]{1,0:T(8,128)(2,1)}, u32[]{:S(2)}, u32[]{:S(2)}) collective-permute-start(bf16[128,2048]{1,0:T(8,128)(2,1)} %shard_map.274), channel_id=1, source_target_pairs={{0,2},{1,3},{2,0},{3,1},{4,6},{5,7},{6,4},{7,5},{8,10},{9,11},{10,... | collective-permute-start | bytes 1572872 | tf_op jit(solution)/shard_map/ppermute | solution.py:42
  249.7 26.0 %collective-permute-start.17 = (bf16[128,2048]{1,0:T(8,128)(2,1)}, bf16[128,2048]{1,0:T(8,128)(2,1)}, u32[]{:S(2)}, u32[]{:S(2)}) collective-permute-start(bf16[128,2048]{1,0:T(8,128)(2,1)} %shard_map.274), channel_id=1, source_target_pairs={{0,3},{1,2},{2,1},{3,0},{4,7},{5,6},{6,5},{7,4},{8,11},{9,10},{10,... | collective-permute-start | bytes 1572872 | tf_op jit(solution)/shard_map/ppermute | solution.py:42
  250.3 45.2 %collective-permute-start.12 = (bf16[8,64,1024]{2,1,0:T(8,128)(2,1)}, bf16[8,64,1024]{2,1,0:T(8,128)(2,1)S(1)}, u32[]{:S(2)}, u32[]{:S(2)}) collective-permute-start(bf16[8,64,1024]{2,1,0:T(8,128)(2,1)} %shard_map.272), channel_id=1, source_target_pairs={{0,1},{1,0},{2,3},{3,2},{4,5},{5,4},{6,7},{7,6},{8,9},{9,8},{10,11... | collective-permute-start | bytes 3145736 | tf_op jit(solution)/shard_map/ppermute | solution.py:42
  251.7 66.7 %collective-permute-start.13 = (bf16[8,64,1024]{2,1,0:T(8,128)(2,1)}, bf16[8,64,1024]{2,1,0:T(8,128)(2,1)S(1)}, u32[]{:S(2)}, u32[]{:S(2)}) collective-permute-start(bf16[8,64,1024]{2,1,0:T(8,128)(2,1)} %shard_map.272), channel_id=1, source_target_pairs={{0,2},{1,3},{2,0},{3,1},{4,6},{5,7},{6,4},{7,5},{8,10},{9,11},{10,... | collective-permute-start | bytes 3145736 | tf_op jit(solution)/shard_map/ppermute | solution.py:42
  261.9 57.7 %collective-permute-start.14 = (bf16[8,64,1024]{2,1,0:T(8,128)(2,1)}, bf16[8,64,1024]{2,1,0:T(8,128)(2,1)S(1)}, u32[]{:S(2)}, u32[]{:S(2)}) collective-permute-start(bf16[8,64,1024]{2,1,0:T(8,128)(2,1)} %shard_map.272), channel_id=1, source_target_pairs={{0,3},{1,2},{2,1},{3,0},{4,7},{5,6},{6,5},{7,4},{8,11},{9,10},{10,... | collective-permute-start | bytes 3145736 | tf_op jit(solution)/shard_map/ppermute | solution.py:42
  276.8 43.8 %copy-start.61 = (bf16[4,128,2048]{2,1,0:T(8,128)(2,1)}, bf16[4,128,2048]{2,1,0:T(8,128)(2,1)S(1)}, u32[]{:S(2)}) copy-start(bf16[4,128,2048]{2,1,0:T(8,128)(2,1)S(1)} %bitcast_dynamic-update-slice_fusion.7) | copy-start | bytes 6291460
  337.9 200.3 %copy-start.79 = (f32[256]{0:T(256)}, f32[256]{0:T(256)S(1)}, u32[]{:S(2)}) copy-start(f32[256]{0:T(256)S(1)} %get-tuple-element.162) | copy-start | bytes 3076
  337.9 200.3 %copy-start.82 = (f32[256]{0:T(256)}, f32[256]{0:T(256)S(1)}, u32[]{:S(2)}) copy-start(f32[256]{0:T(256)S(1)} %get-tuple-element.161) | copy-start | bytes 3076
  340.5 195.3 %reduce-scatter.7.cloned.1.call-start = ((), (), s32[]{:S(2)}) async-start(), calls=%async_computation.13 | async-start | bytes 9437184 | tf_op jit(solution)/shard_map/reduce_scatter | solution.py:813
  447.5 173.1 %all-gather.11.cloned.1.call-start = ((), (), s32[]{:S(2)}) async-start(), calls=%async_computation.14 | async-start | bytes 9437184 | tf_op jit(solution)/shard_map/all_gather | solution.py:810
  471.0 64.8 %copy-start.44 = (bf16[256,2048]{1,0:T(8,128)(2,1)S(1)}, bf16[256,2048]{1,0:T(8,128)(2,1)}, u32[]{:S(2)}) copy-start(bf16[256,2048]{1,0:T(8,128)(2,1)} %shard_map.275) | copy-start | bytes 3145732
  540.1 207.8 %reduce-scatter.9.cloned.1.call-start = ((), (), s32[]{:S(2)}) async-start(), calls=%async_computation.15 | async-start | bytes 9437184 | tf_op jit(solution)/shard_map/reduce_scatter | solution.py:1038
  541.6 14.9 %collective-permute-start.21 = (bf16[128,2048]{1,0:T(8,128)(2,1)S(1)}, bf16[128,2048]{1,0:T(8,128)(2,1)S(1)}, u32[]{:S(2)}, u32[]{:S(2)}) collective-permute-start(bf16[128,2048]{1,0:T(8,128)(2,1)S(1)} %get-tuple-element.149), channel_id=1, source_target_pairs={{0,1},{1,0},{2,3},{3,2},{4,5},{5,4},{6,7},{7,6},{8,9},{9,8},{10,11... | collective-permute-start | bytes 1572872 | tf_op jit(solution)/shard_map/ppermute | solution.py:42
  543.1 26.1 %collective-permute-start.22 = (bf16[128,2048]{1,0:T(8,128)(2,1)S(1)}, bf16[128,2048]{1,0:T(8,128)(2,1)S(1)}, u32[]{:S(2)}, u32[]{:S(2)}) collective-permute-start(bf16[128,2048]{1,0:T(8,128)(2,1)S(1)} %get-tuple-element.151), channel_id=1, source_target_pairs={{0,2},{1,3},{2,0},{3,1},{4,6},{5,7},{6,4},{7,5},{8,10},{9,11},{10,... | collective-permute-start | bytes 1572872 | tf_op jit(solution)/shard_map/ppermute | solution.py:42
  544.6 24.6 %collective-permute-start.23 = (bf16[128,2048]{1,0:T(8,128)(2,1)S(1)}, bf16[128,2048]{1,0:T(8,128)(2,1)S(1)}, u32[]{:S(2)}, u32[]{:S(2)}) collective-permute-start(bf16[128,2048]{1,0:T(8,128)(2,1)S(1)} %get-tuple-element.150), channel_id=1, source_target_pairs={{0,3},{1,2},{2,1},{3,0},{4,7},{5,6},{6,5},{7,4},{8,11},{9,10},{10,... | collective-permute-start | bytes 1572872 | tf_op jit(solution)/shard_map/ppermute | solution.py:42
  547.8 42.5 %collective-permute-start.18 = (bf16[512,1024]{1,0:T(8,128)(2,1)S(1)}, bf16[512,1024]{1,0:T(8,128)(2,1)S(1)}, u32[]{:S(2)}, u32[]{:S(2)}) collective-permute-start(bf16[512,1024]{1,0:T(8,128)(2,1)S(1)} %get-tuple-element.133), channel_id=1, source_target_pairs={{0,1},{1,0},{2,3},{3,2},{4,5},{5,4},{6,7},{7,6},{8,9},{9,8},{10,11... | collective-permute-start | bytes 3145736 | tf_op jit(solution)/shard_map/ppermute | solution.py:42
  549.4 61.2 %collective-permute-start.19 = (bf16[512,1024]{1,0:T(8,128)(2,1)S(1)}, bf16[512,1024]{1,0:T(8,128)(2,1)S(1)}, u32[]{:S(2)}, u32[]{:S(2)}) collective-permute-start(bf16[512,1024]{1,0:T(8,128)(2,1)S(1)} %get-tuple-element.135), channel_id=1, source_target_pairs={{0,2},{1,3},{2,0},{3,1},{4,6},{5,7},{6,4},{7,5},{8,10},{9,11},{10,... | collective-permute-start | bytes 3145736 | tf_op jit(solution)/shard_map/ppermute | solution.py:42
  556.6 54.0 %collective-permute-start.20 = (bf16[512,1024]{1,0:T(8,128)(2,1)S(1)}, bf16[512,1024]{1,0:T(8,128)(2,1)S(1)}, u32[]{:S(2)}, u32[]{:S(2)}) collective-permute-start(bf16[512,1024]{1,0:T(8,128)(2,1)S(1)} %get-tuple-element.134), channel_id=1, source_target_pairs={{0,3},{1,2},{2,1},{3,0},{4,7},{5,6},{6,5},{7,4},{8,11},{9,10},{10,... | collective-permute-start | bytes 3145736 | tf_op jit(solution)/shard_map/ppermute | solution.py:42
  620.7 105.7 %all-to-all-start.2 = ((bf16[8,64,1024]{2,1,0:T(8,128)(2,1)}), bf16[8,64,1024]{2,1,0:T(8,128)(2,1)}, u32[]{:S(2)}, u32[]{:S(2)}) async-start(bf16[8,64,1024]{2,1,0:T(8,128)(2,1)} %bitcast.66), calls=%async_computation.5 | async-start | bytes 2097152 | tf_op jit(solution)/shard_map/all_to_all | solution.py:70
  625.0 242.6 %reduce-scatter.11.cloned.1.call-start = ((), (), s32[]{:S(2)}) async-start(), calls=%async_computation.16 | async-start | bytes 9437184 | tf_op jit(solution)/shard_map/reduce_scatter | solution.py:1123
  647.0 5.4 collective-permute-start.24
  649.6 76.8 %collective-permute-start.28 = (bf16[128,2048]{1,0:T(8,128)(2,1)}, bf16[128,2048]{1,0:T(8,128)(2,1)}, u32[]{:S(2)}, u32[]{:S(2)}) collective-permute-start(bf16[128,2048]{1,0:T(8,128)(2,1)} %get-tuple-element.147), channel_id=1, source_target_pairs={{0,1},{1,0},{2,3},{3,2},{4,5},{5,4},{6,7},{7,6},{8,9},{9,8},{10,11... | collective-permute-start | bytes 1572872 | tf_op jit(solution)/shard_map/ppermute | solution.py:42
  650.9 75.5 %collective-permute-start.29 = (bf16[128,2048]{1,0:T(8,128)(2,1)}, bf16[128,2048]{1,0:T(8,128)(2,1)}, u32[]{:S(2)}, u32[]{:S(2)}) collective-permute-start(bf16[128,2048]{1,0:T(8,128)(2,1)} %get-tuple-element.148), channel_id=1, source_target_pairs={{0,2},{1,3},{2,0},{3,1},{4,6},{5,7},{6,4},{7,5},{8,10},{9,11},{10,... | collective-permute-start | bytes 1572872 | tf_op jit(solution)/shard_map/ppermute | solution.py:42
  652.9 27.4 %collective-permute-start.25 = (f32[2048]{0:T(1024)}, f32[2048]{0:T(1024)S(1)}, u32[]{:S(2)}, u32[]{:S(2)}) collective-permute-start(f32[2048]{0:T(1024)} %add.291.refs_1_), channel_id=1, source_target_pairs={{0,8},{4,12},{8,0},{12,4},{16,24},{20,28},{24,16},{28,20},{1,9},{5... | collective-permute-start | bytes 24584 | tf_op jit(solution)/shard_map/ppermute | solution.py:42
  654.7 26.4 %collective-permute-start.26 = (f32[2048]{0:T(1024)}, f32[2048]{0:T(1024)S(1)}, u32[]{:S(2)}, u32[]{:S(2)}) collective-permute-start(f32[2048]{0:T(1024)} %add.291.refs_1_), channel_id=1, source_target_pairs={{0,16},{4,20},{8,24},{12,28},{16,0},{20,4},{24,8},{28,12},{1,17},{... | collective-permute-start | bytes 24584 | tf_op jit(solution)/shard_map/ppermute | solution.py:42
  657.1 24.1 %collective-permute-start.27 = (f32[2048]{0:T(1024)}, f32[2048]{0:T(1024)S(1)}, u32[]{:S(2)}, u32[]{:S(2)}) collective-permute-start(f32[2048]{0:T(1024)} %add.291.refs_1_), channel_id=1, source_target_pairs={{0,24},{4,28},{8,16},{12,20},{16,8},{20,12},{24,0},{28,4},{1,25},{... | collective-permute-start | bytes 24584 | tf_op jit(solution)/shard_map/ppermute | solution.py:42
  680.3 46.1 %collective-permute-start.30 = (bf16[128,2048]{1,0:T(8,128)(2,1)}, bf16[128,2048]{1,0:T(8,128)(2,1)}, u32[]{:S(2)}, u32[]{:S(2)}) collective-permute-start(bf16[128,2048]{1,0:T(8,128)(2,1)} %get-tuple-element.146), channel_id=1, source_target_pairs={{0,3},{1,2},{2,1},{3,0},{4,7},{5,6},{6,5},{7,4},{8,11},{9,10},{10,... | collective-permute-start | bytes 1572872 | tf_op jit(solution)/shard_map/ppermute | solution.py:42
  771.7 24.2 %collective-permute-start.43 = (bf16[2,256,1024]{2,1,0:T(8,128)(2,1)S(1)}, bf16[2,256,1024]{2,1,0:T(8,128)(2,1)S(1)}, u32[]{:S(2)}, u32[]{:S(2)}) collective-permute-start(bf16[2,256,1024]{2,1,0:T(8,128)(2,1)S(1)} %pad_maximum_fusion.7), channel_id=1, source_target_pairs={{0,2},{1,3},{2,0},{3,1},{4,6},{5,7},{6,4},{7,5},{8,10},{9,11},{10,... | collective-permute-start | bytes 3145736 | tf_op jit(solution)/shard_map/ppermute | solution.py:42
  773.2 26.4 %collective-permute-start.41 = (bf16[2,256,1024]{2,1,0:T(8,128)(2,1)S(1)}, bf16[2,256,1024]{2,1,0:T(8,128)(2,1)S(1)}, u32[]{:S(2)}, u32[]{:S(2)}) collective-permute-start(bf16[2,256,1024]{2,1,0:T(8,128)(2,1)S(1)} %pad_maximum_fusion.6), channel_id=1, source_target_pairs={{0,1},{1,0},{2,3},{3,2},{4,5},{5,4},{6,7},{7,6},{8,9},{9,8},{10,11... | collective-permute-start | bytes 3145736 | tf_op jit(solution)/shard_map/ppermute | solution.py:42
  806.4 15.2 %collective-permute-start.42 = (bf16[256,1024]{1,0:T(8,128)(2,1)}, bf16[256,1024]{1,0:T(8,128)(2,1)}, u32[]{:S(2)}, u32[]{:S(2)}) collective-permute-start(bf16[256,1024]{1,0:T(8,128)(2,1)} %get-tuple-element.127), channel_id=1, source_target_pairs={{0,2},{1,3},{2,0},{3,1},{4,6},{5,7},{6,4},{7,5},{8,10},{9,11},{10,... | collective-permute-start | bytes 1572872 | tf_op jit(solution)/shard_map/ppermute | solution.py:42
  808.0 15.2 %collective-permute-start.44 = (bf16[256,1024]{1,0:T(8,128)(2,1)}, bf16[256,1024]{1,0:T(8,128)(2,1)}, u32[]{:S(2)}, u32[]{:S(2)}) collective-permute-start(bf16[256,1024]{1,0:T(8,128)(2,1)} %get-tuple-element.128), channel_id=1, source_target_pairs={{0,1},{1,0},{2,3},{3,2},{4,5},{5,4},{6,7},{7,6},{8,9},{9,8},{10,11... | collective-permute-start | bytes 1572872 | tf_op jit(solution)/shard_map/ppermute | solution.py:42
  810.8 24.9 %collective-permute-start.33 = (bf16[2,256,768]{2,1,0:T(8,128)(2,1)}, bf16[2,256,768]{2,1,0:T(8,128)(2,1)}, u32[]{:S(2)}, u32[]{:S(2)}) collective-permute-start(bf16[2,256,768]{2,1,0:T(8,128)(2,1)} %pad_maximum_fusion.10), channel_id=1, source_target_pairs={{0,2},{1,3},{2,0},{3,1},{4,6},{5,7},{6,4},{7,5},{8,10},{9,11},{10,... | collective-permute-start | bytes 2359304 | tf_op jit(solution)/shard_map/ppermute | solution.py:42
  812.3 24.8 %collective-permute-start.31 = (bf16[2,256,768]{2,1,0:T(8,128)(2,1)}, bf16[2,256,768]{2,1,0:T(8,128)(2,1)S(1)}, u32[]{:S(2)}, u32[]{:S(2)}) collective-permute-start(bf16[2,256,768]{2,1,0:T(8,128)(2,1)} %pad_maximum_fusion.9), channel_id=1, source_target_pairs={{0,1},{1,0},{2,3},{3,2},{4,5},{5,4},{6,7},{7,6},{8,9},{9,8},{10,11... | collective-permute-start | bytes 2359304 | tf_op jit(solution)/shard_map/ppermute | solution.py:42
  826.4 33.2 %all-to-all-start.4 = ((bf16[8,64,1024]{2,1,0:T(8,128)(2,1)}), bf16[8,64,1024]{2,1,0:T(8,128)(2,1)}, u32[]{:S(2)}, u32[]{:S(2)}) async-start(bf16[8,64,1024]{2,1,0:T(8,128)(2,1)} %bitcast.97), calls=%async_computation.8 | async-start | bytes 2097152 | tf_op jit(solution)/shard_map/all_to_all | solution.py:70
  840.7 11.6 %collective-permute-start.32 = (bf16[256,768]{1,0:T(8,128)(2,1)S(1)}, bf16[256,768]{1,0:T(8,128)(2,1)S(1)}, u32[]{:S(2)}, u32[]{:S(2)}) collective-permute-start(bf16[256,768]{1,0:T(8,128)(2,1)S(1)} %get-tuple-element.138), channel_id=1, source_target_pairs={{0,2},{1,3},{2,0},{3,1},{4,6},{5,7},{6,4},{7,5},{8,10},{9,11},{10,... | collective-permute-start | bytes 1179656 | tf_op jit(solution)/shard_map/ppermute | solution.py:42
  842.4 10.0 %collective-permute-start.34 = (bf16[256,768]{1,0:T(8,128)(2,1)S(1)}, bf16[256,768]{1,0:T(8,128)(2,1)S(1)}, u32[]{:S(2)}, u32[]{:S(2)}) collective-permute-start(bf16[256,768]{1,0:T(8,128)(2,1)S(1)} %get-tuple-element.139), channel_id=1, source_target_pairs={{0,1},{1,0},{2,3},{3,2},{4,5},{5,4},{6,7},{7,6},{8,9},{9,8},{10,11... | collective-permute-start | bytes 1179656 | tf_op jit(solution)/shard_map/ppermute | solution.py:42
  859.6 29.9 %all-to-all-start.3 = ((bf16[8,64,768]{2,1,0:T(8,128)(2,1)}), bf16[8,64,768]{2,1,0:T(8,128)(2,1)S(1)}, u32[]{:S(2)}, u32[]{:S(2)}) async-start(bf16[8,64,768]{2,1,0:T(8,128)(2,1)} %bitcast.85), calls=%async_computation.7 | async-start | bytes 1572864 | tf_op jit(solution)/shard_map/all_to_all | solution.py:70
  867.6 5.3 collective-permute-start.35
  873.6 3.6 collective-permute-start.36
  877.2 1.1 collective-permute-start.37
  878.4 9.9 %collective-permute-start.38 = (f32[144]{0:T(256)S(1)}, f32[144]{0:T(256)S(1)}, u32[]{:S(2)}, u32[]{:S(2)}) collective-permute-start(f32[144]{0:T(256)S(1)} %add.311), channel_id=1, source_target_pairs={{0,8},{4,12},{8,0},{12,4},{16,24},{20,28},{24,16},{28,20},{1,9},{5... | collective-permute-start | bytes 1736 | tf_op jit(solution)/shard_map/ppermute | solution.py:42
  880.3 7.9 collective-permute-start.39
  882.7 5.5 collective-permute-start.40
  (85 other events, 514.1 us)
Sparse Core Ops, SparseCore 0:
  58.0 80.9 all-gather.4
  141.1 103.4 all-gather.6
  246.9 87.9 reduce-scatter.4
  340.7 80.4 all-gather.8
  447.6 88.1 reduce-scatter.6
  540.2 80.3 all-gather.10
  622.9 104.2 reduce-scatter.8
  748.0 91.4 reduce-scatter.10

commit v4 on v3

--- a/solution.py
+++ b/solution.py
@@ -1113,6 +1113,7 @@
     zx_part = over_dp(zx_total, True, (rest_total,))
     zx_sum = to_owners(zx_part)
     rest_sum = to_owners(over_dp(rest_total, True, (zx_total,)))
+    gu_sum, down_grad = after(gu_sum, rest_total), after(down_grad, rest_total)
     gate_up_grad = assembled(
         (owner, 2 * FF), f32, [(0, cube, flat) for flat, cube in gu_moves], gu_sum
     )

time: 913 us -> 913 us (level)
  transfers between devices with their start and end apart: 58 -> 58, of which waited for: 28 -> 26; matrix products, arithmetic and copies ran while one was open for 27% -> 27% of each run, Pallas kernels for 12% -> 12%
where the time goes in v4:
time: 913 us; the launch traced here: 903 us
  waiting for transfers between devices  369 us (40%)
  matrix products  137 us (15%)
  Pallas kernels  132 us (14%)
  local copies, waits for them, and re-layouts  99.2 us (11%)
  starting transfers between devices  81.9 us (9%)
  other arithmetic  67.4 us (7%)
  between operations  16.2 us (2%)
    ppermute x45, waiting for transfers between devices, permuted(): return lax.ppermute(value, axis, pairs)  173 us
    reduce_scatter x2, waiting for transfers between devices, scattered(): lax.psum_scatter(value.astype(bf16), 'seq', scatter_dimension=0, tiled=True)  79.1 us
    all_gather x4, waiting for transfers between devices, gathered(): return lax.all_gather(value, 'seq', axis=0, tiled=True)  77.8 us
    dot_general x5, matrix products, cross(): lax.dot_general(left, right, (((0,), (0,)), ((), ())), preferred_element_...  58.8 us
    ppermute x45, starting transfers between devices, permuted(): return lax.ppermute(value, axis, pairs)  57 us
    unnamed x195, local copies, waits for them, and re-layouts  51.3 us
    pallas_call x1, Pallas kernels, ssd_backward(): pl.pallas_call(ssd_backward_kernel, grid=(micro, n), out_shape=(jax.Shape...  41.3 us
    dot_general x3, matrix products, dot_t(): lax.dot_general(left, right, (((1,), (1,)), ((), ())), preferred_element_...  41.3 us
  transfers between devices with their start and end apart: 58, of which 26 were waited for; matrix products, arithmetic and copies ran while one was open for 27% of the time, Pallas kernels for 12%

profile of v4, /device:TPU:0, one launch (start us, length us, event | category | flops | bytes accessed | tf_op | source)
XLA Modules:
  0.0 902.5 jit_solution(2874942194597759547)
XLA Ops:
  9.0 2.8 concatenate.98
  15.4 6.3 all-to-all-start
  24.1 32.6 %all-to-all-done.refs_1_ = bf16[8,64,1408]{2,1,0:T(8,128)(2,1)S(1)} async-done(((bf16[8,64,1408]{2,1,0:T(8,128)(2,1)}), bf16[8,64,1408]{2,1,0:T(8,128)(2,1)S(1)}, u32[]{:S(2)}, u32[]{:S(2)}) %all-to-all-start) | async-done | bytes 1441824 | tf_op jit(solution)/shard_map/all_to_all | solution.py:70
  63.1 29.1 %collective-permute-done = bf16[8,64,1408]{2,1,0:T(8,128)(2,1)S(1)} collective-permute-done((bf16[8,64,1408]{2,1,0:T(8,128)(2,1)}, bf16[8,64,1408]{2,1,0:T(8,128)(2,1)S(1)}, u32[]{:S(2)}, u32[]{:S(2)}) %collective-permute-start) | collective-permute-done | bytes 1441824 | tf_op jit(solution)/shard_map/ppermute | solution.py:42
  95.9 13.3 %collective-permute-done.2 = bf16[4,64,1408]{2,1,0:T(8,128)(2,1)S(1)} collective-permute-done((bf16[4,64,1408]{2,1,0:T(8,128)(2,1)S(1)}, bf16[4,64,1408]{2,1,0:T(8,128)(2,1)S(1)}, u32[]{:S(2)}, u32[]{:S(2)}) %collective-permute-start.2) | collective-permute-done | bytes 720928 | tf_op jit(solution)/shard_map/ppermute | solution.py:42
  127.3 2.1 broadcast_select_fusion
  134.5 4.5 all-gather.5.cloned.1.call-done.refs_1_
  144.3 2.5 collective-permute-start.11
  147.8 4.3 all-to-all-start.1
  152.3 5.1 fusion
  158.1 21.9 %fusion.78.mixed_ref.before_ref.refs_1_ = f32[2048,1792]{1,0:T(8,128)} fusion(bf16[2048,1792]{1,0:T(8,128)(2,1)} %shard_map.257.refs_1_.refs_2_, bf16[2048,2048]{1,0:T(8,128)(2,1)} %all-gather.5.cloned.1.call-done.refs_1_, f32[2048]{0:T(1024)S(1)} %mul.290, f32[2048]{0:T(1024)S(1)} %add_rsqrt_fusion.1), kind=kOutput, calls=%fused_computation.250 | convolution fusion | flops 15049162752 | bytes 30425088 | tf_op jit(solution)/shard_map/dot_general | solution.py:216
  180.1 19.0 %shard_map.258 = (f32[2048,384]{1,0:T(8,128)S(1)}, f32[2048,384]{1,0:T(8,128)S(1)}, bf16[16,256,384]{2,1,0:T(8,128)(2,1)S(1)}) custom-call(f32[2048,1792]{1,0:T(8,128)} %fusion.78.mixed_ref.before_ref.refs_1_, f32[2048,1792]{1,0:T(8,128)} %fusion.78.mixed_ref.before_ref.refs_1_, f32[2048,8]{1,0:T(8,128)S(1)} %bitcast.245, f32[16,1,128]{2,1,0:T(1,128)S(1)} %bitcast.254, ...), custom_call_target="tpu_custom_call" | custom-call | bytes 72000000 | tf_op jit(solution)/shard_map/pallas_call | solution.py:512
  209.9 2.3 collective-permute-start.7
  215.7 14.7 %shard_map.262 = bf16[8,256,128]{2,1,0:T(8,128)(2,1)S(1)} custom-call(f32[8,256,1792]{2,1,0:T(8,128)} %bitcast.256, f32[8,256,1792]{2,1,0:T(8,128)} %bitcast.257, f32[8,256,1792]{2,1,0:T(8,128)} %bitcast.258, f32[8,128,256]{2,1,0:T(8,128)S(1)} %copy-done.8, f32[8,128,256]{2,1,0:T(8,128)S(1)} %copy-done.8, f32[8,256,8]{2,1,0:T(8,128)S(1)} %copy-done.10, ...), custom_call_target="tpu_custom_call" | custom-call | bytes 50400000 | tf_op jit(solution)/shard_map/pallas_call | solution.py:686
  232.7 8.3 convolution_convert_fusion.2.refs_0_
  241.0 3.7 all-gather.7.cloned.1.call-done.refs_1_
  253.5 2.5 broadcast_in_dim.111
  256.1 2.3 bitcast_dynamic-update-slice_fusion.6
  258.4 3.5 collective-permute-done.15
  261.9 2.4 collective-permute-start.14
  265.3 9.3 %collective-permute-done.16 = bf16[128,2048]{1,0:T(8,128)(2,1)} collective-permute-done((bf16[128,2048]{1,0:T(8,128)(2,1)}, bf16[128,2048]{1,0:T(8,128)(2,1)}, u32[]{:S(2)}, u32[]{:S(2)}) %collective-permute-start.16) | collective-permute-done | bytes 524320 | tf_op jit(solution)/shard_map/ppermute | solution.py:42
  276.8 18.7 %collective-permute-done.12 = bf16[8,64,1024]{2,1,0:T(8,128)(2,1)S(1)} collective-permute-done((bf16[8,64,1024]{2,1,0:T(8,128)(2,1)}, bf16[8,64,1024]{2,1,0:T(8,128)(2,1)S(1)}, u32[]{:S(2)}, u32[]{:S(2)}) %collective-permute-start.12) | collective-permute-done | bytes 1048608 | tf_op jit(solution)/shard_map/ppermute | solution.py:42
  296.6 21.8 %collective-permute-done.13 = bf16[8,64,1024]{2,1,0:T(8,128)(2,1)S(1)} collective-permute-done((bf16[8,64,1024]{2,1,0:T(8,128)(2,1)}, bf16[8,64,1024]{2,1,0:T(8,128)(2,1)S(1)}, u32[]{:S(2)}, u32[]{:S(2)}) %collective-permute-start.13) | collective-permute-done | bytes 1048608 | tf_op jit(solution)/shard_map/ppermute | solution.py:42
  320.6 14.3 %reduce-scatter.5.cloned.1.call-done.refs_0_ = bf16[256,2048]{1,0:T(8,128)(2,1)} async-done(((bf16[2048,2048]{1,0:T(8,128)(2,1)}), bf16[256,2048]{1,0:T(8,128)(2,1)}) %reduce-scatter.5.cloned.1.call-update) | async-done | bytes 1048592 | tf_op jit(solution)/shard_map/reduce_scatter | solution.py:813
  337.9 2.6 multiply_convert_fusion.1
  340.6 6.6 copy.164.refs_0_
  347.2 11.3 %fusion.81.refs_0_ = f32[2048,512]{1,0:T(8,128)} fusion(bf16[2048,2048]{1,0:T(8,128)(2,1)} %all-gather.7.cloned.1.call-done.refs_1_, bf16[512,2048]{1,0:T(8,128)(2,1)} %bitcast.280), kind=kOutput, calls=%fused_computation.252 | convolution fusion | flops 4294967296 | bytes 14680064 | tf_op jit(solution)/shard_map/dot_general | solution.py:220
  358.5 62.6 %all-gather.9.cloned.1.call-done.rows_ref = bf16[2048,2048]{1,0:T(8,128)(2,1)} async-done(((bf16[256,2048]{1,0:T(8,128)(2,1)}), bf16[2048,2048]{1,0:T(8,128)(2,1)}) %all-gather.9.cloned.1.call-update) | async-done | bytes 8388624 | tf_op jit(solution)/shard_map/all_gather | solution.py:810
  421.1 25.1 %shard_map.278 = (bf16[2048,512]{1,0:T(8,128)(2,1)S(1)}, bf16[2048,1024]{1,0:T(8,128)(2,1)}, bf16[2048,2048]{1,0:T(8,128)(2,1)}) custom-call(bf16[2048,2048]{1,0:T(8,128)(2,1)} %all-gather.9.cloned.1.call-done.rows_ref, bf16[2048,1024]{1,0:T(8,128)(2,1)} %bitcast.43.refs_1_.weight_ref, bf16[1024,2048]{1,0:T(8,128)(2,1)} %shard_map.276.turned_ref, ...), custom_call_target="tpu_custom_call" | custom-call | bytes 79200000 | tf_op jit(solution)/shard_map/pallas_call | solution.py:744
  448.0 10.1 %convolution_convert_fusion.6.refs_2_ = bf16[512,2048]{1,0:T(8,128)(2,1)} fusion(bf16[2048,512]{1,0:T(8,128)(2,1)} %copy-done.42, bf16[2048,2048]{1,0:T(8,128)(2,1)} %all-gather.7.cloned.1.call-done.refs_1_), kind=kOutput, calls=%fused_computation.30 | convolution fusion | flops 4296015872 | bytes 12582912 | tf_op jit(solution)/shard_map/dot_general | solution.py:224
  458.1 12.9 %convolution_convert_fusion.3.refs_1_ = bf16[2048,1024]{1,0:T(8,128)(2,1)} fusion(bf16[2048,2048]{1,0:T(8,128)(2,1)} %all-gather.9.cloned.1.call-done.rows_ref, bf16[2048,1024]{1,0:T(8,128)(2,1)S(1)} %copy-done.90), kind=kOutput, calls=%fused_computation.12 | convolution fusion | flops 8592031744 | bytes 16777216 | tf_op jit(solution)/shard_map/dot_general | solution.py:224
  471.0 64.8 %reduce-scatter.7.cloned.1.call-done.refs_0_ = bf16[256,2048]{1,0:T(8,128)(2,1)} async-done(((bf16[2048,2048]{1,0:T(8,128)(2,1)}), bf16[256,2048]{1,0:T(8,128)(2,1)}) %reduce-scatter.7.cloned.1.call-update) | async-done | bytes 1048592 | tf_op jit(solution)/shard_map/reduce_scatter | solution.py:813
  535.8 2.3 fusion.14
  545.2 2.6 dynamic-slice_bitcast_fusion.2
  550.8 5.7 collective-permute-done.21
  556.6 2.4 collective-permute-start.20
  558.9 6.8 convolution_convert_fusion.1.refs_0_
  565.7 3.5 collective-permute-done.22
  569.3 2.4 fusion.35.refs_2_.refs_0_
  571.6 18.7 %collective-permute-done.18 = bf16[512,1024]{1,0:T(8,128)(2,1)S(1)} collective-permute-done((bf16[512,1024]{1,0:T(8,128)(2,1)S(1)}, bf16[512,1024]{1,0:T(8,128)(2,1)S(1)}, u32[]{:S(2)}, u32[]{:S(2)}) %collective-permute-start.18) | collective-permute-done | bytes 1048608 | tf_op jit(solution)/shard_map/ppermute | solution.py:42
  590.3 20.3 %collective-permute-done.19 = bf16[512,1024]{1,0:T(8,128)(2,1)S(1)} collective-permute-done((bf16[512,1024]{1,0:T(8,128)(2,1)S(1)}, bf16[512,1024]{1,0:T(8,128)(2,1)S(1)}, u32[]{:S(2)}, u32[]{:S(2)}) %collective-permute-start.19) | collective-permute-done | bytes 1048608 | tf_op jit(solution)/shard_map/ppermute | solution.py:42
  610.6 3.1 fusion.22.refs_1_
  613.7 7.0 all-gather.11.cloned.1.call-done.refs_0_
  620.7 4.3 all-to-all-start.2
  625.2 8.4 fusion.82
  633.6 9.8 %convolution_convert_fusion.5 = bf16[512,2048]{1,0:T(8,128)(2,1)S(1)} fusion(bf16[2048,2048]{1,0:T(8,128)(2,1)} %shard_map.280.refs_1_, bf16[2048,128]{1,0:T(8,128)(2,1)S(1)} %bitcast.252, bf16[2048,384]{1,0:T(8,128)(2,1)S(1)} %copy-done.71), kind=kOutput, calls=%fused_computation.29 | convolution fusion | flops 4300210176 | bytes 12582912 | tf_op jit(solution)/shard_map/dot_general | solution.py:224
  643.7 2.2 copy-done.7
  654.7 2.4 collective-permute-start.26
  660.8 19.3 %shard_map.284 = (bf16[8,256,128]{2,1,0:T(8,128)(2,1)S(1)}, bf16[8,256,128]{2,1,0:T(8,128)(2,1)S(1)}, bf16[8,256,128]{2,1,0:T(8,128)(2,1)S(1)}) custom-call(f32[8,256,1792]{2,1,0:T(8,128)} %bitcast.259, f32[8,256,1792]{2,1,0:T(8,128)} %bitcast.260, f32[8,256,1792]{2,1,0:T(8,128)} %bitcast.261, f32[8,128,256]{2,1,0:T(8,128)S(1)} %copy-done.9, ...), custom_call_target="tpu_custom_call" | custom-call | bytes 68400000 | tf_op jit(solution)/shard_map/pallas_call | solution.py:704
  685.1 41.3 %shard_map.285 = (bf16[2048,1792]{1,0:T(8,128)(2,1)}, f32[8,896]{1,0:T(8,128)S(1)}, f32[8,128]{1,0:T(8,128)S(1)}, f32[8,384]{1,0:T(8,128)S(1)}) custom-call(f32[2048,1792]{1,0:T(8,128)} %fusion.78.mixed_ref.before_ref.refs_1_, f32[2048,1792]{1,0:T(8,128)} %fusion.78.mixed_ref.before_ref.refs_1_, f32[2048,8]{1,0:T(8,128)S(1)} %bitcast.246, ...), custom_call_target="tpu_custom_call" | custom-call | bytes 154800000 | tf_op jit(solution)/shard_map/pallas_call | solution.py:549
  726.4 21.5 %convolution_convert_fusion.refs_0_ = bf16[2048,2048]{1,0:T(8,128)(2,1)} fusion(bf16[2048,1792]{1,0:T(8,128)(2,1)} %shard_map.286.refs_0_, bf16[2048,1792]{1,0:T(8,128)(2,1)} %shard_map.257.refs_1_.refs_2_), kind=kOutput, calls=%fused_computation.7 | convolution fusion | flops 15036579840 | bytes 23068672 | tf_op jit(solution)/shard_map/dot_general | solution.py:220
  750.8 13.7 %add_convert_fusion.refs_1_ = bf16[2048,1024]{1,0:T(8,128)(2,1)S(1)} fusion(f32[2048,12]{1,0:T(8,128)S(1)} %bitcast.287, bf16[2048,1792]{1,0:T(8,128)(2,1)} %shard_map.288, bf16[2048,2048]{1,0:T(8,128)(2,1)} %all-gather.5.cloned.1.call-done.refs_1_, f32[2048]{0:T(1024)S(1)} %copy-done.77, f32[2048]{0:T(1024)S(1)} %copy-done.87), kind=kOutput, calls=%fused_computation.6 | convolution fusion | flops 8610906112 | bytes 16891904 | tf_op jit(solution)/shard_map/dot_general | solution.py:224
  769.5 12.3 %convolution_convert_fusion.4.refs_1_ = bf16[2048,768]{1,0:T(8,128)(2,1)} fusion(bf16[2048,1792]{1,0:T(8,128)(2,1)} %shard_map.288, bf16[2048,2048]{1,0:T(8,128)(2,1)} %all-gather.5.cloned.1.call-done.refs_1_, f32[2048]{0:T(1024)S(1)} %copy-done.77, f32[2048]{0:T(1024)S(1)} %copy-done.87), kind=kOutput, calls=%fused_computation.21 | convolution fusion | flops 6460801024 | bytes 14696448 | tf_op jit(solution)/shard_map/dot_general | solution.py:224
  781.8 8.2 collective-permute-done.43.refs_0_
  791.0 2.8 convert_element_type.383
  797.7 2.8 fusion.44
  806.9 8.8 collective-permute-done.42
  820.4 4.9 all-to-all-start.4
  832.4 2.7 shard_map.290.refs_1_
  843.9 7.8 collective-permute-done.32
  854.1 5.4 all-to-all-done.4
  859.6 3.8 all-to-all-start.3
  880.3 2.4 collective-permute-start.39
  882.7 3.5 fusion.18.in_ref
  (505 shorter events, 179.8 us)
Async XLA Ops:
  7.2 131.8 %copy-start = (f32[3,48]{1,0:T(4,128)S(1)}, f32[3,48]{1,0:T(4,128)}, u32[]{:S(2)}) copy-start(f32[3,48]{1,0:T(4,128)} %param.21) | copy-start | bytes 1732
  15.4 41.3 %all-to-all-start = ((bf16[8,64,1408]{2,1,0:T(8,128)(2,1)}), bf16[8,64,1408]{2,1,0:T(8,128)(2,1)S(1)}, u32[]{:S(2)}, u32[]{:S(2)}) async-start(bf16[8,64,1408]{2,1,0:T(8,128)(2,1)} %shard_map.255), calls=%async_computation | async-start | bytes 2883584 | tf_op jit(solution)/shard_map/all_to_all | solution.py:70
  21.7 117.3 %all-gather.5.cloned.1.call-start = ((), (), s32[]{:S(2)}) async-start(), calls=%async_computation.9 | async-start | bytes 9437184 | tf_op jit(solution)/shard_map/all_gather | solution.py:810
  57.9 186.8 %all-gather.7.cloned.1.call-start = ((), (), s32[]{:S(2)}) async-start(), calls=%async_computation.10 | async-start | bytes 9437184 | tf_op jit(solution)/shard_map/all_gather | solution.py:810
  58.8 33.4 %collective-permute-start = (bf16[8,64,1408]{2,1,0:T(8,128)(2,1)}, bf16[8,64,1408]{2,1,0:T(8,128)(2,1)S(1)}, u32[]{:S(2)}, u32[]{:S(2)}) collective-permute-start(bf16[8,64,1408]{2,1,0:T(8,128)(2,1)} %copy-done.54), channel_id=1, source_target_pairs={{0,1},{1,0},{2,3},{3,2},{4,5},{5,4},{6,7},{7,6},{8,9},{9,8},{10,11... | collective-permute-start | bytes 4325384 | tf_op jit(solution)/shard_map/ppermute | solution.py:42
  60.3 33.5 %collective-permute-start.1 = (bf16[8,64,1408]{2,1,0:T(8,128)(2,1)}, bf16[8,64,1408]{2,1,0:T(8,128)(2,1)S(1)}, u32[]{:S(2)}, u32[]{:S(2)}) collective-permute-start(bf16[8,64,1408]{2,1,0:T(8,128)(2,1)} %copy-done.54), channel_id=1, source_target_pairs={{0,2},{1,3},{2,0},{3,1},{4,6},{5,7},{6,4},{7,5},{8,10},{9,11},{10,... | collective-permute-start | bytes 4325384 | tf_op jit(solution)/shard_map/ppermute | solution.py:42
  92.2 17.0 %collective-permute-start.2 = (bf16[4,64,1408]{2,1,0:T(8,128)(2,1)S(1)}, bf16[4,64,1408]{2,1,0:T(8,128)(2,1)S(1)}, u32[]{:S(2)}, u32[]{:S(2)}) collective-permute-start(bf16[4,64,1408]{2,1,0:T(8,128)(2,1)S(1)} %slice.337), channel_id=1, source_target_pairs={{0,2},{1,3},{2,0},{3,1},{4,6},{5,7},{6,4},{7,5},{8,10},{9,11},{10,... | collective-permute-start | bytes 2162696 | tf_op jit(solution)/shard_map/ppermute | solution.py:42
  93.9 16.7 %collective-permute-start.3 = (bf16[4,64,1408]{2,1,0:T(8,128)(2,1)S(1)}, bf16[4,64,1408]{2,1,0:T(8,128)(2,1)S(1)}, u32[]{:S(2)}, u32[]{:S(2)}) collective-permute-start(bf16[4,64,1408]{2,1,0:T(8,128)(2,1)S(1)} %slice.338), channel_id=1, source_target_pairs={{0,1},{1,0},{2,3},{3,2},{4,5},{5,4},{6,7},{7,6},{8,9},{9,8},{10,11... | collective-permute-start | bytes 2162696 | tf_op jit(solution)/shard_map/ppermute | solution.py:42
  116.3 11.1 %collective-permute-start.4 = (bf16[2048,384]{1,0:T(8,128)(2,1)}, bf16[2048,384]{1,0:T(8,128)(2,1)}, u32[]{:S(2)}, u32[]{:S(2)}) collective-permute-start(bf16[2048,384]{1,0:T(8,128)(2,1)} %pad_maximum_fusion.1), channel_id=1, source_target_pairs={{0,4},{4,0},{8,12},{12,8},{16,20},{20,16},{24,28},{28,24},{1,5},{5... | collective-permute-start | bytes 4718600 | tf_op jit(solution)/shard_map/ppermute | solution.py:42
  144.3 59.0 %collective-permute-start.11 = (bf16[128,2048]{1,0:T(8,128)(2,1)}, bf16[128,2048]{1,0:T(8,128)(2,1)}, u32[]{:S(2)}, u32[]{:S(2)}) collective-permute-start(bf16[128,2048]{1,0:T(8,128)(2,1)} %shard_map.264.refs_0_), channel_id=1, source_target_pairs={{0,3},{1,2},{2,1},{3,0},{4,7},{5,6},{6,5},{7,4},{8,11},{9,10},{10,... | collective-permute-start | bytes 1572872 | tf_op jit(solution)/shard_map/ppermute | solution.py:42
  146.8 57.4 %collective-permute-start.10 = (bf16[128,2048]{1,0:T(8,128)(2,1)}, bf16[128,2048]{1,0:T(8,128)(2,1)}, u32[]{:S(2)}, u32[]{:S(2)}) collective-permute-start(bf16[128,2048]{1,0:T(8,128)(2,1)} %shard_map.264.refs_0_), channel_id=1, source_target_pairs={{0,2},{1,3},{2,0},{3,1},{4,6},{5,7},{6,4},{7,5},{8,10},{9,11},{10,... | collective-permute-start | bytes 1572872 | tf_op jit(solution)/shard_map/ppermute | solution.py:42
  147.3 56.9 %collective-permute-start.9 = (bf16[128,2048]{1,0:T(8,128)(2,1)}, bf16[128,2048]{1,0:T(8,128)(2,1)}, u32[]{:S(2)}, u32[]{:S(2)}) collective-permute-start(bf16[128,2048]{1,0:T(8,128)(2,1)} %shard_map.264.refs_0_), channel_id=1, source_target_pairs={{0,1},{1,0},{2,3},{3,2},{4,5},{5,4},{6,7},{7,6},{8,9},{9,8},{10,11... | collective-permute-start | bytes 1572872 | tf_op jit(solution)/shard_map/ppermute | solution.py:42
  147.8 65.4 %all-to-all-start.1 = ((bf16[8,64,1024]{2,1,0:T(8,128)(2,1)}), bf16[8,64,1024]{2,1,0:T(8,128)(2,1)}, u32[]{:S(2)}, u32[]{:S(2)}) async-start(bf16[8,64,1024]{2,1,0:T(8,128)(2,1)} %shard_map.260), calls=%async_computation.1 | async-start | bytes 2097152 | tf_op jit(solution)/shard_map/all_to_all | solution.py:70
  152.1 182.9 %reduce-scatter.5.cloned.1.call-start = ((), (), s32[]{:S(2)}) async-start(), calls=%async_computation.11 | async-start | bytes 9437184 | tf_op jit(solution)/shard_map/reduce_scatter | solution.py:813
  202.9 5.1 collective-permute-start.5
  208.0 22.4 %collective-permute-start.6 = (f32[2048]{0:T(1024)S(1)}, f32[2048]{0:T(1024)S(1)}, u32[]{:S(2)}, u32[]{:S(2)}) collective-permute-start(f32[2048]{0:T(1024)S(1)} %add.275), channel_id=1, source_target_pairs={{0,8},{4,12},{8,0},{12,4},{16,24},{20,28},{24,16},{28,20},{1,9},{5... | collective-permute-start | bytes 24584 | tf_op jit(solution)/shard_map/ppermute | solution.py:42
  209.9 20.6 %collective-permute-start.7 = (f32[2048]{0:T(1024)S(1)}, f32[2048]{0:T(1024)S(1)}, u32[]{:S(2)}, u32[]{:S(2)}) collective-permute-start(f32[2048]{0:T(1024)S(1)} %add.275), channel_id=1, source_target_pairs={{0,16},{4,20},{8,24},{12,28},{16,0},{20,4},{24,8},{28,12},{1,17},{... | collective-permute-start | bytes 24584 | tf_op jit(solution)/shard_map/ppermute | solution.py:42
  212.2 18.3 %collective-permute-start.8 = (f32[2048]{0:T(1024)S(1)}, f32[2048]{0:T(1024)S(1)}, u32[]{:S(2)}, u32[]{:S(2)}) collective-permute-start(f32[2048]{0:T(1024)S(1)} %add.275), channel_id=1, source_target_pairs={{0,24},{4,28},{8,16},{12,20},{16,8},{20,12},{24,0},{28,4},{1,25},{... | collective-permute-start | bytes 24584 | tf_op jit(solution)/shard_map/ppermute | solution.py:42
  244.7 176.4 %all-gather.9.cloned.1.call-start = ((), (), s32[]{:S(2)}) async-start(), calls=%async_computation.12 | async-start | bytes 9437184 | tf_op jit(solution)/shard_map/all_gather | solution.py:810
  246.8 291.4 %copy-start.73 = (f32[2048]{0:T(1024)}, f32[2048]{0:T(1024)S(1)}, u32[]{:S(2)}) copy-start(f32[2048]{0:T(1024)S(1)} %mul.308) | copy-start | bytes 24580
  246.8 15.1 %collective-permute-start.15 = (bf16[128,2048]{1,0:T(8,128)(2,1)}, bf16[128,2048]{1,0:T(8,128)(2,1)}, u32[]{:S(2)}, u32[]{:S(2)}) collective-permute-start(bf16[128,2048]{1,0:T(8,128)(2,1)} %shard_map.274), channel_id=1, source_target_pairs={{0,1},{1,0},{2,3},{3,2},{4,5},{5,4},{6,7},{7,6},{8,9},{9,8},{10,11... | collective-permute-start | bytes 1572872 | tf_op jit(solution)/shard_map/ppermute | solution.py:42
  248.3 26.3 %collective-permute-start.16 = (bf16[128,2048]{1,0:T(8,128)(2,1)}, bf16[128,2048]{1,0:T(8,128)(2,1)}, u32[]{:S(2)}, u32[]{:S(2)}) collective-permute-start(bf16[128,2048]{1,0:T(8,128)(2,1)} %shard_map.274), channel_id=1, source_target_pairs={{0,2},{1,3},{2,0},{3,1},{4,6},{5,7},{6,4},{7,5},{8,10},{9,11},{10,... | collective-permute-start | bytes 1572872 | tf_op jit(solution)/shard_map/ppermute | solution.py:42
  249.7 26.0 %collective-permute-start.17 = (bf16[128,2048]{1,0:T(8,128)(2,1)}, bf16[128,2048]{1,0:T(8,128)(2,1)}, u32[]{:S(2)}, u32[]{:S(2)}) collective-permute-start(bf16[128,2048]{1,0:T(8,128)(2,1)} %shard_map.274), channel_id=1, source_target_pairs={{0,3},{1,2},{2,1},{3,0},{4,7},{5,6},{6,5},{7,4},{8,11},{9,10},{10,... | collective-permute-start | bytes 1572872 | tf_op jit(solution)/shard_map/ppermute | solution.py:42
  250.3 45.2 %collective-permute-start.12 = (bf16[8,64,1024]{2,1,0:T(8,128)(2,1)}, bf16[8,64,1024]{2,1,0:T(8,128)(2,1)S(1)}, u32[]{:S(2)}, u32[]{:S(2)}) collective-permute-start(bf16[8,64,1024]{2,1,0:T(8,128)(2,1)} %shard_map.272), channel_id=1, source_target_pairs={{0,1},{1,0},{2,3},{3,2},{4,5},{5,4},{6,7},{7,6},{8,9},{9,8},{10,11... | collective-permute-start | bytes 3145736 | tf_op jit(solution)/shard_map/ppermute | solution.py:42
  251.7 66.7 %collective-permute-start.13 = (bf16[8,64,1024]{2,1,0:T(8,128)(2,1)}, bf16[8,64,1024]{2,1,0:T(8,128)(2,1)S(1)}, u32[]{:S(2)}, u32[]{:S(2)}) collective-permute-start(bf16[8,64,1024]{2,1,0:T(8,128)(2,1)} %shard_map.272), channel_id=1, source_target_pairs={{0,2},{1,3},{2,0},{3,1},{4,6},{5,7},{6,4},{7,5},{8,10},{9,11},{10,... | collective-permute-start | bytes 3145736 | tf_op jit(solution)/shard_map/ppermute | solution.py:42
  261.9 57.7 %collective-permute-start.14 = (bf16[8,64,1024]{2,1,0:T(8,128)(2,1)}, bf16[8,64,1024]{2,1,0:T(8,128)(2,1)S(1)}, u32[]{:S(2)}, u32[]{:S(2)}) collective-permute-start(bf16[8,64,1024]{2,1,0:T(8,128)(2,1)} %shard_map.272), channel_id=1, source_target_pairs={{0,3},{1,2},{2,1},{3,0},{4,7},{5,6},{6,5},{7,4},{8,11},{9,10},{10,... | collective-permute-start | bytes 3145736 | tf_op jit(solution)/shard_map/ppermute | solution.py:42
  276.8 43.8 %copy-start.61 = (bf16[4,128,2048]{2,1,0:T(8,128)(2,1)}, bf16[4,128,2048]{2,1,0:T(8,128)(2,1)S(1)}, u32[]{:S(2)}) copy-start(bf16[4,128,2048]{2,1,0:T(8,128)(2,1)S(1)} %bitcast_dynamic-update-slice_fusion.7) | copy-start | bytes 6291460
  337.9 200.3 %copy-start.79 = (f32[256]{0:T(256)}, f32[256]{0:T(256)S(1)}, u32[]{:S(2)}) copy-start(f32[256]{0:T(256)S(1)} %get-tuple-element.162) | copy-start | bytes 3076
  337.9 200.3 %copy-start.82 = (f32[256]{0:T(256)}, f32[256]{0:T(256)S(1)}, u32[]{:S(2)}) copy-start(f32[256]{0:T(256)S(1)} %get-tuple-element.161) | copy-start | bytes 3076
  340.5 195.3 %reduce-scatter.7.cloned.1.call-start = ((), (), s32[]{:S(2)}) async-start(), calls=%async_computation.13 | async-start | bytes 9437184 | tf_op jit(solution)/shard_map/reduce_scatter | solution.py:813
  447.5 173.1 %all-gather.11.cloned.1.call-start = ((), (), s32[]{:S(2)}) async-start(), calls=%async_computation.14 | async-start | bytes 9437184 | tf_op jit(solution)/shard_map/all_gather | solution.py:810
  471.0 64.8 %copy-start.45 = (bf16[256,2048]{1,0:T(8,128)(2,1)S(1)}, bf16[256,2048]{1,0:T(8,128)(2,1)}, u32[]{:S(2)}) copy-start(bf16[256,2048]{1,0:T(8,128)(2,1)} %shard_map.275) | copy-start | bytes 3145732
  540.1 207.8 %reduce-scatter.9.cloned.1.call-start = ((), (), s32[]{:S(2)}) async-start(), calls=%async_computation.15 | async-start | bytes 9437184 | tf_op jit(solution)/shard_map/reduce_scatter | solution.py:1038
  541.6 14.9 %collective-permute-start.21 = (bf16[128,2048]{1,0:T(8,128)(2,1)S(1)}, bf16[128,2048]{1,0:T(8,128)(2,1)S(1)}, u32[]{:S(2)}, u32[]{:S(2)}) collective-permute-start(bf16[128,2048]{1,0:T(8,128)(2,1)S(1)} %get-tuple-element.149), channel_id=1, source_target_pairs={{0,1},{1,0},{2,3},{3,2},{4,5},{5,4},{6,7},{7,6},{8,9},{9,8},{10,11... | collective-permute-start | bytes 1572872 | tf_op jit(solution)/shard_map/ppermute | solution.py:42
  543.1 26.1 %collective-permute-start.22 = (bf16[128,2048]{1,0:T(8,128)(2,1)S(1)}, bf16[128,2048]{1,0:T(8,128)(2,1)S(1)}, u32[]{:S(2)}, u32[]{:S(2)}) collective-permute-start(bf16[128,2048]{1,0:T(8,128)(2,1)S(1)} %get-tuple-element.151), channel_id=1, source_target_pairs={{0,2},{1,3},{2,0},{3,1},{4,6},{5,7},{6,4},{7,5},{8,10},{9,11},{10,... | collective-permute-start | bytes 1572872 | tf_op jit(solution)/shard_map/ppermute | solution.py:42
  544.6 24.6 %collective-permute-start.23 = (bf16[128,2048]{1,0:T(8,128)(2,1)S(1)}, bf16[128,2048]{1,0:T(8,128)(2,1)S(1)}, u32[]{:S(2)}, u32[]{:S(2)}) collective-permute-start(bf16[128,2048]{1,0:T(8,128)(2,1)S(1)} %get-tuple-element.150), channel_id=1, source_target_pairs={{0,3},{1,2},{2,1},{3,0},{4,7},{5,6},{6,5},{7,4},{8,11},{9,10},{10,... | collective-permute-start | bytes 1572872 | tf_op jit(solution)/shard_map/ppermute | solution.py:42
  547.8 42.5 %collective-permute-start.18 = (bf16[512,1024]{1,0:T(8,128)(2,1)S(1)}, bf16[512,1024]{1,0:T(8,128)(2,1)S(1)}, u32[]{:S(2)}, u32[]{:S(2)}) collective-permute-start(bf16[512,1024]{1,0:T(8,128)(2,1)S(1)} %get-tuple-element.133), channel_id=1, source_target_pairs={{0,1},{1,0},{2,3},{3,2},{4,5},{5,4},{6,7},{7,6},{8,9},{9,8},{10,11... | collective-permute-start | bytes 3145736 | tf_op jit(solution)/shard_map/ppermute | solution.py:42
  549.4 61.2 %collective-permute-start.19 = (bf16[512,1024]{1,0:T(8,128)(2,1)S(1)}, bf16[512,1024]{1,0:T(8,128)(2,1)S(1)}, u32[]{:S(2)}, u32[]{:S(2)}) collective-permute-start(bf16[512,1024]{1,0:T(8,128)(2,1)S(1)} %get-tuple-element.135), channel_id=1, source_target_pairs={{0,2},{1,3},{2,0},{3,1},{4,6},{5,7},{6,4},{7,5},{8,10},{9,11},{10,... | collective-permute-start | bytes 3145736 | tf_op jit(solution)/shard_map/ppermute | solution.py:42
  556.6 54.0 %collective-permute-start.20 = (bf16[512,1024]{1,0:T(8,128)(2,1)S(1)}, bf16[512,1024]{1,0:T(8,128)(2,1)S(1)}, u32[]{:S(2)}, u32[]{:S(2)}) collective-permute-start(bf16[512,1024]{1,0:T(8,128)(2,1)S(1)} %get-tuple-element.134), channel_id=1, source_target_pairs={{0,3},{1,2},{2,1},{3,0},{4,7},{5,6},{6,5},{7,4},{8,11},{9,10},{10,... | collective-permute-start | bytes 3145736 | tf_op jit(solution)/shard_map/ppermute | solution.py:42
  620.7 105.7 %all-to-all-start.2 = ((bf16[8,64,1024]{2,1,0:T(8,128)(2,1)}), bf16[8,64,1024]{2,1,0:T(8,128)(2,1)}, u32[]{:S(2)}, u32[]{:S(2)}) async-start(bf16[8,64,1024]{2,1,0:T(8,128)(2,1)} %bitcast.66), calls=%async_computation.5 | async-start | bytes 2097152 | tf_op jit(solution)/shard_map/all_to_all | solution.py:70
  625.0 242.5 %reduce-scatter.11.cloned.1.call-start = ((), (), s32[]{:S(2)}) async-start(), calls=%async_computation.16 | async-start | bytes 9437184 | tf_op jit(solution)/shard_map/reduce_scatter | solution.py:1124
  647.0 5.3 collective-permute-start.24
  649.5 76.8 %collective-permute-start.28 = (bf16[128,2048]{1,0:T(8,128)(2,1)}, bf16[128,2048]{1,0:T(8,128)(2,1)}, u32[]{:S(2)}, u32[]{:S(2)}) collective-permute-start(bf16[128,2048]{1,0:T(8,128)(2,1)} %get-tuple-element.147), channel_id=1, source_target_pairs={{0,1},{1,0},{2,3},{3,2},{4,5},{5,4},{6,7},{7,6},{8,9},{9,8},{10,11... | collective-permute-start | bytes 1572872 | tf_op jit(solution)/shard_map/ppermute | solution.py:42
  650.9 75.5 %collective-permute-start.29 = (bf16[128,2048]{1,0:T(8,128)(2,1)}, bf16[128,2048]{1,0:T(8,128)(2,1)}, u32[]{:S(2)}, u32[]{:S(2)}) collective-permute-start(bf16[128,2048]{1,0:T(8,128)(2,1)} %get-tuple-element.148), channel_id=1, source_target_pairs={{0,2},{1,3},{2,0},{3,1},{4,6},{5,7},{6,4},{7,5},{8,10},{9,11},{10,... | collective-permute-start | bytes 1572872 | tf_op jit(solution)/shard_map/ppermute | solution.py:42
  652.9 27.4 %collective-permute-start.25 = (f32[2048]{0:T(1024)}, f32[2048]{0:T(1024)S(1)}, u32[]{:S(2)}, u32[]{:S(2)}) collective-permute-start(f32[2048]{0:T(1024)} %add.291.refs_1_), channel_id=1, source_target_pairs={{0,8},{4,12},{8,0},{12,4},{16,24},{20,28},{24,16},{28,20},{1,9},{5... | collective-permute-start | bytes 24584 | tf_op jit(solution)/shard_map/ppermute | solution.py:42
  654.7 26.4 %collective-permute-start.26 = (f32[2048]{0:T(1024)}, f32[2048]{0:T(1024)S(1)}, u32[]{:S(2)}, u32[]{:S(2)}) collective-permute-start(f32[2048]{0:T(1024)} %add.291.refs_1_), channel_id=1, source_target_pairs={{0,16},{4,20},{8,24},{12,28},{16,0},{20,4},{24,8},{28,12},{1,17},{... | collective-permute-start | bytes 24584 | tf_op jit(solution)/shard_map/ppermute | solution.py:42
  657.1 24.1 %collective-permute-start.27 = (f32[2048]{0:T(1024)}, f32[2048]{0:T(1024)S(1)}, u32[]{:S(2)}, u32[]{:S(2)}) collective-permute-start(f32[2048]{0:T(1024)} %add.291.refs_1_), channel_id=1, source_target_pairs={{0,24},{4,28},{8,16},{12,20},{16,8},{20,12},{24,0},{28,4},{1,25},{... | collective-permute-start | bytes 24584 | tf_op jit(solution)/shard_map/ppermute | solution.py:42
  680.3 46.1 %collective-permute-start.30 = (bf16[128,2048]{1,0:T(8,128)(2,1)}, bf16[128,2048]{1,0:T(8,128)(2,1)}, u32[]{:S(2)}, u32[]{:S(2)}) collective-permute-start(bf16[128,2048]{1,0:T(8,128)(2,1)} %get-tuple-element.146), channel_id=1, source_target_pairs={{0,3},{1,2},{2,1},{3,0},{4,7},{5,6},{6,5},{7,4},{8,11},{9,10},{10,... | collective-permute-start | bytes 1572872 | tf_op jit(solution)/shard_map/ppermute | solution.py:42
  766.5 23.5 %collective-permute-start.43 = (bf16[2,256,1024]{2,1,0:T(8,128)(2,1)S(1)}, bf16[2,256,1024]{2,1,0:T(8,128)(2,1)S(1)}, u32[]{:S(2)}, u32[]{:S(2)}) collective-permute-start(bf16[2,256,1024]{2,1,0:T(8,128)(2,1)S(1)} %pad_maximum_fusion.7), channel_id=1, source_target_pairs={{0,2},{1,3},{2,0},{3,1},{4,6},{5,7},{6,4},{7,5},{8,10},{9,11},{10,... | collective-permute-start | bytes 3145736 | tf_op jit(solution)/shard_map/ppermute | solution.py:42
  768.0 25.8 %collective-permute-start.41 = (bf16[2,256,1024]{2,1,0:T(8,128)(2,1)S(1)}, bf16[2,256,1024]{2,1,0:T(8,128)(2,1)S(1)}, u32[]{:S(2)}, u32[]{:S(2)}) collective-permute-start(bf16[2,256,1024]{2,1,0:T(8,128)(2,1)S(1)} %pad_maximum_fusion.6), channel_id=1, source_target_pairs={{0,1},{1,0},{2,3},{3,2},{4,5},{5,4},{6,7},{7,6},{8,9},{9,8},{10,11... | collective-permute-start | bytes 3145736 | tf_op jit(solution)/shard_map/ppermute | solution.py:42
  800.5 15.2 %collective-permute-start.42 = (bf16[256,1024]{1,0:T(8,128)(2,1)}, bf16[256,1024]{1,0:T(8,128)(2,1)}, u32[]{:S(2)}, u32[]{:S(2)}) collective-permute-start(bf16[256,1024]{1,0:T(8,128)(2,1)} %get-tuple-element.127), channel_id=1, source_target_pairs={{0,2},{1,3},{2,0},{3,1},{4,6},{5,7},{6,4},{7,5},{8,10},{9,11},{10,... | collective-permute-start | bytes 1572872 | tf_op jit(solution)/shard_map/ppermute | solution.py:42
  802.1 15.2 %collective-permute-start.44 = (bf16[256,1024]{1,0:T(8,128)(2,1)}, bf16[256,1024]{1,0:T(8,128)(2,1)}, u32[]{:S(2)}, u32[]{:S(2)}) collective-permute-start(bf16[256,1024]{1,0:T(8,128)(2,1)} %get-tuple-element.128), channel_id=1, source_target_pairs={{0,1},{1,0},{2,3},{3,2},{4,5},{5,4},{6,7},{7,6},{8,9},{9,8},{10,11... | collective-permute-start | bytes 1572872 | tf_op jit(solution)/shard_map/ppermute | solution.py:42
  804.9 30.2 %collective-permute-start.33 = (bf16[2,256,768]{2,1,0:T(8,128)(2,1)}, bf16[2,256,768]{2,1,0:T(8,128)(2,1)}, u32[]{:S(2)}, u32[]{:S(2)}) collective-permute-start(bf16[2,256,768]{2,1,0:T(8,128)(2,1)} %pad_maximum_fusion.10), channel_id=1, source_target_pairs={{0,2},{1,3},{2,0},{3,1},{4,6},{5,7},{6,4},{7,5},{8,10},{9,11},{10,... | collective-permute-start | bytes 2359304 | tf_op jit(solution)/shard_map/ppermute | solution.py:42
  806.4 29.9 %collective-permute-start.31 = (bf16[2,256,768]{2,1,0:T(8,128)(2,1)}, bf16[2,256,768]{2,1,0:T(8,128)(2,1)S(1)}, u32[]{:S(2)}, u32[]{:S(2)}) collective-permute-start(bf16[2,256,768]{2,1,0:T(8,128)(2,1)} %pad_maximum_fusion.9), channel_id=1, source_target_pairs={{0,1},{1,0},{2,3},{3,2},{4,5},{5,4},{6,7},{7,6},{8,9},{9,8},{10,11... | collective-permute-start | bytes 2359304 | tf_op jit(solution)/shard_map/ppermute | solution.py:42
  820.4 39.2 %all-to-all-start.4 = ((bf16[8,64,1024]{2,1,0:T(8,128)(2,1)}), bf16[8,64,1024]{2,1,0:T(8,128)(2,1)}, u32[]{:S(2)}, u32[]{:S(2)}) async-start(bf16[8,64,1024]{2,1,0:T(8,128)(2,1)} %bitcast.97), calls=%async_computation.8 | async-start | bytes 2097152 | tf_op jit(solution)/shard_map/all_to_all | solution.py:70
  839.9 11.7 %collective-permute-start.32 = (bf16[256,768]{1,0:T(8,128)(2,1)S(1)}, bf16[256,768]{1,0:T(8,128)(2,1)S(1)}, u32[]{:S(2)}, u32[]{:S(2)}) collective-permute-start(bf16[256,768]{1,0:T(8,128)(2,1)S(1)} %get-tuple-element.138), channel_id=1, source_target_pairs={{0,2},{1,3},{2,0},{3,1},{4,6},{5,7},{6,4},{7,5},{8,10},{9,11},{10,... | collective-permute-start | bytes 1179656 | tf_op jit(solution)/shard_map/ppermute | solution.py:42
  840.5 11.3 %collective-permute-start.34 = (bf16[256,768]{1,0:T(8,128)(2,1)S(1)}, bf16[256,768]{1,0:T(8,128)(2,1)S(1)}, u32[]{:S(2)}, u32[]{:S(2)}) collective-permute-start(bf16[256,768]{1,0:T(8,128)(2,1)S(1)} %get-tuple-element.139), channel_id=1, source_target_pairs={{0,1},{1,0},{2,3},{3,2},{4,5},{5,4},{6,7},{7,6},{8,9},{9,8},{10,11... | collective-permute-start | bytes 1179656 | tf_op jit(solution)/shard_map/ppermute | solution.py:42
  859.6 29.9 %all-to-all-start.3 = ((bf16[8,64,768]{2,1,0:T(8,128)(2,1)}), bf16[8,64,768]{2,1,0:T(8,128)(2,1)S(1)}, u32[]{:S(2)}, u32[]{:S(2)}) async-start(bf16[8,64,768]{2,1,0:T(8,128)(2,1)} %bitcast.85), calls=%async_computation.7 | async-start | bytes 1572864 | tf_op jit(solution)/shard_map/all_to_all | solution.py:70
  867.6 5.3 collective-permute-start.35
  873.6 3.6 collective-permute-start.36
  877.2 1.1 collective-permute-start.37
  878.3 9.9 %collective-permute-start.38 = (f32[144]{0:T(256)S(1)}, f32[144]{0:T(256)S(1)}, u32[]{:S(2)}, u32[]{:S(2)}) collective-permute-start(f32[144]{0:T(256)S(1)} %add.311), channel_id=1, source_target_pairs={{0,8},{4,12},{8,0},{12,4},{16,24},{20,28},{24,16},{28,20},{1,9},{5... | collective-permute-start | bytes 1736 | tf_op jit(solution)/shard_map/ppermute | solution.py:42
  880.3 7.9 collective-permute-start.39
  882.7 5.5 collective-permute-start.40
  (85 other events, 511.3 us)
Sparse Core Ops, SparseCore 0:
  58.0 80.9 all-gather.4
  141.1 103.4 all-gather.6
  246.9 87.9 reduce-scatter.4
  340.7 80.4 all-gather.8
  447.6 88.1 reduce-scatter.6
  540.2 80.3 all-gather.10
  622.9 104.2 reduce-scatter.8
  748.0 97.2 reduce-scatter.10

commit v5 on v4

--- a/solution.py
+++ b/solution.py
@@ -1112,7 +1112,20 @@
     ).astype(bf16)
     zx_part = over_dp(zx_total, True, (rest_total,))
     zx_sum = to_owners(zx_part)
-    rest_sum = to_owners(over_dp(rest_total, True, (zx_total,)))
+    rest_part = over_dp(rest_total, True, (zx_total,))
+    at_kv = at_heads + ATT_DIM
+    first_part = jnp.concatenate(
+        [rest_part[:, :STATE], rest_part[:, at_kv : at_kv + ATT_DIM]], axis=1
+    )
+    second_part = jnp.concatenate(
+        [rest_part[:, STATE:at_steps], rest_part[:, at_kv + ATT_DIM :]], axis=1
+    )
+    side = jnp.where(odd_place, second_part, first_part).astype(f32) + permuted(
+        jnp.where(odd_place, first_part, second_part), "seq", 1
+    ).astype(f32)
+    rest_sum = to_owners(
+        jnp.concatenate([side.astype(bf16), rest_part[:, at_steps:at_kv]], axis=1)
+    )
     gu_sum, down_grad = after(gu_sum, rest_total), after(down_grad, rest_total)
     gate_up_grad = assembled(
         (owner, 2 * FF), f32, [(0, cube, flat) for flat, cube in gu_moves], gu_sum
@@ -1138,12 +1151,10 @@
     token_grad = plain_order(token_part + hidden_grad)
     zx_sum = after(zx_sum, token_grad, head_g)
 
-    bc_sum = jnp.sum(rest_sum[:, :, :at_steps].astype(f32), axis=0)
-    step_sum = (
-        rest_sum[:, :, at_steps : at_steps + heads]
-        .transpose(1, 0, 2)
-        .reshape(owner, HEADS)
-    )
+    at_own = STATE + ATT_DIM
+    halves = rest_sum[:, :, :STATE].astype(f32).reshape(n // 2, 2, owner, STATE).sum(axis=0)
+    bc_sum = jnp.concatenate([halves[0], halves[1]], axis=1)
+    step_sum = rest_sum[:, :, at_own : at_own + heads].transpose(1, 0, 2).reshape(owner, HEADS)
     moves = []
     for k in range(n):
         for half in range(2):
@@ -1153,17 +1164,17 @@
     moves.append((1, (every, every), (every, slice(2 * INNER, 2 * INNER + 2 * STATE))))
     moves.append((2, (every, every), (every, slice(2 * INNER + 2 * STATE, PROJ))))
     mixer_in_grad = assembled((owner, PROJ), f32, moves, zx_sum, bc_sum, step_sum)
-    head_sum = rest_sum[:, :, at_heads:].astype(f32)
-    head_sum = [head_sum[:, :, k * ATT_DIM : (k + 1) * ATT_DIM] for k in range(3)]
-    q_sum = head_sum[0].reshape(ATT_HEADS, parts, owner, ATT_DIM).sum(axis=1)
-    k_sum = head_sum[1].reshape(KV_HEADS, n // KV_HEADS, owner, ATT_DIM).sum(axis=1)
-    v_sum = head_sum[2].reshape(KV_HEADS, n // KV_HEADS, owner, ATT_DIM).sum(axis=1)
+    q_sum = rest_sum[:, :, at_own + DT_PAD :].astype(f32)
+    q_sum = q_sum.reshape(ATT_HEADS, parts, owner, ATT_DIM).sum(axis=1)
+    kv_sum = rest_sum[:, :, STATE:at_own].astype(f32)
+    kv_sum = kv_sum.reshape(KV_HEADS, n // (2 * KV_HEADS), 2, owner, ATT_DIM).sum(axis=1)
+    k_sum, v_sum = kv_sum[:, 0], kv_sum[:, 1]
     attn_qkv_grad = (
         jnp.concatenate([q_sum, k_sum, v_sum]).transpose(1, 0, 2).reshape(owner, -1)
     )
 
     vectors = jnp.sum(
-        rest_sum[:, :, at_steps + heads : at_steps + heads + vector_cols].astype(f32), axis=0
+        rest_sum[:, :, at_own + heads : at_own + heads + vector_cols].astype(f32), axis=0
     ).reshape(-1)[:vector_count]
     ends = [(CONV + 1) * tap_count, (CONV + 1) * tap_count + mixer_gain.shape[0]]
     conv_own = vectors[: ends[0]].reshape(CONV + 1, tap_count)

time: 913 us -> 916 us (level)
    unnamed x195 -> x203, local copies, waits for them, and re-layouts: 51.3 us -> 52.9 us
    ppermute x45 -> x46, starting transfers between devices: 57 us -> 56.8 us  [permuted(): return lax.ppermute(value, axis, pairs)]
    ppermute x45 -> x46, waiting for transfers between devices: 173 us -> 173 us  [permuted(): return lax.ppermute(value, axis, pairs)]
  transfers between devices with their start and end apart: 58 -> 59, of which waited for: 26 -> 26; matrix products, arithmetic and copies ran while one was open for 27% -> 28% of each run, Pallas kernels for 12% -> 12%
where the time goes in v5:
time: 916 us; the launch traced here: 905 us
  waiting for transfers between devices  365 us (40%)
  matrix products  137 us (15%)
  Pallas kernels  132 us (14%)
  local copies, waits for them, and re-layouts  102 us (11%)
  starting transfers between devices  81.7 us (9%)
  other arithmetic  70.9 us (8%)
  between operations  16.2 us (2%)
    ppermute x46, waiting for transfers between devices, permuted(): return lax.ppermute(value, axis, pairs)  173 us
    reduce_scatter x2, waiting for transfers between devices, scattered(): lax.psum_scatter(value.astype(bf16), 'seq', scatter_dimension=0, tiled=True)  79.1 us
    all_gather x4, waiting for transfers between devices, gathered(): return lax.all_gather(value, 'seq', axis=0, tiled=True)  77.8 us
    dot_general x5, matrix products, cross(): lax.dot_general(left, right, (((0,), (0,)), ((), ())), preferred_element_...  58.8 us
    ppermute x46, starting transfers between devices, permuted(): return lax.ppermute(value, axis, pairs)  56.8 us
    unnamed x203, local copies, waits for them, and re-layouts  52.9 us
    pallas_call x1, Pallas kernels, ssd_backward(): pl.pallas_call(ssd_backward_kernel, grid=(micro, n), out_shape=(jax.Shape...  41.3 us
    dot_general x3, matrix products, dot_t(): lax.dot_general(left, right, (((1,), (1,)), ((), ())), preferred_element_...  41.2 us
  transfers between devices with their start and end apart: 59, of which 26 were waited for; matrix products, arithmetic and copies ran while one was open for 28% of the time, Pallas kernels for 12%

profile of v5, /device:TPU:0, one launch (start us, length us, event | category | flops | bytes accessed | tf_op | source)
XLA Modules:
  0.0 905.1 jit_solution(17004540097630463456)
XLA Ops:
  9.0 2.8 concatenate.110
  15.4 6.3 all-to-all-start
  24.1 32.6 %all-to-all-done.refs_1_ = bf16[8,64,1408]{2,1,0:T(8,128)(2,1)S(1)} async-done(((bf16[8,64,1408]{2,1,0:T(8,128)(2,1)}), bf16[8,64,1408]{2,1,0:T(8,128)(2,1)S(1)}, u32[]{:S(2)}, u32[]{:S(2)}) %all-to-all-start) | async-done | bytes 1441824 | tf_op jit(solution)/shard_map/all_to_all | solution.py:70
  63.1 29.1 %collective-permute-done = bf16[8,64,1408]{2,1,0:T(8,128)(2,1)S(1)} collective-permute-done((bf16[8,64,1408]{2,1,0:T(8,128)(2,1)}, bf16[8,64,1408]{2,1,0:T(8,128)(2,1)S(1)}, u32[]{:S(2)}, u32[]{:S(2)}) %collective-permute-start) | collective-permute-done | bytes 1441824 | tf_op jit(solution)/shard_map/ppermute | solution.py:42
  95.9 13.3 %collective-permute-done.2 = bf16[4,64,1408]{2,1,0:T(8,128)(2,1)S(1)} collective-permute-done((bf16[4,64,1408]{2,1,0:T(8,128)(2,1)S(1)}, bf16[4,64,1408]{2,1,0:T(8,128)(2,1)S(1)}, u32[]{:S(2)}, u32[]{:S(2)}) %collective-permute-start.2) | collective-permute-done | bytes 720928 | tf_op jit(solution)/shard_map/ppermute | solution.py:42
  134.4 4.5 all-gather.5.cloned.1.call-done.refs_1_
  144.3 2.5 collective-permute-start.11
  147.8 4.3 all-to-all-start.1
  152.3 5.1 fusion
  158.1 21.9 %fusion.86.mixed_ref.before_ref.refs_1_ = f32[2048,1792]{1,0:T(8,128)} fusion(bf16[2048,1792]{1,0:T(8,128)(2,1)} %shard_map.257.refs_1_.refs_2_, bf16[2048,2048]{1,0:T(8,128)(2,1)} %all-gather.5.cloned.1.call-done.refs_1_, f32[2048]{0:T(1024)S(1)} %mul.290, f32[2048]{0:T(1024)S(1)} %add_rsqrt_fusion.1), kind=kOutput, calls=%fused_computation.272 | convolution fusion | flops 15049162752 | bytes 30425088 | tf_op jit(solution)/shard_map/dot_general | solution.py:216
  180.0 19.0 %shard_map.258 = (f32[2048,384]{1,0:T(8,128)S(1)}, f32[2048,384]{1,0:T(8,128)S(1)}, bf16[16,256,384]{2,1,0:T(8,128)(2,1)S(1)}) custom-call(f32[2048,1792]{1,0:T(8,128)} %fusion.86.mixed_ref.before_ref.refs_1_, f32[2048,1792]{1,0:T(8,128)} %fusion.86.mixed_ref.before_ref.refs_1_, f32[2048,8]{1,0:T(8,128)S(1)} %bitcast.251, f32[16,1,128]{2,1,0:T(1,128)S(1)} %bitcast.260, ...), custom_call_target="tpu_custom_call" | custom-call | bytes 72000000 | tf_op jit(solution)/shard_map/pallas_call | solution.py:512
  209.9 2.3 collective-permute-start.7
  215.8 14.7 %shard_map.262 = bf16[8,256,128]{2,1,0:T(8,128)(2,1)S(1)} custom-call(f32[8,256,1792]{2,1,0:T(8,128)} %bitcast.262, f32[8,256,1792]{2,1,0:T(8,128)} %bitcast.263, f32[8,256,1792]{2,1,0:T(8,128)} %bitcast.264, f32[8,128,256]{2,1,0:T(8,128)S(1)} %copy-done.8, f32[8,128,256]{2,1,0:T(8,128)S(1)} %copy-done.8, f32[8,256,8]{2,1,0:T(8,128)S(1)} %copy-done.10, ...), custom_call_target="tpu_custom_call" | custom-call | bytes 50400000 | tf_op jit(solution)/shard_map/pallas_call | solution.py:686
  232.7 8.3 convolution_convert_fusion.2.refs_0_
  241.0 3.6 all-gather.7.cloned.1.call-done.refs_1_
  253.5 2.5 broadcast_in_dim.111
  256.1 2.3 bitcast_dynamic-update-slice_fusion.6
  258.4 3.5 collective-permute-done.15
  261.9 2.4 collective-permute-start.14
  265.3 9.3 %collective-permute-done.16 = bf16[128,2048]{1,0:T(8,128)(2,1)} collective-permute-done((bf16[128,2048]{1,0:T(8,128)(2,1)}, bf16[128,2048]{1,0:T(8,128)(2,1)}, u32[]{:S(2)}, u32[]{:S(2)}) %collective-permute-start.16) | collective-permute-done | bytes 524320 | tf_op jit(solution)/shard_map/ppermute | solution.py:42
  276.8 18.7 %collective-permute-done.12 = bf16[8,64,1024]{2,1,0:T(8,128)(2,1)S(1)} collective-permute-done((bf16[8,64,1024]{2,1,0:T(8,128)(2,1)}, bf16[8,64,1024]{2,1,0:T(8,128)(2,1)S(1)}, u32[]{:S(2)}, u32[]{:S(2)}) %collective-permute-start.12) | collective-permute-done | bytes 1048608 | tf_op jit(solution)/shard_map/ppermute | solution.py:42
  296.6 21.8 %collective-permute-done.13 = bf16[8,64,1024]{2,1,0:T(8,128)(2,1)S(1)} collective-permute-done((bf16[8,64,1024]{2,1,0:T(8,128)(2,1)}, bf16[8,64,1024]{2,1,0:T(8,128)(2,1)S(1)}, u32[]{:S(2)}, u32[]{:S(2)}) %collective-permute-start.13) | collective-permute-done | bytes 1048608 | tf_op jit(solution)/shard_map/ppermute | solution.py:42
  320.7 14.3 %reduce-scatter.5.cloned.1.call-done.refs_0_ = bf16[256,2048]{1,0:T(8,128)(2,1)} async-done(((bf16[2048,2048]{1,0:T(8,128)(2,1)}), bf16[256,2048]{1,0:T(8,128)(2,1)}) %reduce-scatter.5.cloned.1.call-update) | async-done | bytes 1048592 | tf_op jit(solution)/shard_map/reduce_scatter | solution.py:813
  337.9 2.6 multiply_convert_fusion.1
  340.6 6.6 copy.170.refs_0_
  347.2 11.3 %fusion.90.refs_0_ = f32[2048,512]{1,0:T(8,128)} fusion(bf16[2048,2048]{1,0:T(8,128)(2,1)} %all-gather.7.cloned.1.call-done.refs_1_, bf16[512,2048]{1,0:T(8,128)(2,1)} %bitcast.286), kind=kOutput, calls=%fused_computation.275 | convolution fusion | flops 4294967296 | bytes 14680064 | tf_op jit(solution)/shard_map/dot_general | solution.py:220
  358.5 62.7 %all-gather.9.cloned.1.call-done.rows_ref = bf16[2048,2048]{1,0:T(8,128)(2,1)} async-done(((bf16[256,2048]{1,0:T(8,128)(2,1)}), bf16[2048,2048]{1,0:T(8,128)(2,1)}) %all-gather.9.cloned.1.call-update) | async-done | bytes 8388624 | tf_op jit(solution)/shard_map/all_gather | solution.py:810
  421.1 25.0 %shard_map.278 = (bf16[2048,512]{1,0:T(8,128)(2,1)S(1)}, bf16[2048,1024]{1,0:T(8,128)(2,1)}, bf16[2048,2048]{1,0:T(8,128)(2,1)}) custom-call(bf16[2048,2048]{1,0:T(8,128)(2,1)} %all-gather.9.cloned.1.call-done.rows_ref, bf16[2048,1024]{1,0:T(8,128)(2,1)} %bitcast.43.refs_1_.weight_ref, bf16[1024,2048]{1,0:T(8,128)(2,1)} %shard_map.276.turned_ref, ...), custom_call_target="tpu_custom_call" | custom-call | bytes 79200000 | tf_op jit(solution)/shard_map/pallas_call | solution.py:744
  448.0 10.1 %convolution_convert_fusion.6.refs_2_ = bf16[512,2048]{1,0:T(8,128)(2,1)} fusion(bf16[2048,512]{1,0:T(8,128)(2,1)} %copy-done.42, bf16[2048,2048]{1,0:T(8,128)(2,1)} %all-gather.7.cloned.1.call-done.refs_1_), kind=kOutput, calls=%fused_computation.30 | convolution fusion | flops 4296015872 | bytes 12582912 | tf_op jit(solution)/shard_map/dot_general | solution.py:224
  458.1 12.9 %convolution_convert_fusion.3.refs_1_ = bf16[2048,1024]{1,0:T(8,128)(2,1)} fusion(bf16[2048,2048]{1,0:T(8,128)(2,1)} %all-gather.9.cloned.1.call-done.rows_ref, bf16[2048,1024]{1,0:T(8,128)(2,1)S(1)} %copy-done.93), kind=kOutput, calls=%fused_computation.12 | convolution fusion | flops 8592031744 | bytes 16777216 | tf_op jit(solution)/shard_map/dot_general | solution.py:224
  471.0 64.8 %reduce-scatter.7.cloned.1.call-done.refs_0_ = bf16[256,2048]{1,0:T(8,128)(2,1)} async-done(((bf16[2048,2048]{1,0:T(8,128)(2,1)}), bf16[256,2048]{1,0:T(8,128)(2,1)}) %reduce-scatter.7.cloned.1.call-update) | async-done | bytes 1048592 | tf_op jit(solution)/shard_map/reduce_scatter | solution.py:813
  535.8 2.3 fusion.14
  545.2 2.6 dynamic-slice_bitcast_fusion.2
  550.9 5.7 collective-permute-done.21
  556.6 2.4 collective-permute-start.20
  559.0 6.7 convolution_convert_fusion.1.refs_0_
  565.7 3.6 collective-permute-done.22
  569.3 2.4 fusion.37.refs_2_.refs_0_
  571.6 18.7 %collective-permute-done.18 = bf16[512,1024]{1,0:T(8,128)(2,1)S(1)} collective-permute-done((bf16[512,1024]{1,0:T(8,128)(2,1)S(1)}, bf16[512,1024]{1,0:T(8,128)(2,1)S(1)}, u32[]{:S(2)}, u32[]{:S(2)}) %collective-permute-start.18) | collective-permute-done | bytes 1048608 | tf_op jit(solution)/shard_map/ppermute | solution.py:42
  590.3 20.3 %collective-permute-done.19 = bf16[512,1024]{1,0:T(8,128)(2,1)S(1)} collective-permute-done((bf16[512,1024]{1,0:T(8,128)(2,1)S(1)}, bf16[512,1024]{1,0:T(8,128)(2,1)S(1)}, u32[]{:S(2)}, u32[]{:S(2)}) %collective-permute-start.19) | collective-permute-done | bytes 1048608 | tf_op jit(solution)/shard_map/ppermute | solution.py:42
  610.6 3.1 fusion.22.refs_1_
  613.7 7.0 all-gather.11.cloned.1.call-done.refs_0_
  620.7 4.3 all-to-all-start.2
  625.2 8.4 fusion.91
  633.7 9.8 %convolution_convert_fusion.5 = bf16[512,2048]{1,0:T(8,128)(2,1)S(1)} fusion(bf16[2048,2048]{1,0:T(8,128)(2,1)} %shard_map.280.refs_1_, bf16[2048,128]{1,0:T(8,128)(2,1)S(1)} %bitcast.258, bf16[2048,384]{1,0:T(8,128)(2,1)S(1)} %copy-done.74), kind=kOutput, calls=%fused_computation.29 | convolution fusion | flops 4300210176 | bytes 12582912 | tf_op jit(solution)/shard_map/dot_general | solution.py:224
  643.7 2.2 copy-done.7
  654.7 2.4 collective-permute-start.26
  660.8 19.3 %shard_map.284 = (bf16[8,256,128]{2,1,0:T(8,128)(2,1)S(1)}, bf16[8,256,128]{2,1,0:T(8,128)(2,1)S(1)}, bf16[8,256,128]{2,1,0:T(8,128)(2,1)S(1)}) custom-call(f32[8,256,1792]{2,1,0:T(8,128)} %bitcast.265, f32[8,256,1792]{2,1,0:T(8,128)} %bitcast.266, f32[8,256,1792]{2,1,0:T(8,128)} %bitcast.267, f32[8,128,256]{2,1,0:T(8,128)S(1)} %copy-done.9, ...), custom_call_target="tpu_custom_call" | custom-call | bytes 68400000 | tf_op jit(solution)/shard_map/pallas_call | solution.py:704
  685.1 41.3 %shard_map.285 = (bf16[2048,1792]{1,0:T(8,128)(2,1)}, f32[8,896]{1,0:T(8,128)S(1)}, f32[8,128]{1,0:T(8,128)S(1)}, f32[8,384]{1,0:T(8,128)S(1)}) custom-call(f32[2048,1792]{1,0:T(8,128)} %fusion.86.mixed_ref.before_ref.refs_1_, f32[2048,1792]{1,0:T(8,128)} %fusion.86.mixed_ref.before_ref.refs_1_, f32[2048,8]{1,0:T(8,128)S(1)} %bitcast.252, ...), custom_call_target="tpu_custom_call" | custom-call | bytes 154800000 | tf_op jit(solution)/shard_map/pallas_call | solution.py:549
  726.4 21.5 %convolution_convert_fusion.refs_0_ = bf16[2048,2048]{1,0:T(8,128)(2,1)} fusion(bf16[2048,1792]{1,0:T(8,128)(2,1)} %shard_map.286.refs_0_, bf16[2048,1792]{1,0:T(8,128)(2,1)} %shard_map.257.refs_1_.refs_2_), kind=kOutput, calls=%fused_computation.7 | convolution fusion | flops 15036579840 | bytes 23068672 | tf_op jit(solution)/shard_map/dot_general | solution.py:220
  751.0 13.7 %add_convert_fusion.refs_1_ = bf16[2048,1024]{1,0:T(8,128)(2,1)S(1)} fusion(f32[2048,12]{1,0:T(8,128)S(1)} %bitcast.294, bf16[2048,1792]{1,0:T(8,128)(2,1)} %shard_map.288, bf16[2048,2048]{1,0:T(8,128)(2,1)} %all-gather.5.cloned.1.call-done.refs_1_, f32[2048]{0:T(1024)S(1)} %copy-done.80, f32[2048]{0:T(1024)S(1)} %copy-done.90), kind=kOutput, calls=%fused_computation.6 | convolution fusion | flops 8610906112 | bytes 16891904 | tf_op jit(solution)/shard_map/dot_general | solution.py:224
  769.8 12.3 %convolution_convert_fusion.4.refs_1_ = bf16[2048,768]{1,0:T(8,128)(2,1)} fusion(bf16[2048,1792]{1,0:T(8,128)(2,1)} %shard_map.288, bf16[2048,2048]{1,0:T(8,128)(2,1)} %all-gather.5.cloned.1.call-done.refs_1_, f32[2048]{0:T(1024)S(1)} %copy-done.80, f32[2048]{0:T(1024)S(1)} %copy-done.90), kind=kOutput, calls=%fused_computation.21 | convolution fusion | flops 6460801024 | bytes 14696448 | tf_op jit(solution)/shard_map/dot_general | solution.py:224
  782.1 8.2 collective-permute-done.43.refs_0_
  791.3 2.8 convert_element_type.387
  798.0 2.8 fusion.48
  807.8 8.2 collective-permute-done.42
  827.5 2.7 shard_map.290.refs_1_
  831.1 2.4 convert_element_type.374
  834.4 2.4 convert_element_type.368
  838.9 4.9 all-to-all-start.4
  849.9 7.3 collective-permute-done.32
  862.1 3.8 all-to-all-start.3
  882.9 2.4 collective-permute-start.39
  885.4 3.5 fusion.18.in_ref
  (524 shorter events, 186.1 us)
Async XLA Ops:
  7.2 131.8 %copy-start = (f32[3,48]{1,0:T(4,128)S(1)}, f32[3,48]{1,0:T(4,128)}, u32[]{:S(2)}) copy-start(f32[3,48]{1,0:T(4,128)} %param.21) | copy-start | bytes 1732
  15.4 41.3 %all-to-all-start = ((bf16[8,64,1408]{2,1,0:T(8,128)(2,1)}), bf16[8,64,1408]{2,1,0:T(8,128)(2,1)S(1)}, u32[]{:S(2)}, u32[]{:S(2)}) async-start(bf16[8,64,1408]{2,1,0:T(8,128)(2,1)} %shard_map.255), calls=%async_computation | async-start | bytes 2883584 | tf_op jit(solution)/shard_map/all_to_all | solution.py:70
  21.7 117.3 %all-gather.5.cloned.1.call-start = ((), (), s32[]{:S(2)}) async-start(), calls=%async_computation.9 | async-start | bytes 9437184 | tf_op jit(solution)/shard_map/all_gather | solution.py:810
  57.9 186.8 %all-gather.7.cloned.1.call-start = ((), (), s32[]{:S(2)}) async-start(), calls=%async_computation.10 | async-start | bytes 9437184 | tf_op jit(solution)/shard_map/all_gather | solution.py:810
  58.8 33.4 %collective-permute-start = (bf16[8,64,1408]{2,1,0:T(8,128)(2,1)}, bf16[8,64,1408]{2,1,0:T(8,128)(2,1)S(1)}, u32[]{:S(2)}, u32[]{:S(2)}) collective-permute-start(bf16[8,64,1408]{2,1,0:T(8,128)(2,1)} %copy-done.54), channel_id=1, source_target_pairs={{0,1},{1,0},{2,3},{3,2},{4,5},{5,4},{6,7},{7,6},{8,9},{9,8},{10,11... | collective-permute-start | bytes 4325384 | tf_op jit(solution)/shard_map/ppermute | solution.py:42
  60.3 33.5 %collective-permute-start.1 = (bf16[8,64,1408]{2,1,0:T(8,128)(2,1)}, bf16[8,64,1408]{2,1,0:T(8,128)(2,1)S(1)}, u32[]{:S(2)}, u32[]{:S(2)}) collective-permute-start(bf16[8,64,1408]{2,1,0:T(8,128)(2,1)} %copy-done.54), channel_id=1, source_target_pairs={{0,2},{1,3},{2,0},{3,1},{4,6},{5,7},{6,4},{7,5},{8,10},{9,11},{10,... | collective-permute-start | bytes 4325384 | tf_op jit(solution)/shard_map/ppermute | solution.py:42
  92.2 17.0 %collective-permute-start.2 = (bf16[4,64,1408]{2,1,0:T(8,128)(2,1)S(1)}, bf16[4,64,1408]{2,1,0:T(8,128)(2,1)S(1)}, u32[]{:S(2)}, u32[]{:S(2)}) collective-permute-start(bf16[4,64,1408]{2,1,0:T(8,128)(2,1)S(1)} %slice.365), channel_id=1, source_target_pairs={{0,2},{1,3},{2,0},{3,1},{4,6},{5,7},{6,4},{7,5},{8,10},{9,11},{10,... | collective-permute-start | bytes 2162696 | tf_op jit(solution)/shard_map/ppermute | solution.py:42
  93.9 16.7 %collective-permute-start.3 = (bf16[4,64,1408]{2,1,0:T(8,128)(2,1)S(1)}, bf16[4,64,1408]{2,1,0:T(8,128)(2,1)S(1)}, u32[]{:S(2)}, u32[]{:S(2)}) collective-permute-start(bf16[4,64,1408]{2,1,0:T(8,128)(2,1)S(1)} %slice.366), channel_id=1, source_target_pairs={{0,1},{1,0},{2,3},{3,2},{4,5},{5,4},{6,7},{7,6},{8,9},{9,8},{10,11... | collective-permute-start | bytes 2162696 | tf_op jit(solution)/shard_map/ppermute | solution.py:42
  116.2 11.0 %collective-permute-start.4 = (bf16[2048,384]{1,0:T(8,128)(2,1)}, bf16[2048,384]{1,0:T(8,128)(2,1)}, u32[]{:S(2)}, u32[]{:S(2)}) collective-permute-start(bf16[2048,384]{1,0:T(8,128)(2,1)} %pad_maximum_fusion.1), channel_id=1, source_target_pairs={{0,4},{4,0},{8,12},{12,8},{16,20},{20,16},{24,28},{28,24},{1,5},{5... | collective-permute-start | bytes 4718600 | tf_op jit(solution)/shard_map/ppermute | solution.py:42
  144.3 59.0 %collective-permute-start.11 = (bf16[128,2048]{1,0:T(8,128)(2,1)}, bf16[128,2048]{1,0:T(8,128)(2,1)}, u32[]{:S(2)}, u32[]{:S(2)}) collective-permute-start(bf16[128,2048]{1,0:T(8,128)(2,1)} %shard_map.264.refs_0_), channel_id=1, source_target_pairs={{0,3},{1,2},{2,1},{3,0},{4,7},{5,6},{6,5},{7,4},{8,11},{9,10},{10,... | collective-permute-start | bytes 1572872 | tf_op jit(solution)/shard_map/ppermute | solution.py:42
  146.8 57.5 %collective-permute-start.10 = (bf16[128,2048]{1,0:T(8,128)(2,1)}, bf16[128,2048]{1,0:T(8,128)(2,1)}, u32[]{:S(2)}, u32[]{:S(2)}) collective-permute-start(bf16[128,2048]{1,0:T(8,128)(2,1)} %shard_map.264.refs_0_), channel_id=1, source_target_pairs={{0,2},{1,3},{2,0},{3,1},{4,6},{5,7},{6,4},{7,5},{8,10},{9,11},{10,... | collective-permute-start | bytes 1572872 | tf_op jit(solution)/shard_map/ppermute | solution.py:42
  147.3 56.9 %collective-permute-start.9 = (bf16[128,2048]{1,0:T(8,128)(2,1)}, bf16[128,2048]{1,0:T(8,128)(2,1)}, u32[]{:S(2)}, u32[]{:S(2)}) collective-permute-start(bf16[128,2048]{1,0:T(8,128)(2,1)} %shard_map.264.refs_0_), channel_id=1, source_target_pairs={{0,1},{1,0},{2,3},{3,2},{4,5},{5,4},{6,7},{7,6},{8,9},{9,8},{10,11... | collective-permute-start | bytes 1572872 | tf_op jit(solution)/shard_map/ppermute | solution.py:42
  147.8 65.5 %all-to-all-start.1 = ((bf16[8,64,1024]{2,1,0:T(8,128)(2,1)}), bf16[8,64,1024]{2,1,0:T(8,128)(2,1)}, u32[]{:S(2)}, u32[]{:S(2)}) async-start(bf16[8,64,1024]{2,1,0:T(8,128)(2,1)} %shard_map.260), calls=%async_computation.1 | async-start | bytes 2097152 | tf_op jit(solution)/shard_map/all_to_all | solution.py:70
  152.1 182.9 %reduce-scatter.5.cloned.1.call-start = ((), (), s32[]{:S(2)}) async-start(), calls=%async_computation.11 | async-start | bytes 9437184 | tf_op jit(solution)/shard_map/reduce_scatter | solution.py:813
  202.9 5.2 collective-permute-start.5
  208.1 22.4 %collective-permute-start.6 = (f32[2048]{0:T(1024)S(1)}, f32[2048]{0:T(1024)S(1)}, u32[]{:S(2)}, u32[]{:S(2)}) collective-permute-start(f32[2048]{0:T(1024)S(1)} %add.278), channel_id=1, source_target_pairs={{0,8},{4,12},{8,0},{12,4},{16,24},{20,28},{24,16},{28,20},{1,9},{5... | collective-permute-start | bytes 24584 | tf_op jit(solution)/shard_map/ppermute | solution.py:42
  209.9 20.6 %collective-permute-start.7 = (f32[2048]{0:T(1024)S(1)}, f32[2048]{0:T(1024)S(1)}, u32[]{:S(2)}, u32[]{:S(2)}) collective-permute-start(f32[2048]{0:T(1024)S(1)} %add.278), channel_id=1, source_target_pairs={{0,16},{4,20},{8,24},{12,28},{16,0},{20,4},{24,8},{28,12},{1,17},{... | collective-permute-start | bytes 24584 | tf_op jit(solution)/shard_map/ppermute | solution.py:42
  212.3 18.3 %collective-permute-start.8 = (f32[2048]{0:T(1024)S(1)}, f32[2048]{0:T(1024)S(1)}, u32[]{:S(2)}, u32[]{:S(2)}) collective-permute-start(f32[2048]{0:T(1024)S(1)} %add.278), channel_id=1, source_target_pairs={{0,24},{4,28},{8,16},{12,20},{16,8},{20,12},{24,0},{28,4},{1,25},{... | collective-permute-start | bytes 24584 | tf_op jit(solution)/shard_map/ppermute | solution.py:42
  244.7 176.5 %all-gather.9.cloned.1.call-start = ((), (), s32[]{:S(2)}) async-start(), calls=%async_computation.12 | async-start | bytes 9437184 | tf_op jit(solution)/shard_map/all_gather | solution.py:810
  246.8 291.4 %copy-start.76 = (f32[2048]{0:T(1024)}, f32[2048]{0:T(1024)S(1)}, u32[]{:S(2)}) copy-start(f32[2048]{0:T(1024)S(1)} %mul.308) | copy-start | bytes 24580
  246.8 15.1 %collective-permute-start.15 = (bf16[128,2048]{1,0:T(8,128)(2,1)}, bf16[128,2048]{1,0:T(8,128)(2,1)}, u32[]{:S(2)}, u32[]{:S(2)}) collective-permute-start(bf16[128,2048]{1,0:T(8,128)(2,1)} %shard_map.274), channel_id=1, source_target_pairs={{0,1},{1,0},{2,3},{3,2},{4,5},{5,4},{6,7},{7,6},{8,9},{9,8},{10,11... | collective-permute-start | bytes 1572872 | tf_op jit(solution)/shard_map/ppermute | solution.py:42
  248.3 26.3 %collective-permute-start.16 = (bf16[128,2048]{1,0:T(8,128)(2,1)}, bf16[128,2048]{1,0:T(8,128)(2,1)}, u32[]{:S(2)}, u32[]{:S(2)}) collective-permute-start(bf16[128,2048]{1,0:T(8,128)(2,1)} %shard_map.274), channel_id=1, source_target_pairs={{0,2},{1,3},{2,0},{3,1},{4,6},{5,7},{6,4},{7,5},{8,10},{9,11},{10,... | collective-permute-start | bytes 1572872 | tf_op jit(solution)/shard_map/ppermute | solution.py:42
  249.7 26.0 %collective-permute-start.17 = (bf16[128,2048]{1,0:T(8,128)(2,1)}, bf16[128,2048]{1,0:T(8,128)(2,1)}, u32[]{:S(2)}, u32[]{:S(2)}) collective-permute-start(bf16[128,2048]{1,0:T(8,128)(2,1)} %shard_map.274), channel_id=1, source_target_pairs={{0,3},{1,2},{2,1},{3,0},{4,7},{5,6},{6,5},{7,4},{8,11},{9,10},{10,... | collective-permute-start | bytes 1572872 | tf_op jit(solution)/shard_map/ppermute | solution.py:42
  250.3 45.2 %collective-permute-start.12 = (bf16[8,64,1024]{2,1,0:T(8,128)(2,1)}, bf16[8,64,1024]{2,1,0:T(8,128)(2,1)S(1)}, u32[]{:S(2)}, u32[]{:S(2)}) collective-permute-start(bf16[8,64,1024]{2,1,0:T(8,128)(2,1)} %shard_map.272), channel_id=1, source_target_pairs={{0,1},{1,0},{2,3},{3,2},{4,5},{5,4},{6,7},{7,6},{8,9},{9,8},{10,11... | collective-permute-start | bytes 3145736 | tf_op jit(solution)/shard_map/ppermute | solution.py:42
  251.7 66.7 %collective-permute-start.13 = (bf16[8,64,1024]{2,1,0:T(8,128)(2,1)}, bf16[8,64,1024]{2,1,0:T(8,128)(2,1)S(1)}, u32[]{:S(2)}, u32[]{:S(2)}) collective-permute-start(bf16[8,64,1024]{2,1,0:T(8,128)(2,1)} %shard_map.272), channel_id=1, source_target_pairs={{0,2},{1,3},{2,0},{3,1},{4,6},{5,7},{6,4},{7,5},{8,10},{9,11},{10,... | collective-permute-start | bytes 3145736 | tf_op jit(solution)/shard_map/ppermute | solution.py:42
  261.9 57.7 %collective-permute-start.14 = (bf16[8,64,1024]{2,1,0:T(8,128)(2,1)}, bf16[8,64,1024]{2,1,0:T(8,128)(2,1)S(1)}, u32[]{:S(2)}, u32[]{:S(2)}) collective-permute-start(bf16[8,64,1024]{2,1,0:T(8,128)(2,1)} %shard_map.272), channel_id=1, source_target_pairs={{0,3},{1,2},{2,1},{3,0},{4,7},{5,6},{6,5},{7,4},{8,11},{9,10},{10,... | collective-permute-start | bytes 3145736 | tf_op jit(solution)/shard_map/ppermute | solution.py:42
  337.9 200.3 %copy-start.82 = (f32[256]{0:T(256)}, f32[256]{0:T(256)S(1)}, u32[]{:S(2)}) copy-start(f32[256]{0:T(256)S(1)} %get-tuple-element.170) | copy-start | bytes 3076
  337.9 200.3 %copy-start.85 = (f32[256]{0:T(256)}, f32[256]{0:T(256)S(1)}, u32[]{:S(2)}) copy-start(f32[256]{0:T(256)S(1)} %get-tuple-element.169) | copy-start | bytes 3076
  340.6 195.3 %reduce-scatter.7.cloned.1.call-start = ((), (), s32[]{:S(2)}) async-start(), calls=%async_computation.13 | async-start | bytes 9437184 | tf_op jit(solution)/shard_map/reduce_scatter | solution.py:813
  447.5 173.2 %all-gather.11.cloned.1.call-start = ((), (), s32[]{:S(2)}) async-start(), calls=%async_computation.14 | async-start | bytes 9437184 | tf_op jit(solution)/shard_map/all_gather | solution.py:810
  471.0 64.8 %copy-start.45 = (bf16[256,2048]{1,0:T(8,128)(2,1)S(1)}, bf16[256,2048]{1,0:T(8,128)(2,1)}, u32[]{:S(2)}) copy-start(bf16[256,2048]{1,0:T(8,128)(2,1)} %shard_map.275) | copy-start | bytes 3145732
  540.1 207.8 %reduce-scatter.9.cloned.1.call-start = ((), (), s32[]{:S(2)}) async-start(), calls=%async_computation.15 | async-start | bytes 9437184 | tf_op jit(solution)/shard_map/reduce_scatter | solution.py:1038
  541.7 14.9 %collective-permute-start.21 = (bf16[128,2048]{1,0:T(8,128)(2,1)S(1)}, bf16[128,2048]{1,0:T(8,128)(2,1)S(1)}, u32[]{:S(2)}, u32[]{:S(2)}) collective-permute-start(bf16[128,2048]{1,0:T(8,128)(2,1)S(1)} %get-tuple-element.147), channel_id=1, source_target_pairs={{0,1},{1,0},{2,3},{3,2},{4,5},{5,4},{6,7},{7,6},{8,9},{9,8},{10,11... | collective-permute-start | bytes 1572872 | tf_op jit(solution)/shard_map/ppermute | solution.py:42
  543.2 26.1 %collective-permute-start.22 = (bf16[128,2048]{1,0:T(8,128)(2,1)S(1)}, bf16[128,2048]{1,0:T(8,128)(2,1)S(1)}, u32[]{:S(2)}, u32[]{:S(2)}) collective-permute-start(bf16[128,2048]{1,0:T(8,128)(2,1)S(1)} %get-tuple-element.149), channel_id=1, source_target_pairs={{0,2},{1,3},{2,0},{3,1},{4,6},{5,7},{6,4},{7,5},{8,10},{9,11},{10,... | collective-permute-start | bytes 1572872 | tf_op jit(solution)/shard_map/ppermute | solution.py:42
  544.7 24.6 %collective-permute-start.23 = (bf16[128,2048]{1,0:T(8,128)(2,1)S(1)}, bf16[128,2048]{1,0:T(8,128)(2,1)S(1)}, u32[]{:S(2)}, u32[]{:S(2)}) collective-permute-start(bf16[128,2048]{1,0:T(8,128)(2,1)S(1)} %get-tuple-element.148), channel_id=1, source_target_pairs={{0,3},{1,2},{2,1},{3,0},{4,7},{5,6},{6,5},{7,4},{8,11},{9,10},{10,... | collective-permute-start | bytes 1572872 | tf_op jit(solution)/shard_map/ppermute | solution.py:42
  547.9 42.5 %collective-permute-start.18 = (bf16[512,1024]{1,0:T(8,128)(2,1)S(1)}, bf16[512,1024]{1,0:T(8,128)(2,1)S(1)}, u32[]{:S(2)}, u32[]{:S(2)}) collective-permute-start(bf16[512,1024]{1,0:T(8,128)(2,1)S(1)} %get-tuple-element.131), channel_id=1, source_target_pairs={{0,1},{1,0},{2,3},{3,2},{4,5},{5,4},{6,7},{7,6},{8,9},{9,8},{10,11... | collective-permute-start | bytes 3145736 | tf_op jit(solution)/shard_map/ppermute | solution.py:42
  549.4 61.2 %collective-permute-start.19 = (bf16[512,1024]{1,0:T(8,128)(2,1)S(1)}, bf16[512,1024]{1,0:T(8,128)(2,1)S(1)}, u32[]{:S(2)}, u32[]{:S(2)}) collective-permute-start(bf16[512,1024]{1,0:T(8,128)(2,1)S(1)} %get-tuple-element.133), channel_id=1, source_target_pairs={{0,2},{1,3},{2,0},{3,1},{4,6},{5,7},{6,4},{7,5},{8,10},{9,11},{10,... | collective-permute-start | bytes 3145736 | tf_op jit(solution)/shard_map/ppermute | solution.py:42
  556.6 54.0 %collective-permute-start.20 = (bf16[512,1024]{1,0:T(8,128)(2,1)S(1)}, bf16[512,1024]{1,0:T(8,128)(2,1)S(1)}, u32[]{:S(2)}, u32[]{:S(2)}) collective-permute-start(bf16[512,1024]{1,0:T(8,128)(2,1)S(1)} %get-tuple-element.132), channel_id=1, source_target_pairs={{0,3},{1,2},{2,1},{3,0},{4,7},{5,6},{6,5},{7,4},{8,11},{9,10},{10,... | collective-permute-start | bytes 3145736 | tf_op jit(solution)/shard_map/ppermute | solution.py:42
  620.7 105.7 %all-to-all-start.2 = ((bf16[8,64,1024]{2,1,0:T(8,128)(2,1)}), bf16[8,64,1024]{2,1,0:T(8,128)(2,1)}, u32[]{:S(2)}, u32[]{:S(2)}) async-start(bf16[8,64,1024]{2,1,0:T(8,128)(2,1)} %bitcast.66), calls=%async_computation.5 | async-start | bytes 2097152 | tf_op jit(solution)/shard_map/all_to_all | solution.py:70
  625.0 246.1 %reduce-scatter.11.cloned.1.call-start = ((), (), s32[]{:S(2)}) async-start(), calls=%async_computation.16 | async-start | bytes 9437184 | tf_op jit(solution)/shard_map/reduce_scatter | solution.py:1137
  647.0 5.4 collective-permute-start.24
  649.6 76.8 %collective-permute-start.28 = (bf16[128,2048]{1,0:T(8,128)(2,1)}, bf16[128,2048]{1,0:T(8,128)(2,1)}, u32[]{:S(2)}, u32[]{:S(2)}) collective-permute-start(bf16[128,2048]{1,0:T(8,128)(2,1)} %get-tuple-element.145), channel_id=1, source_target_pairs={{0,1},{1,0},{2,3},{3,2},{4,5},{5,4},{6,7},{7,6},{8,9},{9,8},{10,11... | collective-permute-start | bytes 1572872 | tf_op jit(solution)/shard_map/ppermute | solution.py:42
  650.9 75.5 %collective-permute-start.29 = (bf16[128,2048]{1,0:T(8,128)(2,1)}, bf16[128,2048]{1,0:T(8,128)(2,1)}, u32[]{:S(2)}, u32[]{:S(2)}) collective-permute-start(bf16[128,2048]{1,0:T(8,128)(2,1)} %get-tuple-element.146), channel_id=1, source_target_pairs={{0,2},{1,3},{2,0},{3,1},{4,6},{5,7},{6,4},{7,5},{8,10},{9,11},{10,... | collective-permute-start | bytes 1572872 | tf_op jit(solution)/shard_map/ppermute | solution.py:42
  653.0 27.4 %collective-permute-start.25 = (f32[2048]{0:T(1024)}, f32[2048]{0:T(1024)S(1)}, u32[]{:S(2)}, u32[]{:S(2)}) collective-permute-start(f32[2048]{0:T(1024)} %add.294.refs_1_), channel_id=1, source_target_pairs={{0,8},{4,12},{8,0},{12,4},{16,24},{20,28},{24,16},{28,20},{1,9},{5... | collective-permute-start | bytes 24584 | tf_op jit(solution)/shard_map/ppermute | solution.py:42
  654.7 26.4 %collective-permute-start.26 = (f32[2048]{0:T(1024)}, f32[2048]{0:T(1024)S(1)}, u32[]{:S(2)}, u32[]{:S(2)}) collective-permute-start(f32[2048]{0:T(1024)} %add.294.refs_1_), channel_id=1, source_target_pairs={{0,16},{4,20},{8,24},{12,28},{16,0},{20,4},{24,8},{28,12},{1,17},{... | collective-permute-start | bytes 24584 | tf_op jit(solution)/shard_map/ppermute | solution.py:42
  657.1 24.0 %collective-permute-start.27 = (f32[2048]{0:T(1024)}, f32[2048]{0:T(1024)S(1)}, u32[]{:S(2)}, u32[]{:S(2)}) collective-permute-start(f32[2048]{0:T(1024)} %add.294.refs_1_), channel_id=1, source_target_pairs={{0,24},{4,28},{8,16},{12,20},{16,8},{20,12},{24,0},{28,4},{1,25},{... | collective-permute-start | bytes 24584 | tf_op jit(solution)/shard_map/ppermute | solution.py:42
  680.4 46.0 %collective-permute-start.30 = (bf16[128,2048]{1,0:T(8,128)(2,1)}, bf16[128,2048]{1,0:T(8,128)(2,1)}, u32[]{:S(2)}, u32[]{:S(2)}) collective-permute-start(bf16[128,2048]{1,0:T(8,128)(2,1)} %get-tuple-element.144), channel_id=1, source_target_pairs={{0,3},{1,2},{2,1},{3,0},{4,7},{5,6},{6,5},{7,4},{8,11},{9,10},{10,... | collective-permute-start | bytes 1572872 | tf_op jit(solution)/shard_map/ppermute | solution.py:42
  766.8 23.5 %collective-permute-start.43 = (bf16[2,256,1024]{2,1,0:T(8,128)(2,1)S(1)}, bf16[2,256,1024]{2,1,0:T(8,128)(2,1)S(1)}, u32[]{:S(2)}, u32[]{:S(2)}) collective-permute-start(bf16[2,256,1024]{2,1,0:T(8,128)(2,1)S(1)} %pad_maximum_fusion.7), channel_id=1, source_target_pairs={{0,2},{1,3},{2,0},{3,1},{4,6},{5,7},{6,4},{7,5},{8,10},{9,11},{10,... | collective-permute-start | bytes 3145736 | tf_op jit(solution)/shard_map/ppermute | solution.py:42
  768.2 25.8 %collective-permute-start.41 = (bf16[2,256,1024]{2,1,0:T(8,128)(2,1)S(1)}, bf16[2,256,1024]{2,1,0:T(8,128)(2,1)S(1)}, u32[]{:S(2)}, u32[]{:S(2)}) collective-permute-start(bf16[2,256,1024]{2,1,0:T(8,128)(2,1)S(1)} %pad_maximum_fusion.6), channel_id=1, source_target_pairs={{0,1},{1,0},{2,3},{3,2},{4,5},{5,4},{6,7},{7,6},{8,9},{9,8},{10,11... | collective-permute-start | bytes 3145736 | tf_op jit(solution)/shard_map/ppermute | solution.py:42
  800.8 15.2 %collective-permute-start.42 = (bf16[256,1024]{1,0:T(8,128)(2,1)}, bf16[256,1024]{1,0:T(8,128)(2,1)}, u32[]{:S(2)}, u32[]{:S(2)}) collective-permute-start(bf16[256,1024]{1,0:T(8,128)(2,1)} %get-tuple-element.125), channel_id=1, source_target_pairs={{0,2},{1,3},{2,0},{3,1},{4,6},{5,7},{6,4},{7,5},{8,10},{9,11},{10,... | collective-permute-start | bytes 1572872 | tf_op jit(solution)/shard_map/ppermute | solution.py:42
  802.4 15.2 %collective-permute-start.44 = (bf16[256,1024]{1,0:T(8,128)(2,1)}, bf16[256,1024]{1,0:T(8,128)(2,1)}, u32[]{:S(2)}, u32[]{:S(2)}) collective-permute-start(bf16[256,1024]{1,0:T(8,128)(2,1)} %get-tuple-element.126), channel_id=1, source_target_pairs={{0,1},{1,0},{2,3},{3,2},{4,5},{5,4},{6,7},{7,6},{8,9},{9,8},{10,11... | collective-permute-start | bytes 1572872 | tf_op jit(solution)/shard_map/ppermute | solution.py:42
  805.8 24.4 %collective-permute-start.33 = (bf16[2,256,768]{2,1,0:T(8,128)(2,1)}, bf16[2,256,768]{2,1,0:T(8,128)(2,1)S(1)}, u32[]{:S(2)}, u32[]{:S(2)}) collective-permute-start(bf16[2,256,768]{2,1,0:T(8,128)(2,1)} %pad_maximum_fusion.9), channel_id=1, source_target_pairs={{0,2},{1,3},{2,0},{3,1},{4,6},{5,7},{6,4},{7,5},{8,10},{9,11},{10,... | collective-permute-start | bytes 2359304 | tf_op jit(solution)/shard_map/ppermute | solution.py:42
  807.3 26.2 %collective-permute-start.31 = (bf16[2,256,768]{2,1,0:T(8,128)(2,1)}, bf16[2,256,768]{2,1,0:T(8,128)(2,1)S(1)}, u32[]{:S(2)}, u32[]{:S(2)}) collective-permute-start(bf16[2,256,768]{2,1,0:T(8,128)(2,1)} %pad_maximum_fusion.8), channel_id=1, source_target_pairs={{0,1},{1,0},{2,3},{3,2},{4,5},{5,4},{6,7},{7,6},{8,9},{9,8},{10,11... | collective-permute-start | bytes 2359304 | tf_op jit(solution)/shard_map/ppermute | solution.py:42
  820.6 16.1 %collective-permute-start.45 = (bf16[512,384]{1,0:T(8,128)(2,1)}, bf16[512,384]{1,0:T(8,128)(2,1)}, u32[]{:S(2)}, u32[]{:S(2)}) collective-permute-start(bf16[512,384]{1,0:T(8,128)(2,1)} %broadcast_select_fusion.2), channel_id=1, source_target_pairs={{0,4},{4,0},{8,12},{12,8},{16,20},{20,16},{24,28},{28,24},{1,5},{5... | collective-permute-start | bytes 1179656 | tf_op jit(solution)/shard_map/ppermute | solution.py:42
  838.9 23.2 %all-to-all-start.4 = ((bf16[8,64,640]{2,1,0:T(8,128)(2,1)}), bf16[8,64,640]{2,1,0:T(8,128)(2,1)}, u32[]{:S(2)}, u32[]{:S(2)}) async-start(bf16[8,64,640]{2,1,0:T(8,128)(2,1)} %bitcast.293), calls=%async_computation.8 | async-start | bytes 1310720 | tf_op jit(solution)/shard_map/all_to_all | solution.py:70
  845.6 11.6 %collective-permute-start.32 = (bf16[256,768]{1,0:T(8,128)(2,1)S(1)}, bf16[256,768]{1,0:T(8,128)(2,1)S(1)}, u32[]{:S(2)}, u32[]{:S(2)}) collective-permute-start(bf16[256,768]{1,0:T(8,128)(2,1)S(1)} %get-tuple-element.136), channel_id=1, source_target_pairs={{0,2},{1,3},{2,0},{3,1},{4,6},{5,7},{6,4},{7,5},{8,10},{9,11},{10,... | collective-permute-start | bytes 1179656 | tf_op jit(solution)/shard_map/ppermute | solution.py:42
  846.5 11.2 %collective-permute-start.34 = (bf16[256,768]{1,0:T(8,128)(2,1)S(1)}, bf16[256,768]{1,0:T(8,128)(2,1)S(1)}, u32[]{:S(2)}, u32[]{:S(2)}) collective-permute-start(bf16[256,768]{1,0:T(8,128)(2,1)S(1)} %get-tuple-element.137), channel_id=1, source_target_pairs={{0,1},{1,0},{2,3},{3,2},{4,5},{5,4},{6,7},{7,6},{8,9},{9,8},{10,11... | collective-permute-start | bytes 1179656 | tf_op jit(solution)/shard_map/ppermute | solution.py:42
  862.1 30.0 %all-to-all-start.3 = ((bf16[8,64,768]{2,1,0:T(8,128)(2,1)}), bf16[8,64,768]{2,1,0:T(8,128)(2,1)S(1)}, u32[]{:S(2)}, u32[]{:S(2)}) async-start(bf16[8,64,768]{2,1,0:T(8,128)(2,1)} %bitcast.85), calls=%async_computation.7 | async-start | bytes 1572864 | tf_op jit(solution)/shard_map/all_to_all | solution.py:70
  871.2 4.4 collective-permute-start.35
  876.2 3.6 collective-permute-start.36
  879.8 1.1 collective-permute-start.37
  880.9 9.9 %collective-permute-start.38 = (f32[144]{0:T(256)S(1)}, f32[144]{0:T(256)S(1)}, u32[]{:S(2)}, u32[]{:S(2)}) collective-permute-start(f32[144]{0:T(256)S(1)} %add.314), channel_id=1, source_target_pairs={{0,8},{4,12},{8,0},{12,4},{16,24},{20,28},{24,16},{28,20},{1,9},{5... | collective-permute-start | bytes 1736 | tf_op jit(solution)/shard_map/ppermute | solution.py:42
  882.9 7.9 collective-permute-start.39
  885.3 5.5 collective-permute-start.40
  (89 other events, 575.3 us)
Sparse Core Ops, SparseCore 0:
  58.0 80.9 all-gather.4
  141.1 103.4 all-gather.6
  246.9 87.9 reduce-scatter.4
  340.7 80.4 all-gather.8
  447.6 88.1 reduce-scatter.6
  540.2 80.3 all-gather.10
  623.0 104.2 reduce-scatter.8
  748.1 90.5 reduce-scatter.10
